TPU v7x, 32 devices: a whole 2x2x4 slice. The times are simulated.
32 devices in a mesh: seq: 8 (over z, y), ctx: 4 (over x, core).
Axes of the slice: x: 2, y: 2, z: 4, core: 2. Of those that a mesh axis runs over, the one named last changes fastest.
Arguments:
- tokens: bfloat16 [16, 1024, 1536], P('seq', 'ctx'), may hold values from -6 to 6
- norm_gain: bfloat16 [1536], P(('seq', 'ctx')), may hold values from 0.5 to 1.5
- input_weight: bfloat16 [1536, 6448], P(('seq', 'ctx')), may hold values from -0.15625 to 0.15625
- conv_w: bfloat16 [4, 3328], P(None, ('seq', 'ctx')), may hold values from -3 to 3
- conv_b: bfloat16 [3328], P(('seq', 'ctx')), may hold values from -3 to 3
- dt_bias: float32 [48], replicated, may hold values from -5.5 to -2.5
- a_log: float32 [48], replicated, may hold values from -5.5 to 0
- d_skip: float32 [48], replicated, may hold values from 0.5 to 1.5
- gate_gain: bfloat16 [3072], P(('seq', 'ctx')), may hold values from 0.5 to 1.5
- output_weight: bfloat16 [3072, 1536], P(('seq', 'ctx')), may hold values from -0.109375 to 0.109375
- segments: int32 [16, 1024], P('seq', 'ctx'), may hold values from 0 to 17, as said below
- cotangent: bfloat16 [16, 1024, 1536], P('seq', 'ctx'), may hold values from -6 to 6
Outputs:
- output: bfloat16 [16, 1024, 1536], P('seq', 'ctx')
- input_grad: bfloat16 [16, 1024, 1536], P('seq', 'ctx')
- grad_norm_gain: float32 [1536], P(('seq', 'ctx'))
- grad_w_in: float32 [1536, 6448], P(('seq', 'ctx'))
- grad_conv_w: float32 [4, 3328], P(None, ('seq', 'ctx'))
- grad_conv_b: float32 [3328], P(('seq', 'ctx'))
- grad_dt_bias: float32 [48], replicated
- grad_a_log: float32 [48], replicated
- grad_d_skip: float32 [48], replicated
- grad_gate_gain: float32 [3072], P(('seq', 'ctx'))
- out_weight_gradient: float32 [3072, 1536], P(('seq', 'ctx'))
Inputs may be any that keep to these rules, and one draw needn't show every extreme that they name: `segments`: document numbers start at 0 in every sequence, never fall along it, and rise by one at each document's first token; documents hold 60 tokens or more except a sequence's last one. In each aligned group of 2 sequences one sequence, drawn from the seed, has a first document that starts at its first token and ends within its last 256 tokens. The largest document number is reached in every draw.
All inputs are finite; a program needn't handle non-finite values.
Results may differ from a plain program's by a relative error of at most 0.0087.
Values may be sent and summed in bfloat16 or wider, within the bound.
A program may use at most 320 MiB of HBM per device.

v0:
```python
from functools import partial

import jax
import jax.numpy as jnp
from jax import lax
from jax.sharding import PartitionSpec as P

HEADS = 48
STATE = 128
HEADDIM = 64
CONV = 4


EPSILON = 1e-05
PRECISION_MAX = lax.Precision.HIGHEST


def passed_along(shard, axis, by):
    size = lax.axis_size(axis)
    pairs = [(i, i + by) for i in range(size) if 0 <= i + by < size]
    return lax.ppermute(shard, axis, pairs)


def entering(part, axis, combine, identity, reverse):
    count = lax.axis_size(axis)
    place = lax.axis_index(axis)
    ahead = count - 1 - place if reverse else place
    gathered = jax.tree.map(lambda a: lax.all_gather(a, axis), part)
    state = jax.tree.map(lambda a, e: jnp.zeros_like(a) + jnp.asarray(e, a.dtype), part, identity)

    def one(turn, state):
        source = count - 1 - turn if reverse else turn
        return combine(
            state, jax.tree.map(lambda a: lax.dynamic_index_in_dim(a, source, 0, False), gathered)
        )

    return lax.fori_loop(0, ahead, one, state)


def rms_scale(source, gain_vec):
    return (
        source * lax.rsqrt(jnp.mean(source * source, axis=-1, keepdims=True) + EPSILON) * gain_vec
    )


def conv_local(extended, step_raw, conv_w, conv_b, dt_bias, a_log, ids_ext):
    seq_count = extended.shape[0]
    length = extended.shape[1] - (CONV - 1)
    inner_width = HEADS * HEADDIM
    own_ids = ids_ext[:, CONV - 1 :]
    conv_out = conv_b + conv_w[0] * extended[:, CONV - 1 :]
    for shift_by in range(1, CONV):
        earlier = extended[:, CONV - 1 - shift_by : CONV - 1 - shift_by + length]
        same_doc = own_ids == ids_ext[:, CONV - 1 - shift_by : CONV - 1 - shift_by + length]
        conv_out = conv_out + conv_w[shift_by] * earlier * same_doc[..., None].astype(jnp.float32)
    activated = jax.nn.silu(conv_out)
    values = activated[..., :inner_width].reshape(seq_count, length, HEADS, HEADDIM)
    keys_b = activated[..., inner_width : inner_width + STATE]
    queries_c = activated[..., inner_width + STATE :]
    step_sizes = jax.nn.softplus(step_raw + dt_bias)
    log_decay = jnp.cumsum(-step_sizes * jnp.exp(a_log), axis=1)
    prev_ids = ids_ext[:, CONV - 2]
    ending = (own_ids == own_ids[:, -1:]).astype(jnp.float32)
    toward = jnp.exp(log_decay[:, -1:, :] - log_decay) * step_sizes * ending[:, :, None]
    fresh_state = jnp.einsum(
        "sqhp,sqn->shpn", toward[..., None] * values, keys_b, precision=PRECISION_MAX
    )
    carried = (own_ids[:, -1] == prev_ids).astype(jnp.float32)
    decay_total = jnp.exp(log_decay[:, -1, :]) * carried[:, None]
    return (values, keys_b, queries_c, step_sizes, log_decay, decay_total, fresh_state)


def mix_one(
    values,
    keys_b,
    queries_c,
    step_sizes,
    log_decay,
    state_in,
    gate_z,
    own_ids,
    prev_id,
    d_skip,
    gain_vec,
):
    length = own_ids.shape[0]
    across = log_decay.T
    causal = jnp.arange(length)[:, None] >= jnp.arange(length)[None, :]
    inside = ((own_ids[:, None] == own_ids[None, :]) & causal)[None]
    spread = across[:, :, None] - across[:, None, :]
    weights = jnp.where(inside, jnp.exp(jnp.where(inside, spread, 0.0)), 0.0)
    intersection = jnp.dot(queries_c, keys_b.T, precision=PRECISION_MAX)
    scores = intersection[None] * weights * step_sizes.T[:, None, :]
    output = jnp.einsum("hqk,khp->qhp", scores, values, precision=PRECISION_MAX)
    carried = (own_ids == prev_id).astype(jnp.float32)
    from_state = jnp.einsum("qn,hpn->qhp", queries_c, state_in, precision=PRECISION_MAX)
    output = output + (jnp.exp(log_decay) * carried[:, None])[..., None] * from_state
    output = output + d_skip[:, None] * values
    gated_out = output.reshape(length, HEADS * HEADDIM) * jax.nn.silu(gate_z)
    return rms_scale(gated_out, gain_vec)


def chain_step(earlier_part, later_part):
    return (
        earlier_part[0] * later_part[0],
        later_part[0][:, :, None, None] * earlier_part[1] + later_part[1],
    )


def local(
    tokens,
    norm_gain,
    input_weight,
    conv_w,
    conv_b,
    dt_bias,
    a_log,
    d_skip,
    gate_gain,
    output_weight,
    segments,
    cotangent,
):
    gathered = (
        lax.all_gather(norm_gain, ("seq", "ctx"), axis=0, tiled=True),
        lax.all_gather(input_weight, ("seq", "ctx"), axis=0, tiled=True),
        lax.all_gather(conv_w, ("seq", "ctx"), axis=1, tiled=True),
        lax.all_gather(conv_b, ("seq", "ctx"), axis=0, tiled=True),
        lax.all_gather(gate_gain, ("seq", "ctx"), axis=0, tiled=True),
        lax.all_gather(output_weight, ("seq", "ctx"), axis=0, tiled=True),
    )
    norm_full, input_complete, conv_w_full, conv_b_full, gate_full, output_complete = gathered
    length = tokens.shape[1]
    inner_width = HEADS * HEADDIM
    channels = inner_width + 2 * STATE
    inputs = tokens.astype(jnp.float32)
    normalized_input, norm_pull = jax.vjp(rms_scale, inputs, norm_full.astype(jnp.float32))
    normalized_reduced = normalized_input.astype(jnp.bfloat16)
    projected_input = jnp.einsum(
        "ive,eu->ivu", normalized_reduced, input_complete, preferred_element_type=jnp.float32
    ).astype(jnp.bfloat16)
    mixed_in = projected_input[..., inner_width : inner_width + channels]
    tail_rows = mixed_in[:, length - (CONV - 1) :]
    tail_ids = segments[:, length - (CONV - 1) :].astype(jnp.bfloat16)
    prev_tail, prev_ids = passed_along((tail_rows, tail_ids), "ctx", 1)
    extended = jnp.concatenate([prev_tail, mixed_in], axis=1).astype(jnp.float32)
    own_ids = segments.astype(jnp.float32)
    ids_ext = jnp.concatenate([prev_ids.astype(jnp.float32), own_ids], axis=1)
    prev_id = ids_ext[:, CONV - 2]
    step_raw = projected_input[..., inner_width + channels :].astype(jnp.float32)
    gate_z = projected_input[..., :inner_width].astype(jnp.float32)
    local_fn = partial(conv_local, ids_ext=ids_ext)
    pieces, conv_pull = jax.vjp(
        local_fn,
        extended,
        step_raw,
        conv_w_full.astype(jnp.float32),
        conv_b_full.astype(jnp.float32),
        dt_bias,
        a_log,
    )
    values, keys_b, queries_c, step_sizes, log_decay, decay_total, fresh_state = pieces
    identity = (jnp.ones_like(decay_total), jnp.zeros_like(fresh_state))
    state_in = entering((decay_total, fresh_state), "ctx", chain_step, identity, False)[1]
    gate_f = gate_full.astype(jnp.float32)
    per_seq = (values, keys_b, queries_c, step_sizes, log_decay, state_in, gate_z)

    def forward_one(entries):
        seq_items, ids_row, prev_row = entries
        return mix_one(
            seq_items[0],
            seq_items[1],
            seq_items[2],
            seq_items[3],
            seq_items[4],
            seq_items[5],
            seq_items[6],
            ids_row,
            prev_row,
            d_skip,
            gate_f,
        )

    gated_normalized = lax.map(forward_one, (per_seq, own_ids, prev_id))
    gated_reduced = gated_normalized.astype(jnp.bfloat16)
    branch_value = jnp.einsum(
        "rph,hw->rpw", gated_reduced, output_complete, preferred_element_type=jnp.float32
    )
    output = (inputs + branch_value).astype(jnp.bfloat16)
    input_backward, output_backward = (
        lax.all_gather(input_weight, ("seq", "ctx"), axis=0, tiled=True),
        lax.all_gather(output_weight, ("seq", "ctx"), axis=0, tiled=True),
    )
    out_weight_gradient = jnp.einsum(
        "xpo,xph->oh", gated_reduced, cotangent, preferred_element_type=jnp.float32
    )
    gated_gradient = jnp.einsum(
        "ixy,ny->ixn", cotangent, output_backward, preferred_element_type=jnp.float32
    )

    def backward_one(entries):
        seq_items, ids_row, prev_row, cot_row = entries

        def local_mix(
            values_row,
            keys_row,
            queries_row,
            steps_row,
            decay_row,
            state_row,
            gate_row,
            skip_vec,
            gain_vec,
        ):
            return mix_one(
                values_row,
                keys_row,
                queries_row,
                steps_row,
                decay_row,
                state_row,
                gate_row,
                ids_row,
                prev_row,
                skip_vec,
                gain_vec,
            )

        unused, pullback = jax.vjp(
            local_mix,
            seq_items[0],
            seq_items[1],
            seq_items[2],
            seq_items[3],
            seq_items[4],
            seq_items[5],
            seq_items[6],
            d_skip,
            gate_f,
        )
        return pullback(cot_row)

    mixed_grads = lax.map(backward_one, (per_seq, own_ids, prev_id, gated_gradient))
    direct_state = mixed_grads[5]
    grad_gate_z = mixed_grads[6]
    grad_skip = jnp.sum(mixed_grads[7], axis=0)
    grad_gate_gain = jnp.sum(mixed_grads[8], axis=0)
    later_grad = entering((decay_total, direct_state), "ctx", chain_step, identity, True)[1]
    grad_decay = jnp.sum(later_grad * state_in, axis=(2, 3))
    conv_grads = conv_pull(
        (
            mixed_grads[0],
            mixed_grads[1],
            mixed_grads[2],
            mixed_grads[3],
            mixed_grads[4],
            grad_decay,
            later_grad,
        )
    )
    grad_extended, grad_step_raw, grad_conv_w, grad_conv_b, grad_dt_bias, grad_a_log = conv_grads
    back_edge = passed_along(grad_extended[:, : CONV - 1].astype(jnp.bfloat16), "ctx", -1).astype(
        jnp.float32
    )
    own_grad = grad_extended[:, CONV - 1 :]
    grad_mixed = jnp.concatenate(
        [own_grad[:, : length - (CONV - 1)], own_grad[:, length - (CONV - 1) :] + back_edge], axis=1
    )
    projected_gradient = jnp.concatenate([grad_gate_z, grad_mixed, grad_step_raw], axis=-1).astype(
        jnp.bfloat16
    )
    grad_w_in = jnp.einsum(
        "gyb,gyc->bc", normalized_reduced, projected_gradient, preferred_element_type=jnp.float32
    )
    grad_normed = jnp.einsum(
        "whq,fq->whf", projected_gradient, input_backward, preferred_element_type=jnp.float32
    )
    grad_inputs, grad_norm_gain = norm_pull(grad_normed)
    input_grad = (cotangent.astype(jnp.float32) + grad_inputs).astype(jnp.bfloat16)
    shares = (
        lax.psum_scatter(grad_norm_gain, ("seq", "ctx"), scatter_dimension=0, tiled=True),
        lax.psum_scatter(grad_w_in, ("seq", "ctx"), scatter_dimension=0, tiled=True),
        lax.psum_scatter(grad_conv_w, ("seq", "ctx"), scatter_dimension=1, tiled=True),
        lax.psum_scatter(grad_conv_b, ("seq", "ctx"), scatter_dimension=0, tiled=True),
        lax.psum_scatter(grad_gate_gain, ("seq", "ctx"), scatter_dimension=0, tiled=True),
        lax.psum_scatter(out_weight_gradient, ("seq", "ctx"), scatter_dimension=0, tiled=True),
    )
    head_sums = lax.psum((grad_dt_bias, grad_a_log, grad_skip), ("seq", "ctx"))
    return (
        output,
        input_grad,
        shares[0],
        shares[1],
        shares[2],
        shares[3],
        head_sums[0],
        head_sums[1],
        head_sums[2],
        shares[4],
        shares[5],
    )


def solution(mesh):
    in_specs = (
        P("seq", "ctx", None),
        P(("seq", "ctx")),
        P(("seq", "ctx"), None),
        P(None, ("seq", "ctx")),
        P(("seq", "ctx")),
        P(),
        P(),
        P(),
        P(("seq", "ctx")),
        P(("seq", "ctx"), None),
        P("seq", "ctx"),
        P("seq", "ctx", None),
    )
    out_specs = (
        P("seq", "ctx", None),
        P("seq", "ctx", None),
        P(("seq", "ctx")),
        P(("seq", "ctx"), None),
        P(None, ("seq", "ctx")),
        P(("seq", "ctx")),
        P(),
        P(),
        P(),
        P(("seq", "ctx")),
        P(("seq", "ctx"), None),
    )
    return jax.shard_map(local, mesh=mesh, in_specs=in_specs, out_specs=out_specs, check_vma=False)
```

profile of v0, /device:TPU:0, one launch (start us, length us, event | category | flops | bytes accessed | tf_op | source)
XLA Modules:
  0.0 1678.2 jit_solution(2020675621425951640)
XLA Ops:
  15.6 43.8 %all-reduce.21 = (bf16[1536]{0:T(1024)(128)(2,1)S(1)}, bf16[3328]{0:T(1024)(128)(2,1)S(1)}, bf16[3072]{0:T(1024)(128)(2,1)S(1)}) all-reduce(bf16[1536]{0:T(1024)(128)(2,1)S(1)} %dynamic-update-slice.1, bf16[3328]{0:T(1024)(128)(2,1)S(1)} %dynamic-update-slice, ...), channel_id=1, replica_groups=mesh['seq'=8,'ctx'=4] {'seq','ctx'}, use_global_device_ids=true, to_apply=%add.14 | all-reduce | flops 7936 | bytes 31744
  59.4 40.0 %all-gather.2 = bf16[32,104,4]{1,2,0:T(4,128)(2,1)S(1)} all-gather(bf16[1,104,4]{1,2,0:T(4,128)(2,1)} %bitcast.398), channel_id=1, replica_groups=mesh['seq'=8,'ctx'=4] {'seq','ctx'}, dimensions={0}, use_global_device_ids=true | all-gather | bytes 27456 | tf_op jit(solution)/shard_map/all_gather | solution.py:127
  105.2 39.8 %all-gather.8.cloned.1.call-done = bf16[1536,6448]{1,0:T(8,128)(2,1)} async-done(((bf16[48,6448]{1,0:T(8,128)(2,1)}), bf16[1536,6448]{1,0:T(8,128)(2,1)}) %all-gather.8.cloned.1.call-update) | async-done | bytes 19808272 | tf_op jit(solution)/shard_map/all_gather | solution.py:126
  145.1 17.2 %fusion.130 = bf16[2,256,6448]{1,2,0:T(8,128)(2,1)} fusion(bf16[1536,6448]{1,0:T(8,128)(2,1)} %all-gather.8.cloned.1.call-done, bf16[2,256,1536]{2,1,0:T(8,128)(2,1)S(1)} %copy-done.14, f32[1536]{0:T(1024)S(1)} %convert_element_type.88, f32[2,256]{1,0:T(2,128)S(1)} %fusion.176), kind=kOutput, calls=%fused_computation.167 | convolution fusion | flops 10144972800 | bytes 27992064 | tf_op jit(solution)/shard_map/ive,eu->ivu/dot_general | solution.py:139
  162.3 17.7 %copy.167 = bf16[2,256,6448]{2,0,1:T(2,128)(2,1)} copy(bf16[2,256,6448]{1,2,0:T(8,128)(2,1)} %fusion.130) | data formatting | bytes 13205504 | tf_op jit(solution)/shard_map/ive,eu->ivu/dot_general | solution.py:139
  198.7 17.2 %fusion.179 = (f32[2,256,3328]{2,0,1:T(2,128)}, f32[2,256,3328]{2,0,1:T(2,128)}) fusion(f32[2,256]{0,1:T(8,128)S(1)} %copy.170, f32[2,259,3328]{2,0,1:T(2,128)S(1)} %maximum_convert_fusion, f32[3328]{0:T(1024)S(1)} %get-tuple-element.564, f32[2,256]{0,1:T(8,128)S(1)} %copy.169, f32[3328]{0:T(1024)S(1)} %get-tuple-element.565, f32[2,256]{0,1:T(8,128)S(1)} %copy.168, ...), kind=kLoop, calls=%fused_computation.278 | loop fusion | flops 25559040 | bytes 40967168 | tf_op jit(solution)/shard_map/jvp(jit(silu))/mul | solution.py:56
  281.9 43.4 %all-gather.12.cloned.1.call-done = f32[8,48,64,128]{3,2,1,0:T(8,128)} async-done(((f32[2,48,64,128]{3,2,1,0:T(8,128)}), f32[8,48,64,128]{3,2,1,0:T(8,128)}) %all-gather.12.cloned.1.call-update) | async-done | bytes 12582928 | tf_op jit(solution)/shard_map/all_gather | solution.py:28
  329.4 356.4 %while.64 = (s32[]{:T(128)}, f32[2,256,48,64]{1,3,2,0:T(8,128)}, f32[2,256,128]{2,0,1:T(2,128)}, f32[2,256,128]{2,0,1:T(2,128)}, f32[2,256,48]{1,2,0:T(8,128)}, ...) while((s32[]{:T(128)}, f32[2,256,48,64]{1,3,2,0:T(8,128)}, ...), condition=%wide.region_18.19_spmd, body=%wide.region_8.18_spmd.sunk | while | flops 11298855936 | bytes 253219568 | solution.py:243
  368.0 19.0 %multiply_reduce_fusion.15 = (f32[256]{0:T(256)S(1)}, f32[256]{0:T(256)S(1)}, f32[256,48,64]{0,2,1:T(8,128)S(1)}) fusion(f32[256,48,64]{0,2,1:T(8,128)} %bitcast.368, f32[256,48,64]{0,2,1:T(8,128)} %bitcast.370, f32[48,64]{1,0:T(8,128)} %mul.1232, f32[2,256,48,64]{1,3,2,0:T(8,128)} %get-tuple-element.1147, s32[]{:T(128)S(6)} %copy.300, ...), kind=kOutput, calls=%fused_computation.103.clone.1 | convolution fusion | flops 2442657280 | bytes 19414208 | tf_op jit(solution)/shard_map/while/body/eval_jaxpr/jvp(hqk,khp->qhp)/dot_general | solution.py:94
  401.2 20.8 %fusion.257 = (f32[48,256]{1,0:T(8,128)}, f32[48,256]{1,0:T(8,128)}, f32[48,256]{1,0:T(8,128)}, f32[256,256]{1,0:T(8,128)S(1)}) fusion(f32[48,256]{1,0:T(8,128)S(1)} %dynamic-slice_bitcast_fusion.13, f32[48,256]{1,0:T(8,128)S(1)} %dynamic-slice_bitcast_fusion.14, f32[256,256]{1,0:T(8,128)S(1)} %fusion.253, pred[256,256]{1,0:T(8,128)(4,1)S(1)} %fusion.254, ...), kind=kOutput, calls=%fused_computation.58.clone.1 | convolution fusion | flops 2463002624 | bytes 7176196 | tf_op jit(solution)/shard_map/while/body/eval_jaxpr/transpose(jvp(hqk,khp->qhp))/dot_general | solution.py:94
  462.0 45.8 %dynamic_update_slice.57 = bf16[2,256,3072]{2,0,1:T(2,128)(2,1)} dynamic-update-slice(bf16[2,256,3072]{2,0,1:T(2,128)(2,1)} %get-tuple-element.1117, bf16[1,256,3072]{2,0,1:T(2,128)(2,1)} %copy.264, s32[]{:T(128)S(6)} %copy.300, s32[]{:T(128)} %constant.154.clone.1..sunk.1, s32[]{:T(128)} %constant.154.clone.1..sunk.1) | dynamic-update-slice | bytes 3145732 | tf_op jit(solution)/shard_map/while/body/jit(dynamic_update_index_in_dim)/dynamic_update_slice | solution.py:184
  532.2 18.9 %multiply_reduce_fusion.15 = (f32[256]{0:T(256)S(1)}, f32[256]{0:T(256)S(1)}, f32[256,48,64]{0,2,1:T(8,128)S(1)}) fusion(f32[256,48,64]{0,2,1:T(8,128)} %bitcast.368, f32[256,48,64]{0,2,1:T(8,128)} %bitcast.370, f32[48,64]{1,0:T(8,128)} %mul.1232, f32[2,256,48,64]{1,3,2,0:T(8,128)} %get-tuple-element.1147, s32[]{:T(128)S(6)} %copy.300, ...), kind=kOutput, calls=%fused_computation.103.clone.1 | convolution fusion | flops 2442657280 | bytes 19414208 | tf_op jit(solution)/shard_map/while/body/eval_jaxpr/jvp(hqk,khp->qhp)/dot_general | solution.py:94
  565.4 20.8 %fusion.257 = (f32[48,256]{1,0:T(8,128)}, f32[48,256]{1,0:T(8,128)}, f32[48,256]{1,0:T(8,128)}, f32[256,256]{1,0:T(8,128)S(1)}) fusion(f32[48,256]{1,0:T(8,128)S(1)} %dynamic-slice_bitcast_fusion.13, f32[48,256]{1,0:T(8,128)S(1)} %dynamic-slice_bitcast_fusion.14, f32[256,256]{1,0:T(8,128)S(1)} %fusion.253, pred[256,256]{1,0:T(8,128)(4,1)S(1)} %fusion.254, ...), kind=kOutput, calls=%fused_computation.58.clone.1 | convolution fusion | flops 2463002624 | bytes 7176196 | tf_op jit(solution)/shard_map/while/body/eval_jaxpr/transpose(jvp(hqk,khp->qhp))/dot_general | solution.py:94
  626.3 45.8 %dynamic_update_slice.57 = bf16[2,256,3072]{2,0,1:T(2,128)(2,1)} dynamic-update-slice(bf16[2,256,3072]{2,0,1:T(2,128)(2,1)} %get-tuple-element.1117, bf16[1,256,3072]{2,0,1:T(2,128)(2,1)} %copy.264, s32[]{:T(128)S(6)} %copy.300, s32[]{:T(128)} %constant.154.clone.1..sunk.1, s32[]{:T(128)} %constant.154.clone.1..sunk.1) | dynamic-update-slice | bytes 3145732 | tf_op jit(solution)/shard_map/while/body/jit(dynamic_update_index_in_dim)/dynamic_update_slice | solution.py:184
  689.6 64.0 %while.63 = (s32[]{:T(128)}, bf16[2,256,3072]{1,2,0:T(8,128)(2,1)}, f32[2,256,48,64]{1,3,2,0:T(8,128)}, f32[2,256,128]{2,1,0:T(8,128)S(1)}, f32[2,256,128]{2,1,0...) while((s32[]{:T(128)}, bf16[2,256,3072]{1,2,0:T(8,128)(2,1)}, ...), condition=%wide.region_7.8_spmd, body=%wide.region_5.7_spmd.sunk | while | flops 3755422464 | bytes 105375024 | solution.py:184
  753.6 29.0 %all-gather.14.cloned.1.call-done = f32[8,48,64,128]{3,2,1,0:T(8,128)} async-done(((f32[2,48,64,128]{3,2,1,0:T(8,128)}), f32[8,48,64,128]{3,2,1,0:T(8,128)}) %all-gather.14.cloned.1.call-update) | async-done | bytes 12582928 | tf_op jit(solution)/shard_map/all_gather | solution.py:28
  837.0 29.9 %multiply_reduce_fusion.9 = (f32[3328]{0:T(1024)S(1)}, f32[3328]{0:T(1024)S(1)}, f32[3328]{0:T(1024)S(1)}, f32[3328]{0:T(1024)S(1)}, f32[3328]{0:T(1024)}, /*index=5*/f32[2,256,3328]{2,0,1:T(2,128)S(1)}) fusion(f32[2,259,3328]{2,0,1:T(2,128)} %copy-done.1, f32[2,256]{0,1:T(8,128)S(1)} %copy-done.25, f32[2,256]{0,1:T(8,128)S(1)} %copy-done.27, ...), kind=kLoop, calls=%fused_computation.181 | loop fusion | flops 39173888 | bytes 47782912 | tf_op jit(solution)/shard_map/transpose(jvp())/reduce_sum | solution.py:55
  892.2 28.8 %pad_maximum_fusion = bf16[2,256,6448]{2,0,1:T(2,128)(2,1)} fusion(bf16[2,256,48]{2,0,1:T(2,128)(2,1)S(1)} %get-tuple-element.672, bf16[2,3,3328]{2,0,1:T(2,128)(2,1)S(1)} %fusion.173, bf16[2,253,3328]{2,0,1:T(2,128)(2,1)S(1)} %slice.150, bf16[2,256,3072]{2,0,1:T(2,128)(2,1)} %get-tuple-element.328), kind=kLoop, calls=%fused_computation.184 | loop fusion | flops 26411008 | bytes 13205504 | tf_op jit(solution)/shard_map/concatenate | solution.py:269
  921.1 17.2 %copy.202 = bf16[2,256,6448]{1,2,0:T(8,128)(2,1)} copy(bf16[2,256,6448]{2,0,1:T(2,128)(2,1)} %pad_maximum_fusion) | data formatting | bytes 13205504 | tf_op jit(solution)/shard_map/concatenate | solution.py:269
  938.3 19.0 %fusion.147 = (f32[1536]{0:T(1024)}, f32[2,256]{1,0:T(2,128)S(1)}, f32[2,256,1536]{2,1,0:T(8,128)}) fusion(bf16[2,256,1536]{2,1,0:T(8,128)(2,1)S(1)} %copy-done.15, f32[2,256]{1,0:T(2,128)S(1)} %copy-done.71, f32[1536]{0:T(1024)S(1)} %copy-done.61, bf16[2,256,6448]{1,2,0:T(8,128)(2,1)} %copy.202, bf16[1536,6448]{1,0:T(8,128)(2,1)} %all-gather.8.cloned.1.call-done), kind=kOutput, calls=%fused_computation.205 | convolution fusion | flops 10147330048 | bytes 31145984 | tf_op jit(solution)/shard_map/whq,fq->whf/dot_general | solution.py:275
  969.0 20.3 %convolution_bitcast_fusion = f32[1536,6448]{1,0:T(8,128)} fusion(bf16[2,256,6448]{1,2,0:T(8,128)(2,1)} %copy.202, bf16[2,256,1536]{2,1,0:T(8,128)(2,1)S(1)} %copy-done.15, f32[1536]{0:T(1024)S(1)} %copy-done.61, f32[2,256]{1,0:T(2,128)S(1)} %copy-done.71), kind=kOutput, calls=%fused_computation.164 | convolution fusion | flops 10144972800 | bytes 47800320 | tf_op jit(solution)/shard_map/gyb,gyc->bc/dot_general | solution.py:272
  1001.9 79.9 %all-reduce.24.cloned.1.call-done = (f32[1536]{0:T(1024)}, f32[4,3328]{1,0:T(4,128)}, f32[3328]{0:T(1024)}, f32[48]{0:T(128)}, f32[48]{0:T(128)}, /*index=5*/f32[48]{0:T(128)}, f32[3072]{0:T(1024)}) async-done(((f32[1536]{0:T(1024)}, f32[4,3328]{1,0:T(4,128)}, f32[3328]{0:T(1024)}, f32[48]{0:T(128)}, f32[48]{0:T(128)}, /*index=5*/f32[48]{0:T(128)}, f32[3072]{0:T(1024)}), (f32[1536]{0:T(1024)}, ...) | async-done | bytes 85584
  1087.0 209.5 %reduce-scatter.6.cloned.1.call-done = f32[96,1536]{1,0:T(8,128)} async-done(((f32[3072,1536]{1,0:T(8,128)}), f32[96,1536]{1,0:T(8,128)}) %reduce-scatter.6.cloned.1.call-update) | async-done | bytes 589840 | tf_op jit(solution)/shard_map/reduce_scatter | solution.py:286
  1296.5 371.2 %reduce-scatter.4.cloned.1.call-done = f32[48,6448]{1,0:T(8,128)} async-done(((f32[1536,6448]{1,0:T(8,128)}), f32[48,6448]{1,0:T(8,128)}) %reduce-scatter.4.cloned.1.call-update) | async-done | bytes 1238032 | tf_op jit(solution)/shard_map/reduce_scatter | solution.py:282
  (464 shorter events, 448.2 us)
Async XLA Ops:
  7.2 97.8 %copy-start.69 = (s32[2,256]{1,0:T(2,128)S(1)}, s32[2,256]{1,0:T(2,128)}, u32[]{:S(2)}) copy-start(s32[2,256]{1,0:T(2,128)} %param.30) | copy-start | bytes 6148
  7.2 137.9 %copy-start.14 = (bf16[2,256,1536]{2,1,0:T(8,128)(2,1)S(1)}, bf16[2,256,1536]{2,1,0:T(8,128)(2,1)}, u32[]{:S(2)}) copy-start(bf16[2,256,1536]{2,1,0:T(8,128)(2,1)} %param.20) | copy-start | bytes 4718596
  7.2 137.8 %all-gather.8.cloned.1.call-start = ((), (), s32[]{:S(2)}) async-start(), calls=%async_computation.2 | async-start | bytes 20680704 | tf_op jit(solution)/shard_map/all_gather | solution.py:126
  7.9 237.2 %all-gather.10.cloned.1.call-start = ((), (), s32[]{:S(2)}) async-start(), calls=%async_computation.3 | async-start | bytes 9732096 | tf_op jit(solution)/shard_map/all_gather | solution.py:130
  8.7 316.6 %all-gather.12.cloned.1.call-start = ((), (), s32[]{:S(2)}) async-start(), calls=%async_computation.6 | async-start | bytes 15728640 | tf_op jit(solution)/shard_map/all_gather | solution.py:28
  9.5 92.7 %collective-permute-start.1 = (bf16[2,3]{1,0:T(2,128)(2,1)S(1)}, bf16[2,3]{1,0:T(2,128)(2,1)S(1)}, u32[]{:S(2)}, u32[]{:S(2)}) collective-permute-start(bf16[2,3]{1,0:T(2,128)(2,1)S(1)} %slice_convert_fusion.1), channel_id=1, source_target_pairs={{0,1},{1,2},{2,3},{4,5},{5,6},{6,7},{8,9},{9,10},{10,11},{12,13},{... | collective-permute-start | bytes 44 | tf_op jit(solution)/shard_map/ppermute | solution.py:21
  59.4 102.8 %copy-start.60 = (f32[1536]{0:T(1024)}, f32[1536]{0:T(1024)S(1)}, u32[]{:S(2)}) copy-start(f32[1536]{0:T(1024)S(1)} %convert_element_type.88) | copy-start | bytes 18436
  100.2 82.9 %copy-start.76 = (f32[48]{0:T(128)}, f32[48]{0:T(128)S(1)}, u32[]{:S(2)}) copy-start(f32[48]{0:T(128)S(1)} %exp.74) | copy-start | bytes 580
  100.3 98.3 %copy-start.48 = (f32[3328]{0:T(1024)}, f32[3328]{0:T(1024)S(1)}, u32[]{:S(2)}) copy-start(f32[3328]{0:T(1024)S(1)} %get-tuple-element.563) | copy-start | bytes 39940
  100.4 98.3 %copy-start.50 = (f32[3328]{0:T(1024)}, f32[3328]{0:T(1024)S(1)}, u32[]{:S(2)}) copy-start(f32[3328]{0:T(1024)S(1)} %get-tuple-element.564) | copy-start | bytes 39940
  100.4 98.3 %copy-start.52 = (f32[3328]{0:T(1024)}, f32[3328]{0:T(1024)S(1)}, u32[]{:S(2)}) copy-start(f32[3328]{0:T(1024)S(1)} %get-tuple-element.565) | copy-start | bytes 39940
  100.4 98.3 %copy-start.54 = (f32[3328]{0:T(1024)}, f32[3328]{0:T(1024)S(1)}, u32[]{:S(2)}) copy-start(f32[3328]{0:T(1024)S(1)} %get-tuple-element.566) | copy-start | bytes 39940
  103.3 95.4 %copy-start.24 = (f32[2,256]{0,1:T(8,128)}, f32[2,256]{0,1:T(8,128)S(1)}, u32[]{:S(2)}) copy-start(f32[2,256]{0,1:T(8,128)S(1)} %copy.170) | copy-start | bytes 6148
  103.4 95.3 %copy-start.26 = (f32[2,256]{0,1:T(8,128)}, f32[2,256]{0,1:T(8,128)S(1)}, u32[]{:S(2)}) copy-start(f32[2,256]{0,1:T(8,128)S(1)} %copy.169) | copy-start | bytes 6148
  103.6 95.1 %copy-start.28 = (f32[2,256]{0,1:T(8,128)}, f32[2,256]{0,1:T(8,128)S(1)}, u32[]{:S(2)}) copy-start(f32[2,256]{0,1:T(8,128)S(1)} %copy.168) | copy-start | bytes 6148
  105.0 170.3 %copy-start.72 = (f32[2]{0:T(128)}, f32[2]{0:T(128)S(1)}, u32[]{:S(2)}) copy-start(f32[2]{0:T(128)S(1)} %get-tuple-element.568) | copy-start | bytes 28
  105.2 81.3 %copy-start.30 = (f32[2,256]{0,1:T(8,128)}, f32[2,256]{0,1:T(8,128)S(1)}, u32[]{:S(2)}) copy-start(f32[2,256]{0,1:T(8,128)S(1)} %copy.174) | copy-start | bytes 6148
  180.7 12.3 collective-permute-start
  186.5 88.8 %copy-start.10 = (f32[2,48,2,128]{1,0,3,2:T(2,128)}, f32[2,48,2,128]{1,0,3,2:T(2,128)S(1)}, u32[]{:S(2)}) copy-start(f32[2,48,2,128]{1,0,3,2:T(2,128)S(1)} %copy.173) | copy-start | bytes 294916
  244.4 538.2 %all-gather.14.cloned.1.call-start = ((), (), s32[]{:S(2)}) async-start(), calls=%async_computation.7 | async-start | bytes 15728640 | tf_op jit(solution)/shard_map/all_gather | solution.py:28
  685.9 395.9 %all-reduce.24.cloned.1.call-start = ((), (), s32[]{:S(2)}) async-start(), calls=%async_computation.8 | async-start | bytes 183296
  884.6 7.5 collective-permute-start.2
  957.4 339.1 %reduce-scatter.6.cloned.1.call-start = ((), (), s32[]{:S(2)}) async-start(), calls=%async_computation.5 | async-start | bytes 19464192 | tf_op jit(solution)/shard_map/reduce_scatter | solution.py:286
  968.9 698.8 %reduce-scatter.4.cloned.1.call-start = ((), (), s32[]{:S(2)}) async-start(), calls=%async_computation.4 | async-start | bytes 41361408 | tf_op jit(solution)/shard_map/reduce_scatter | solution.py:282
  (108 other events, 1626.1 us)
Sparse Core Ops, SparseCore 0:
  10.9 134.0 all-gather.7
  147.9 80.3 all-gather.9
  244.6 80.6 all-gather.11
  686.0 96.5 all-gather.13
  957.5 124.2 all-reduce.23
  1088.7 207.7 reduce-scatter.5
  1303.5 364.1 reduce-scatter.3
where the time goes:
time: 1700 us; the launch traced here: 1680 us
  waiting for transfers between devices  774 us (46%)
  matrix products  310 us (18%)
  local copies, waits for them, and re-layouts  277 us (16%)
  other arithmetic  176 us (10%)
  blocking collectives  89.5 us (5%)
  loops' own time  29.1 us (2%)
    reduce_scatter x1, waiting for transfers between devices, local(): lax.psum_scatter(grad_w_in, ('seq', 'ctx'), scatter_dimension=0, tiled=True)  371 us
    reduce_scatter x1, waiting for transfers between devices, local(): lax.psum_scatter(out_weight_gradient, ('seq', 'ctx'), scatter_dimension=0...  209 us
    dot_general x8, matrix products, mix_one(): output = jnp.einsum('hqk,khp->qhp', scores, values, precision=PRECISION_MAX)  131 us
    dynamic_update_slice x4, local copies, waits for them, and re-layouts, local(): gated_normalized = lax.map(forward_one, (per_seq, own_ids, prev_id))  107 us
    unnamed x8, waiting for transfers between devices  81.4 us
    all_gather x2, waiting for transfers between devices, entering(): gathered = jax.tree.map(lambda a: lax.all_gather(a, axis), part)  72.4 us
    dot_general x8, matrix products, mix_one(): jnp.einsum('qn,hpn->qhp', queries_c, state_in, precision=PRECISION_MAX)  48.7 us
    unnamed x1, blocking collectives  43.8 us
  transfers between devices with their start and end apart: 10, of which 6 were waited for; matrix products, arithmetic and copies ran while one was open for 15% of the time, Pallas kernels for 0%

commit v1 on v0

v1 whole, which is shorter than its diff:
```python
from functools import partial

import jax
import jax.numpy as jnp
from jax import lax
from jax.experimental import pallas as pl
from jax.experimental.pallas import tpu as pltpu
from jax.sharding import PartitionSpec as P

HEADS = 48
STATE = 128
HEADDIM = 64
CONV = 4
INNER = HEADS * HEADDIM
CHANNELS = INNER + 2 * STATE
GROUP = 8
GROUPS = HEADS // GROUP
WIDTH = GROUP * HEADDIM
LANES = 128
EPSILON = 1e-05
VMEM = 60 * 1024 * 1024
BOTH = ("seq", "ctx")
FAR = -1e30
f32 = jnp.float32
bf16 = jnp.bfloat16
MM = partial(jnp.dot, preferred_element_type=f32)


def mm_nt(a, b):
    return lax.dot_general(a, b, (((1,), (1,)), ((), ())), preferred_element_type=f32)


def mm_tn(a, b):
    return lax.dot_general(a, b, (((0,), (0,)), ((), ())), preferred_element_type=f32)


def at(j, width):
    return pl.ds(pl.multiple_of(j * width, width), width)


def low_half(rows):
    return lax.broadcasted_iota(jnp.int32, (rows, LANES), 1) < HEADDIM


def to_front(columns, g):
    return pltpu.roll(columns, lax.rem(LANES - GROUP * g, LANES), 1)


def spread(front, pair, low):
    return jnp.where(low, front[:, 2 * pair : 2 * pair + 1], front[:, 2 * pair + 1 : 2 * pair + 2])


def head_sums(product, g):
    lane = lax.broadcasted_iota(jnp.int32, (WIDTH, LANES), 1)
    row = lax.broadcasted_iota(jnp.int32, (WIDTH, LANES), 0)
    pick = jnp.where(lane == GROUP * g + row // HEADDIM, 1.0, 0.0).astype(bf16)
    high = product.astype(bf16)
    rest = (product - high.astype(f32)).astype(bf16)
    return MM(high, pick) + MM(rest, pick)


def taps(px_ref, tail, j, w_ref, b_ref, masks, ext):
    here = at(j, LANES)
    length = px_ref.shape[0]
    own = px_ref[:, here].astype(f32)
    ext[0:8, :] = tail
    ext[8 : 8 + length, :] = own
    inputs = [own] + [
        masks[k - 1] * ext[8 - k : 8 - k + length, :] for k in range(1, CONV)
    ]
    out = b_ref[0:1, here]
    for k in range(CONV):
        out = out + w_ref[k : k + 1, here] * inputs[k]
    return out, inputs


def tail_of(tail_ref, s, here):
    both = tail_ref[:, here].astype(f32)
    return jnp.where(s == 0, both[0:8], both[8:16])


def lane_masks(cols_ref, length):
    return [
        jnp.broadcast_to(cols_ref[0, :, k : k + 1], (length, LANES)) for k in range(CONV - 1)
    ]


def before_kernel(px_ref, tail_ref, w_ref, b_ref, cols_ref, heads_ref,
                  act_ref, tok_ref, cst_ref, fresh_ref, ext):
    s = pl.program_id(0)
    length = px_ref.shape[0]
    masks = lane_masks(cols_ref, length)

    @pl.loop(0, CHANNELS // LANES)
    def _(j):
        here = at(j, LANES)
        conv, _unused = taps(px_ref, tail_of(tail_ref, s, here), j, w_ref, b_ref, masks, ext)
        act_ref[0, :, here] = conv * jax.nn.sigmoid(conv)

    raw = px_ref[:, CHANNELS : CHANNELS + HEADS].astype(f32) + heads_ref[0:1, :HEADS]
    step = jnp.maximum(raw, 0.0) + jnp.log1p(jnp.exp(-jnp.abs(raw)))
    step = jnp.concatenate([step, jnp.zeros((length, LANES - HEADS), f32)], axis=1)
    rate = -step * jnp.exp(heads_ref[1:2, :])
    before = (
        lax.broadcasted_iota(jnp.int32, (length, length), 0)
        >= lax.broadcasted_iota(jnp.int32, (length, length), 1)
    ).astype(f32)
    decay = jnp.dot(before, rate, precision=lax.Precision.HIGHEST, preferred_element_type=f32)
    tok_ref[0, :, 0:LANES] = step
    tok_ref[0, :, LANES : 2 * LANES] = decay
    cst_ref[0] = decay.T[:HEADS]
    toward = jnp.exp(decay[length - 1 : length] - decay) * step * cols_ref[0, :, 4:5]
    keys = act_ref[0, :, INNER : INNER + STATE].astype(bf16)
    low = low_half(length)

    @pl.loop(0, GROUPS)
    def _(g):
        front = to_front(toward, g)
        for pair in range(GROUP // 2):
            here = pl.ds(pl.multiple_of(g * WIDTH + pair * LANES, LANES), LANES)
            scaled = (act_ref[0, :, here] * spread(front, pair, low)).astype(bf16)
            fresh_ref[0, here, :] = mm_tn(scaled, keys)


def bias_of(ids_col, ids_row, transposed):
    shape = (ids_col.shape[0], ids_row.shape[1])
    down = lax.broadcasted_iota(jnp.int32, shape, 0)
    across = lax.broadcasted_iota(jnp.int32, shape, 1)
    order = (down <= across) if transposed else (down >= across)
    return jnp.where(order & (ids_col == ids_row), 0.0, FAR)


def within_kernel(act_ref, tok_ref, cst_ref, cols_ref, rows_ref, y_ref, cross, bias):
    length = act_ref.shape[1]
    half = length // 2
    cross[...] = mm_nt(
        act_ref[0, :, INNER + STATE :].astype(bf16),
        act_ref[0, :, INNER : INNER + STATE].astype(bf16),
    )
    bias[...] = bias_of(cols_ref[0, :, 5:6], rows_ref[0, 0:1, :], False)
    low = low_half(length)

    @pl.loop(0, GROUPS)
    def _(g):
        step = to_front(tok_ref[0, :, 0:LANES], g)
        decay = to_front(tok_ref[0, :, LANES : 2 * LANES], g)
        rows = cst_ref[0, at(g, GROUP), :]
        for pair in range(GROUP // 2):
            here = pl.ds(pl.multiple_of(g * WIDTH + pair * LANES, LANES), LANES)
            scaled = act_ref[0, :, here] * spread(step, pair, low)
            top, bottom = 0.0, 0.0
            for which in range(2):
                h = 2 * pair + which
                mine = jnp.where(low == (which == 0), scaled, 0.0).astype(bf16)
                col, row = decay[:, h : h + 1], rows[h : h + 1, :]
                w = jnp.exp(col[:half] - row[:, :half] + bias[:half, :half])
                top = top + MM((cross[:half, :half] * w).astype(bf16), mine[:half])
                w = jnp.exp(col[half:] - row + bias[half:, :])
                bottom = bottom + MM((cross[half:, :] * w).astype(bf16), mine)
            y_ref[0, :half, here] = top
            y_ref[0, half:, here] = bottom


def gate_kernel(z_ref, act_ref, tok_ref, cols_ref, y_ref, state_ref, dgn_ref, lanes_ref,
                gn_ref, dz_ref, dy_ref, dstate_ref, q_ref, dq_ref, sums_ref, total, queries_acc):
    length = act_ref.shape[1]
    low = low_half(length)
    enter = jnp.exp(tok_ref[0, :, LANES : 2 * LANES]) * cols_ref[0, :, 3:4]
    queries = act_ref[0, :, INNER + STATE :].astype(bf16)

    def first(g, carry):
        square, inner = carry
        front = to_front(enter, g)
        for pair in range(GROUP // 2):
            here = pl.ds(pl.multiple_of(g * WIDTH + pair * LANES, LANES), LANES)
            far = mm_nt(queries, state_ref[0, here, :])
            y = y_ref[0, :, here] + spread(front, pair, low) * far
            total[:, here] = y
            y = y + lanes_ref[1:2, here] * act_ref[0, :, here]
            z = z_ref[:, here].astype(f32)
            gated = y * (z * jax.nn.sigmoid(z))
            square = square + gated * gated
            inner = inner + lanes_ref[0:1, here] * dgn_ref[:, here] * gated
        return square, inner

    zero = jnp.zeros((length, LANES), f32)
    square, inner = lax.fori_loop(0, GROUPS, first, (zero, zero))
    scale = lax.rsqrt(jnp.sum(square, axis=1, keepdims=True) * (1.0 / INNER) + EPSILON)
    back = scale * scale * scale * (jnp.sum(inner, axis=1, keepdims=True) * (1.0 / INNER))
    scale = jnp.broadcast_to(scale, (length, LANES))
    back = jnp.broadcast_to(back, (length, LANES))
    queries_acc[...] = jnp.zeros_like(queries_acc)
    dq_ref[0] = jnp.zeros_like(dq_ref[0])

    @pl.loop(0, GROUPS)
    def _(g):
        front = to_front(enter, g)
        products = []
        for pair in range(GROUP // 2):
            here = pl.ds(pl.multiple_of(g * WIDTH + pair * LANES, LANES), LANES)
            xs = act_ref[0, :, here]
            inside = total[:, here]
            y = inside + lanes_ref[1:2, here] * xs
            z = z_ref[:, here].astype(f32)
            sg = jax.nn.sigmoid(z)
            gate = z * sg
            gated = y * gate
            gain = lanes_ref[0:1, here]
            dgn = dgn_ref[:, here]
            gn = gated * scale
            gn_ref[:, here] = (gn * gain).astype(bf16)
            dgated = scale * (gain * dgn) - gated * back
            dy = dgated * gate
            dz_ref[:, here] = (dgated * y * (sg * (1.0 + z * (1.0 - sg)))).astype(bf16)
            rounded = dy.astype(bf16)
            dy_ref[0, :, here] = rounded
            sums_ref[0, 0:1, here] = jnp.sum(dgn * gn, axis=0, keepdims=True)
            sums_ref[0, 1:2, here] = jnp.sum(dy * xs, axis=0, keepdims=True)
            entered = (rounded.astype(f32) * spread(front, pair, low)).astype(bf16)
            dstate_ref[0, here, :] = mm_tn(entered, queries)
            queries_acc[...] += MM(entered, state_ref[0, here, :])
            products.append(rounded.astype(f32) * inside)
        dq_ref[0] += head_sums(jnp.concatenate(products, axis=1), g)

    q_ref[0] = queries_acc[...]


def scan_back_kernel(act_ref, tok_ref, cst_ref, cols_ref, rows_ref, dy_ref,
                     dx_ref, dbc_ref, cross, bias, dcross):
    length = act_ref.shape[1]
    half = length // 2
    keys = act_ref[0, :, INNER : INNER + STATE].astype(bf16)
    queries = act_ref[0, :, INNER + STATE :].astype(bf16)
    cross[...] = mm_nt(keys, queries)
    bias[...] = bias_of(cols_ref[0, :, 5:6], rows_ref[0, 0:1, :], True)
    dcross[...] = jnp.zeros_like(dcross)
    low = low_half(length)

    @pl.loop(0, GROUPS)
    def _(g):
        step = to_front(tok_ref[0, :, 0:LANES], g)
        decay = to_front(tok_ref[0, :, LANES : 2 * LANES], g)
        rows = cst_ref[0, at(g, GROUP), :]
        for pair in range(GROUP // 2):
            here = pl.ds(pl.multiple_of(g * WIDTH + pair * LANES, LANES), LANES)
            scaled = (act_ref[0, :, here] * spread(step, pair, low)).astype(bf16)
            dy = dy_ref[0, :, here].astype(f32)
            top, bottom = 0.0, 0.0
            for which in range(2):
                h = 2 * pair + which
                mine = jnp.where(low == (which == 0), dy, 0.0).astype(bf16)
                col, row = decay[:, h : h + 1], rows[h : h + 1, :]
                w = jnp.exp(row - col[:half] + bias[:half, :])
                dcross[:half, :] += mm_nt(scaled[:half], mine) * w
                top = top + MM((cross[:half, :] * w).astype(bf16), mine)
                w = jnp.exp(row[:, half:] - col[half:] + bias[half:, half:])
                dcross[half:, half:] += mm_nt(scaled[half:], mine[half:]) * w
                bottom = bottom + MM((cross[half:, half:] * w).astype(bf16), mine[half:])
            dx_ref[0, :half, here] = top
            dx_ref[0, half:, here] = bottom

    d = dcross[...].astype(bf16)
    dbc_ref[0, :, :STATE] = MM(d, queries)
    dbc_ref[0, :, STATE:] = mm_tn(d, keys)


def after_kernel(px_ref, tail_ref, w_ref, b_ref, cols_ref, heads_ref, act_ref, tok_ref, lanes_ref,
                 dy_ref, dx_ref, dbc_ref, q_ref, dq_ref, later_ref, kept_ref,
                 dpx_ref, edge_ref, dconv_ref, dheads_ref, ext, moved, grad, dstep_acc, dcol_acc, keys_acc, ends, sent):
    s = pl.program_id(0)
    length = act_ref.shape[1]
    low = low_half(length)
    step = tok_ref[0, :, 0:LANES]
    decay = tok_ref[0, :, LANES : 2 * LANES]
    leave = jnp.exp(decay[length - 1 : length] - decay) * cols_ref[0, :, 4:5]
    keys = act_ref[0, :, INNER : INNER + STATE].astype(bf16)
    dstep_acc[...] = jnp.zeros_like(dstep_acc)
    dcol_acc[...] = jnp.zeros_like(dcol_acc)
    sent[...] = jnp.zeros_like(sent)
    keys_acc[...] = dbc_ref[0, :, :STATE]
    ends[...] = jnp.zeros_like(ends)

    @pl.loop(0, GROUPS)
    def _(g):
        step_front, leave_front = to_front(step, g), to_front(leave, g)
        products, columns = [], []
        for pair in range(GROUP // 2):
            here = pl.ds(pl.multiple_of(g * WIDTH + pair * LANES, LANES), LANES)
            later = later_ref[0, here, :]
            xs = act_ref[0, :, here]
            steps = spread(step_front, pair, low)
            leaving = spread(leave_front, pair, low)
            through = leaving * mm_nt(keys, later)
            dscaled = dx_ref[0, :, here] + through
            scaled = steps * xs
            rounded = scaled.astype(bf16).astype(f32)
            keys_acc[...] += MM((leaving * scaled).astype(bf16), later)
            products.append(xs * dscaled)
            columns.append(rounded * dscaled)
            sent[0:1, here] = jnp.sum(rounded * through, axis=0, keepdims=True)
            grad[:, here] = steps * dscaled + lanes_ref[1:2, here] * dy_ref[0, :, here].astype(f32)
            both = later.astype(f32) * kept_ref[0, here, :]
            at_row = GROUP * g + 2 * pair
            ends[pl.ds(at_row, 1), :] = jnp.sum(both[:HEADDIM], axis=0, keepdims=True)
            ends[pl.ds(at_row + 1, 1), :] = jnp.sum(both[HEADDIM:], axis=0, keepdims=True)
        dstep_acc[...] += head_sums(jnp.concatenate(products, axis=1), g)
        dcol_acc[...] += head_sums(jnp.concatenate(columns, axis=1), g)

    grad[:, INNER : INNER + STATE] = keys_acc[...]
    grad[:, INNER + STATE :] = dbc_ref[0, :, STATE:] + q_ref[0]
    dstep = dstep_acc[...]
    at_end = jnp.sum(ends[...].T, axis=0, keepdims=True)
    for g in range(GROUPS):
        at_end = at_end + head_sums(sent[:, g * WIDTH : (g + 1) * WIDTH], g)[0:1]
    row = lax.broadcasted_iota(jnp.int32, (length, LANES), 0)
    ddecay = dq_ref[0] - dcol_acc[...] + jnp.where(row == length - 1, at_end, 0.0)
    onward = (
        lax.broadcasted_iota(jnp.int32, (length, length), 0)
        <= lax.broadcasted_iota(jnp.int32, (length, length), 1)
    ).astype(f32)
    drate = jnp.dot(onward, ddecay, precision=lax.Precision.HIGHEST, preferred_element_type=f32)
    speed = jnp.exp(heads_ref[1:2, :])
    raw = px_ref[:, CHANNELS : CHANNELS + HEADS].astype(f32) + heads_ref[0:1, :HEADS]
    draw = (dstep - drate * speed)[:, :HEADS] * jax.nn.sigmoid(raw)
    dpx_ref[:, CHANNELS:] = jnp.concatenate(
        [draw, jnp.zeros((length, LANES - HEADS), f32)], axis=1
    ).astype(bf16)
    edge_ref[0, :, CHANNELS:] = jnp.zeros((8, LANES), f32)
    dheads_ref[0] = jnp.zeros((8, LANES), f32)
    dheads_ref[0, 0:1, :HEADS] = jnp.sum(draw, axis=0, keepdims=True)
    dheads_ref[0, 1:2, :] = jnp.sum(drate * (-step * speed), axis=0, keepdims=True)

    masks = lane_masks(cols_ref, length)
    moved[...] = jnp.zeros_like(moved)
    dconv_ref[0] = jnp.zeros((8, CHANNELS), f32)

    @pl.loop(0, CHANNELS // LANES)
    def _(j):
        here = at(j, LANES)
        conv, inputs = taps(px_ref, tail_of(tail_ref, s, here), j, w_ref, b_ref, masks, ext)
        sg = jax.nn.sigmoid(conv)
        dconv = grad[:, here] * (sg * (1.0 + conv * (1.0 - sg)))
        for k in range(CONV):
            dconv_ref[0, k : k + 1, here] = jnp.sum(dconv * inputs[k], axis=0, keepdims=True)
        dconv_ref[0, CONV : CONV + 1, here] = jnp.sum(dconv, axis=0, keepdims=True)
        dx = w_ref[0:1, here] * dconv
        edge = jnp.zeros((8, LANES), f32)
        for k in range(1, CONV):
            moved[k - 1, 8 : 8 + length, :] = dconv * masks[k - 1]
            dx = dx + w_ref[k : k + 1, here] * moved[k - 1, 8 + k : 8 + k + length, :]
            edge = edge + w_ref[k : k + 1, here] * moved[k - 1, k : 8 + k, :]
        dpx_ref[:, here] = dx.astype(bf16)
        edge_ref[0, :, here] = edge


def whole(shape):
    return pl.BlockSpec(shape, lambda s: (0,) * len(shape))


def per_seq(*tail):
    return pl.BlockSpec((1,) + tail, lambda s: (s,) + (0,) * len(tail))


def per_rows(rows, width):
    return pl.BlockSpec((rows, width), lambda s: (s, 0))


def call(kernel, count, in_specs, outs, scratch, *args):
    return pl.pallas_call(
        kernel,
        grid=(count,),
        in_specs=in_specs,
        out_specs=[spec for spec, _unused in outs],
        out_shape=[jax.ShapeDtypeStruct(*made) for _unused, made in outs],
        scratch_shapes=scratch,
        compiler_params=pltpu.CompilerParams(vmem_limit_bytes=VMEM),
    )(*args)


def chain(own, factor, steps):
    entered = jnp.zeros(own.shape, bf16)
    for source, target in steps:
        sent = (own + factor * entered.astype(f32)).astype(bf16)
        entered = entered + lax.ppermute(sent, "ctx", [(source, target)])
    return entered


def pad_lanes(v):
    return jnp.pad(v, (0, LANES - v.shape[0]))


NZ = 4


def place():
    seq, ctx = lax.axis_index("seq"), lax.axis_index("ctx")
    return seq // 2, lax.rem(seq, 2), ctx // 2, lax.rem(ctx, 2)


def device(z, y, x, c):
    return {"seq": z * 2 + y, "ctx": x * 2 + c}


def greet(z, y, x, c):
    barrier = pltpu.get_barrier_semaphore()
    others = [device(z, y, x, 1 - c), device(z, y, 1 - x, c), device(z, 1 - y, x, c)]
    others += [device(lax.rem(z + d, NZ), y, x, c) for d in range(1, NZ)]
    for other in others:
        pl.semaphore_signal(barrier, inc=1, device_id=other, device_id_type=pl.DeviceIdType.MESH)
    pl.semaphore_wait(barrier, len(others))


def remote(src, dst, send, recv, target):
    return pltpu.make_async_remote_copy(
        src_ref=src, dst_ref=dst, send_sem=send, recv_sem=recv, device_id=target,
        device_id_type=pl.DeviceIdType.MESH,
    )


def gather_kernel(units, n, *refs):
    ins, outs, (send, recv, local) = refs[:n], refs[n : 2 * n], refs[2 * n :]
    x_first = [first for _array, _row, _rows, first in units]
    z, y, x, c = place()
    greet(z, y, x, c)
    started = []

    def shard(u):
        a, row, rows, _first = units[u]
        return ins[a].at[pl.ds(row, rows)]

    def slot_of(u, *at):
        a, row, rows, _first = units[u]
        return outs[a].at[at + (pl.ds(row, rows),)]

    def push(u, zz, yy, xx, stage, own=False):
        slot = slot_of(u, zz, yy, xx, c)
        kind, index = stage
        target = {
            "x": device(z, y, 1 - x, c), "y": device(z, 1 - y, x, c), "c": device(z, y, x, 1 - c),
        }.get(kind)
        if kind == "z":
            target = device(lax.rem(z + index, NZ), y, x, c)
        copy = remote(shard(u) if own else slot, slot, send.at[u, number(u, stage)], recv.at[u, number(u, stage)], target)
        copy.start()
        started.append(copy)
        return copy

    def number(u, stage):
        kind, index = stage
        first = "x" if x_first[u] else "y"
        base = 0 if kind == "z" else 3 if kind == first else 15 if kind == "c" else 7
        return base + (index - 1 if kind == "z" else index)

    def came(u, zz, yy, xx, cc, stage):
        slot = slot_of(u, zz, yy, xx, cc)
        k = number(u, stage)
        remote(slot, slot, send.at[u, k], recv.at[u, k], device(z, y, x, 1 - c)).wait_recv()

    back = [lax.rem(z + NZ - d, NZ) for d in range(NZ)]
    own_copies = []
    for u in range(len(units)):
        a, b = ("x", "y") if x_first[u] else ("y", "x")
        for d in range(1, NZ):
            push(u, z, y, x, ("z", d), own=True)
        push(u, z, y, x, (b, 0), own=True)
        push(u, z, y, x, (a, 0), own=True)
        push(u, z, y, x, ("c", 0), own=True)
        own_copies.append(pltpu.make_async_copy(shard(u), slot_of(u, z, y, x, c), local.at[u]))
        own_copies[-1].start()
    for d in range(1, NZ + 1):
        for u in range(len(units)):
            a, b = ("x", "y") if x_first[u] else ("y", "x")
            if d < NZ:
                came(u, back[d], y, x, c, ("z", d))
                push(u, back[d], y, x, (b, d))
                push(u, back[d], y, x, (a, d))
                push(u, back[d], y, x, ("c", d))
            yy, xx = (y, 1 - x) if a == "x" else (1 - y, x)
            came(u, back[d - 1], yy, xx, c, (a, d - 1))
            push(u, back[d - 1], yy, xx, (b, NZ + d - 1))
            push(u, back[d - 1], yy, xx, ("c", NZ + d - 1))
    for half in range(2):
        for d in range(NZ):
            for u in range(len(units)):
                a, b = ("x", "y") if x_first[u] else ("y", "x")
                yy, xx = (1 - y, x) if b == "y" else (y, 1 - x)
                if half:
                    yy, xx = 1 - y, 1 - x
                came(u, back[d], yy, xx, c, (b, NZ * half + d))
                push(u, back[d], yy, xx, ("c", 2 * NZ + NZ * half + d))
    for u in range(len(units)):
        for k in range(16):
            a = "x" if x_first[u] else "y"
            away_a, away_b = (k // NZ) % 2, k // (2 * NZ)
            ax, ay = (away_a, away_b) if a == "x" else (away_b, away_a)
            xx = 1 - x if ax else x
            yy = 1 - y if ay else y
            came(u, back[k % NZ], yy, xx, 1 - c, ("c", k))
    for copy in started:
        copy.wait_send()
    for copy in own_copies:
        copy.wait()


def gather_all(shards, units):
    n, m = len(shards), len(units)
    return pl.pallas_call(
        partial(gather_kernel, tuple(units), n),
        out_shape=[jax.ShapeDtypeStruct((NZ, 2, 2, 2) + v.shape, v.dtype) for v in shards],
        in_specs=[pl.BlockSpec(memory_space=pl.ANY)] * n,
        out_specs=[pl.BlockSpec(memory_space=pl.ANY)] * n,
        scratch_shapes=[
            pltpu.SemaphoreType.DMA((m, 31)), pltpu.SemaphoreType.DMA((m, 31)), pltpu.SemaphoreType.DMA((m,)),
        ],
        compiler_params=pltpu.CompilerParams(collective_id=0, has_side_effects=True, vmem_limit_bytes=8 * 1024 * 1024),
    )(*shards)


CUT_ROWS, CUT = 48, 512


def cuts_of(shape):
    rows, columns = shape[-2:]
    return [(r, k, min(CUT, columns - k)) for k in range(0, columns, CUT) for r in range(0, rows, CUT_ROWS)]


def reduce_kernel(n, lead, *refs):
    ins, outs, scratch = refs[: n + 1], refs[n + 1 : 2 * n + 2], refs[2 * n + 2 :]
    (own, core, first, second, last, own_s, core_s, first_s, second_s, last_s, sem, semz) = scratch
    z, y, x, c = place()
    greet(z, y, x, c)
    pieces = [(a, cut) for a in range(n) for cut in cuts_of(ins[a].shape)]
    total = len(pieces) + 1
    sent = []

    def begin(i):
        own_i, core_i = view(i, 0), view(i, 1)
        if i == total - 1:
            src_out, src_own = ins[n].at[:, :, :, 1 - c], ins[n].at[:, :, :, c]
        else:
            a, (r, k, w) = pieces[i]
            rows, cols = pl.ds(r, CUT_ROWS), pl.ds(k, w)
            src_out = ins[a].at[:, :, :, 1 - c, rows, cols]
            src_own = ins[a].at[:, :, :, c, rows, cols]
        go = remote(src_out, core_i, sem.at[0, i], sem.at[1, i], device(z, y, x, 1 - c))
        go.start()
        sent.append(go)
        pltpu.make_async_copy(src_own, own_i, sem.at[2, i]).start()

    def view(i, k):
        if i == total - 1:
            return (own_s, core_s, first_s, second_s, last_s)[k]
        v = (own, core, first, second, last)[k]
        w = pieces[i][1][2]
        if w == CUT:
            return v.at[i]
        free = len(v.shape) - 2
        return v.at[(i,) + (slice(None),) * free + (pl.ds(0, w),)]

    def x_goes_first(i):
        return i % 2 == 0

    def after_core(i):
        own_i, core_i = view(i, 0), view(i, 1)
        remote(core_i, core_i, sem.at[0, i], sem.at[1, i], device(z, y, x, 1 - c)).wait_recv()
        pltpu.make_async_copy(own_i, own_i, sem.at[2, i]).wait()

        @pl.loop(0, NZ)
        def _(zz):
            for yy in range(2):
                for xx in range(2):
                    core_i[zz, yy, xx] = core_i[zz, yy, xx] + own_i[zz, yy, xx]

        if x_goes_first(i):
            src, to = core_i.at[:, :, 1 - x], device(z, y, 1 - x, c)
        else:
            src, to = core_i.at[:, 1 - y], device(z, 1 - y, x, c)
        go = remote(src, view(i, 2), sem.at[3, i], sem.at[4, i], to)
        go.start()
        sent.append(go)

    def after_first(i):
        core_i, first_i = view(i, 1), view(i, 2)
        remote(first_i, first_i, sem.at[3, i], sem.at[4, i], device(z, y, x, 1 - c)).wait_recv()

        @pl.loop(0, NZ)
        def _(zz):
            for o in range(2):
                mine = core_i[zz, o, x] if x_goes_first(i) else core_i[zz, y, o]
                first_i[zz, o] = first_i[zz, o] + mine

        if x_goes_first(i):
            src, to = first_i.at[:, 1 - y], device(z, 1 - y, x, c)
        else:
            src, to = first_i.at[:, 1 - x], device(z, y, 1 - x, c)
        go = remote(src, view(i, 3), sem.at[5, i], sem.at[6, i], to)
        go.start()
        sent.append(go)

    def after_second(i):
        first_i, second_i, last_i = view(i, 2), view(i, 3), view(i, 4)
        remote(second_i, second_i, sem.at[5, i], sem.at[6, i], device(z, y, x, 1 - c)).wait_recv()

        @pl.loop(0, NZ)
        def _(zz):
            second_i[zz] = second_i[zz] + (first_i[zz, y] if x_goes_first(i) else first_i[zz, x])

        for d in range(1, NZ):
            zz = lax.rem(z + d, NZ)
            go = remote(second_i.at[zz], last_i.at[z], semz.at[0, d, i], semz.at[1, d, i], device(zz, y, x, c))
            go.start()
            sent.append(go)
        last_i[z] = second_i[z]

    def after_last(i):
        last_i = view(i, 4)
        for d in range(1, NZ):
            zz = lax.rem(z + NZ - d, NZ)
            remote(last_i.at[zz], last_i.at[zz], semz.at[0, d, i], semz.at[1, d, i], device(z, y, x, 1 - c)).wait_recv()
        value = last_i[0].astype(f32)
        for zz in range(1, NZ):
            value = value + last_i[zz].astype(f32)
        if i == total - 1:
            outs[n][...] = value
        else:
            a, (r, k, w) = pieces[i]
            outs[a][r : r + CUT_ROWS, k : k + w] = value

    order = [total - 1] + list(range(total - 1))
    for i in order:
        begin(i)
    stages = (after_core, after_first, after_second, after_last)
    for t in range(total + lead[-1]):
        for stage, skew in reversed(list(zip(stages, lead))):
            if 0 <= t - skew < total:
                stage(order[t - skew])
    for go in sent:
        go.wait_send()


def reduce_all(arrays, small, lead=(0, 4, 6, 8)):
    n = len(arrays)
    arrays = [v.reshape((NZ, 2, 2, 2, -1, v.shape[-1])) for v in arrays]
    small = small.reshape((NZ, 2, 2, 2, -1, small.shape[-1]))
    p = sum(len(cuts_of(v.shape)) for v in arrays)
    ss = small.shape[-2:]
    made = [jax.ShapeDtypeStruct(v.shape[-2:], f32) for v in arrays + [small]]
    dims = [(NZ, 2, 2), (NZ, 2, 2), (NZ, 2), (NZ,), (NZ,)]
    return pl.pallas_call(
        partial(reduce_kernel, n, tuple(lead)),
        out_shape=made,
        in_specs=[pl.BlockSpec(memory_space=pl.ANY)] * (n + 1),
        out_specs=[pl.BlockSpec(memory_space=pltpu.VMEM)] * (n + 1),
        scratch_shapes=[pltpu.VMEM((p,) + d + (CUT_ROWS, CUT), bf16) for d in dims]
        + [pltpu.VMEM(d + ss, f32) for d in dims]
        + [pltpu.SemaphoreType.DMA((7, p + 1)), pltpu.SemaphoreType.DMA((2, NZ, p + 1))],
        compiler_params=pltpu.CompilerParams(collective_id=1, has_side_effects=True, vmem_limit_bytes=VMEM),
    )(*arrays, small)


def local(tokens, norm_gain, input_weight, conv_w, conv_b, dt_bias, a_log, d_skip, gate_gain,
          output_weight, segments, cotangent):
    seqs, length, width = tokens.shape
    n_ctx = lax.axis_size("ctx")
    n_all = n_ctx * lax.axis_size("seq")
    count = seqs * length
    shares = [norm_gain.shape[0], gate_gain.shape[0], CONV * conv_b.shape[0], conv_b.shape[0]]
    cuts = [sum(shares[: i + 1]) for i in range(3)]
    packed = jnp.concatenate([norm_gain, gate_gain, conv_w.reshape(-1), conv_b])
    torus = lax.axis_size("seq") == 2 * NZ and n_ctx == 4 and norm_gain.shape[0] == CUT_ROWS
    w_z, w_x = input_weight[:, :INNER], input_weight[:, INNER:]
    if torus:
        size = packed.shape[0]
        small = jnp.pad(packed, (0, 16 * LANES - size)).reshape(16, LANES)
        half = output_weight.shape[0] // 2
        w_x, w_z, w_out, packed = gather_all(
            [w_x, w_z, output_weight, small],
            [(0, 0, CUT_ROWS, True), (1, 0, CUT_ROWS, False), (2, 0, half, True),
             (2, half, half, False), (3, 0, 16, True)],
        )
        w_x, w_z, w_out = (w.reshape(-1, w.shape[-1]) for w in (w_x, w_z, w_out))
        packed = packed.reshape(n_all, -1)[:, :size]
    else:
        packed = lax.all_gather(packed, BOTH, axis=0)
        w_in, w_out = (
            lax.all_gather(w, BOTH, axis=0, tiled=True) for w in (input_weight, output_weight)
        )
        w_z, w_x = w_in[:, :INNER], w_in[:, INNER:]
    norm_full, gate_full, conv_w_full, conv_b_full = jnp.split(packed.astype(f32), cuts, axis=1)
    norm_full = norm_full.reshape(1, -1)
    gate_full = gate_full.reshape(1, -1)
    conv_b_full = conv_b_full.reshape(1, -1)
    conv_w_full = conv_w_full.reshape(n_all, CONV, -1).transpose(1, 0, 2).reshape(CONV, -1)

    onward = [(i, i + 1) for i in range(n_ctx - 1)]
    tail_tokens = lax.ppermute(tokens[:, length - (CONV - 1) :], "ctx", onward)
    tail_ids = lax.ppermute(segments[:, length - (CONV - 1) :], "ctx", onward)
    tail_ids = jnp.where(lax.axis_index("ctx") == 0, -1, tail_ids)
    tail_tokens = jnp.pad(tail_tokens, ((0, 0), (8 - (CONV - 1), 0), (0, 0)))
    x_all = jnp.concatenate([tokens.reshape(count, width), tail_tokens.reshape(seqs * 8, width)])
    x_all = x_all.astype(f32)
    r_all = lax.rsqrt(jnp.mean(x_all * x_all, axis=-1, keepdims=True) + EPSILON)
    normed = (x_all * r_all * norm_full).astype(bf16)

    ids_ext = jnp.concatenate([tail_ids, segments], axis=1)
    flags = [
        segments == ids_ext[:, CONV - 1 - k : CONV - 1 - k + length] for k in range(1, CONV)
    ] + [segments == ids_ext[:, CONV - 2 : CONV - 1], segments == segments[:, -1:]]
    cols = jnp.stack([f.astype(f32) for f in flags] + [segments.astype(f32)], axis=-1)
    cols = jnp.pad(cols, ((0, 0), (0, 0), (0, LANES - cols.shape[-1])))
    rows = jnp.pad(segments.astype(f32)[:, None], ((0, 0), (0, 7), (0, 0)))
    heads = jnp.pad(jnp.stack([pad_lanes(dt_bias), pad_lanes(a_log)]), ((0, 6), (0, 0)))
    lanes = jnp.concatenate([gate_full, jnp.repeat(d_skip, HEADDIM)[None]])
    lanes = jnp.pad(lanes, ((0, 6), (0, 0)))
    conv_w8 = jnp.pad(conv_w_full, ((0, 8 - CONV), (0, 0)))
    conv_b8 = jnp.pad(conv_b_full, ((0, 7), (0, 0)))

    px = MM(normed, w_x).astype(bf16)
    px_width, dpx_width = CHANNELS + HEADS, CHANNELS + LANES
    tail_spec = pl.BlockSpec((16, px_width), lambda s: (count // 16, 0))
    act, tok, cst, fresh = call(
        before_kernel, seqs,
        [per_rows(length, px_width), tail_spec, whole((8, CHANNELS)), whole((8, CHANNELS)),
         per_seq(length, LANES), whole((8, LANES))],
        [(per_seq(length, CHANNELS), ((seqs, length, CHANNELS), f32)),
         (per_seq(length, 2 * LANES), ((seqs, length, 2 * LANES), f32)),
         (per_seq(HEADS, length), ((seqs, HEADS, length), f32)),
         (per_seq(INNER, STATE), ((seqs, INNER, STATE), f32))],
        [pltpu.VMEM((length + 8, LANES), f32)],
        px, px, conv_w8, conv_b8, cols, heads,
    )
    carried = cols[:, length - 1, 3]
    kept = jnp.exp(cst[:, :, length - 1]) * carried[:, None]
    kept = jnp.repeat(kept, HEADDIM, axis=1)[..., None]
    entering = chain(fresh, kept, onward)
    stayed = kept * entering.astype(f32)
    pz = MM(normed[:count], w_z).astype(bf16)
    g2 = cotangent.reshape(count, width)
    dgn = lax.dot_general(g2, w_out, (((1,), (1,)), ((), ())), preferred_element_type=f32)
    [y] = call(
        within_kernel, seqs,
        [per_seq(length, CHANNELS), per_seq(length, 2 * LANES), per_seq(HEADS, length),
         per_seq(length, LANES), per_seq(8, length)],
        [(per_seq(length, INNER), ((seqs, length, INNER), f32))],
        [pltpu.VMEM((length, length), f32), pltpu.VMEM((length, length), f32)],
        act, tok, cst, cols, rows,
    )
    gn, dz, dy, dstate, dqueries, ddecay, sums = call(
        gate_kernel, seqs,
        [per_rows(length, INNER), per_seq(length, CHANNELS), per_seq(length, 2 * LANES),
         per_seq(length, LANES), per_seq(length, INNER), per_seq(INNER, STATE),
         per_rows(length, INNER), whole((8, INNER))],
        [(per_rows(length, INNER), ((count, INNER), bf16)),
         (per_rows(length, INNER), ((count, INNER), bf16)),
         (per_seq(length, INNER), ((seqs, length, INNER), bf16)),
         (per_seq(INNER, STATE), ((seqs, INNER, STATE), f32)),
         (per_seq(length, STATE), ((seqs, length, STATE), f32)),
         (per_seq(length, LANES), ((seqs, length, LANES), f32)),
         (per_seq(8, INNER), ((seqs, 8, INNER), f32))],
        [pltpu.VMEM((length, INNER), f32), pltpu.VMEM((length, STATE), f32)],
        pz, act, tok, cols, y, entering, dgn, lanes,
    )
    later = chain(dstate, kept, [(b, a) for a, b in reversed(onward)])
    output = (x_all[:count] + MM(gn, w_out)).astype(bf16)
    dw_out = lax.dot_general(gn, g2, (((0,), (0,)), ((), ())), preferred_element_type=f32)
    dw_z = lax.dot_general(normed[:count], dz, (((0,), (0,)), ((), ())), preferred_element_type=f32)
    dx, dbc = call(
        scan_back_kernel, seqs,
        [per_seq(length, CHANNELS), per_seq(length, 2 * LANES), per_seq(HEADS, length),
         per_seq(length, LANES), per_seq(8, length), per_seq(length, INNER)],
        [(per_seq(length, INNER), ((seqs, length, INNER), f32)),
         (per_seq(length, 2 * STATE), ((seqs, length, 2 * STATE), f32))],
        [pltpu.VMEM((length, length), f32)] * 3,
        act, tok, cst, cols, rows, dy,
    )
    dpx, edge, dconv, dheads = call(
        after_kernel, seqs,
        [per_rows(length, px_width), tail_spec, whole((8, CHANNELS)), whole((8, CHANNELS)),
         per_seq(length, LANES), whole((8, LANES)), per_seq(length, CHANNELS),
         per_seq(length, 2 * LANES), whole((8, INNER)), per_seq(length, INNER),
         per_seq(length, INNER), per_seq(length, 2 * STATE), per_seq(length, STATE),
         per_seq(length, LANES), per_seq(INNER, STATE), per_seq(INNER, STATE)],
        [(per_rows(length, dpx_width), ((count, dpx_width), bf16)),
         (per_seq(8, dpx_width), ((seqs, 8, dpx_width), f32)),
         (per_seq(8, CHANNELS), ((seqs, 8, CHANNELS), f32)),
         (per_seq(8, LANES), ((seqs, 8, LANES), f32))],
        [pltpu.VMEM((length + 8, LANES), f32), pltpu.VMEM((CONV - 1, length + 16, LANES), f32),
         pltpu.VMEM((length, CHANNELS), f32), pltpu.VMEM((length, LANES), f32),
         pltpu.VMEM((length, LANES), f32), pltpu.VMEM((length, STATE), f32), pltpu.VMEM((LANES, LANES), f32),
         pltpu.VMEM((8, INNER), f32)],
        px, px, conv_w8, conv_b8, cols, heads, act, tok, lanes, dy, dx, dbc, dqueries, ddecay,
        later, stayed,
    )
    dpx_all = jnp.concatenate([dpx, edge.reshape(seqs * 8, dpx_width).astype(bf16)])
    dw_x = lax.dot_general(normed, dpx_all, (((0,), (0,)), ((), ())), preferred_element_type=f32)
    nt = (((1,), (1,)), ((), ()))
    dnormed_x = lax.dot_general(dpx_all[:, :px_width], w_x, nt, preferred_element_type=f32)
    dnormed = dnormed_x[:count] + lax.dot_general(dz, w_z, nt, preferred_element_type=f32)
    back = dnormed_x[count:].reshape(seqs, 8, width)[:, 8 - (CONV - 1) :].astype(bf16)
    back = lax.ppermute(back, "ctx", [(b, a) for a, b in onward])
    back = jnp.pad(back.astype(f32), ((0, 0), (length - (CONV - 1), 0), (0, 0)))
    dnormed = dnormed + back.reshape(count, width)
    x, r = x_all[:count], r_all[:count]
    d_gain = jnp.sum(x * r * dnormed, axis=0)
    scaled = norm_full * dnormed
    dx_in = r * (scaled - x * (r * r) * jnp.mean(x * scaled, axis=-1, keepdims=True))
    input_grad = (g2.astype(f32) + dx_in).astype(bf16)

    sums = jnp.sum(sums, axis=0)
    dconv = jnp.sum(dconv, axis=0)
    dheads = jnp.sum(dheads, axis=0)
    d_skip_sum = jnp.sum(sums[1].reshape(HEADS, HEADDIM), axis=1)
    split = [d_gain.reshape(n_all, -1), sums[0].reshape(n_all, -1),
             dconv[:CONV].reshape(CONV, n_all, -1).transpose(1, 0, 2).reshape(n_all, -1),
             dconv[CONV].reshape(n_all, -1)]
    shared = jnp.concatenate([dheads[0, :HEADS], dheads[1, :HEADS], d_skip_sum])
    split = jnp.concatenate(split, axis=1)
    share = sum(shares)
    if torus:
        fill = 8 * LANES - share - shared.shape[0]
        split = [split, jnp.broadcast_to(shared, (n_all,) + shared.shape), jnp.zeros((n_all, fill), f32)]
        dw_out, dw_z, dw_x, mine = reduce_all(
            [v.astype(bf16) for v in (dw_out, dw_z, dw_x)],
            jnp.concatenate(split, axis=1).reshape(n_all, 8, LANES),
        )
        dw_in = jnp.concatenate([dw_z, dw_x[:, :px_width]], axis=1)
        mine = mine.reshape(-1)
        mine, shared = mine[:share], mine[share : share + shared.shape[0]]
    else:
        dw_in = jnp.concatenate([dw_z, dw_x[:, :px_width]], axis=1)
        dw_out, dw_in = (
            lax.psum_scatter(v, BOTH, scatter_dimension=0, tiled=True) for v in (dw_out, dw_in)
        )
        every = lax.psum(jnp.concatenate([split.reshape(-1), shared]), BOTH)
        me = lax.axis_index("seq") * n_ctx + lax.axis_index("ctx")
        mine, shared = lax.dynamic_slice(every, (me * share,), (share,)), every[n_all * share :]
    d_norm, d_gate, d_conv_w, d_conv_b = jnp.split(mine, cuts)
    d_bias, d_alog, d_skips = jnp.split(shared, 3)
    return (
        output.reshape(tokens.shape), input_grad.reshape(tokens.shape), d_norm, dw_in,
        d_conv_w.reshape(CONV, -1), d_conv_b, d_bias, d_alog, d_skips, d_gate, dw_out,
    )


def solution(mesh):
    split = P(BOTH)
    rows = P(BOTH, None)
    seq = P("seq", "ctx", None)
    in_specs = (seq, split, rows, P(None, BOTH), split, P(), P(), P(), split, rows,
                P("seq", "ctx"), seq)
    out_specs = (seq, seq, split, rows, P(None, BOTH), split, P(), P(), P(), split, rows)
    return jax.shard_map(local, mesh=mesh, in_specs=in_specs, out_specs=out_specs, check_vma=False)
```

time: 1700 us -> 645 us (0.38)
  waiting for transfers between devices: 774 us -> 39.3 us
  Pallas kernels: 0 us -> 428 us
  local copies, waits for them, and re-layouts: 277 us -> 34.6 us
  matrix products: 310 us -> 88.1 us
  other arithmetic: 176 us -> 30.1 us
  blocking collectives: 89.5 us -> 0 us
  loops' own time: 29.1 us -> 0 us
    reduce_scatter x2 -> x0, waiting for transfers between devices: 581 us -> none  [the longest x1 371 us: local(): lax.psum_scatter(grad_w_in, ('seq', 'ctx'), scatter_dimension=0, tiled=True)]
    pallas_call x0 -> x7, Pallas kernels: none -> 428 us  [the longest x1 165 us: reduce_all(): pl.pallas_call(partial(reduce_kernel, n, tuple(lead)), out_shape=made, in...]
    dot_general x33 -> x9, matrix products: 310 us -> 88.1 us  [the longest x1 12.5 us: local(): lax.dot_general(dz, w_z, nt, preferred_element_type=f32)]
    dynamic_update_slice x12 -> x0, local copies, waits for them, and re-layouts: 125 us -> none  [the longest x4 107 us: local(): gated_normalized = lax.map(forward_one, (per_seq, own_ids, prev_id))]
    all_gather x4 -> x0, waiting for transfers between devices: 112 us -> none  [the longest x2 72.4 us: entering(): gathered = jax.tree.map(lambda a: lax.all_gather(a, axis), part)]
    unnamed x8 -> x0, waiting for transfers between devices: 81.4 us -> none
    reduce_sum x11 -> x5, other arithmetic: 53.6 us -> 1.48 us  [the longest x1 0.96 us: local(): dconv = jnp.sum(dconv, axis=0)]
    all_gather x2 -> x0, blocking collectives: 45.7 us -> none  [the longest x1 40 us: local(): lax.all_gather(conv_w, ('seq', 'ctx'), axis=1, tiled=True)]
  transfers between devices with their start and end apart: 10 -> 9, of which waited for: 6 -> 3; matrix products, arithmetic and copies ran while one was open for 15% -> 8% of each run, Pallas kernels for 0% -> 27%
where the time goes in v1:
time: 645 us; the launch traced here: 638 us
  Pallas kernels  428 us (66%)
  matrix products  88.1 us (14%)
  waiting for transfers between devices  39.3 us (6%)
  local copies, waits for them, and re-layouts  34.6 us (5%)
  other arithmetic  30.1 us (5%)
  starting transfers between devices  16.1 us (2%)
    pallas_call x1, Pallas kernels, reduce_all(): pl.pallas_call(partial(reduce_kernel, n, tuple(lead)), out_shape=made, in...  165 us
    pallas_call x1, Pallas kernels, gather_all(): pl.pallas_call(partial(gather_kernel, tuple(units), n), out_shape=[jax.Sh...  143 us
    pallas_call x5, Pallas kernels, call(): pl.pallas_call(kernel, grid=(count,), in_specs=in_specs, out_specs=[spec...  121 us
    ppermute x1, waiting for transfers between devices, local(): back = lax.ppermute(back, 'ctx', [(b, a) for a, b in onward])  30.7 us
    unnamed x69, local copies, waits for them, and re-layouts  15.6 us
  transfers between devices with their start and end apart: 9, of which 3 were waited for; matrix products, arithmetic and copies ran while one was open for 8% of the time, Pallas kernels for 27%

profile of v1, /device:TPU:0, one launch (start us, length us, event | category | flops | bytes accessed | tf_op | source)
XLA Modules:
  0.0 638.3 jit_solution(2701881066363786140)
XLA Ops:
  4.6 4.5 collective-permute-start.1
  14.5 142.6 %shard_map.203 = (bf16[4,2,2,2,48,3376]{5,4,3,2,1,0:T(8,128)(2,1)S(1)}, bf16[4,2,2,2,48,3072]{5,4,3,2,1,0:T(8,128)(2,1)S(1)}, bf16[4,2,2,2,96,1536]{5,4,3,2,1,0:...) custom-call(bf16[48,3376]{1,0:T(8,128)(2,1)S(1)} %slice.96.refs_0_, bf16[48,3072]{1,0:T(8,128)(2,1)S(1)} %slice.97.refs_1_, ...), custom_call_target="tpu_custom_call" | custom-call | tf_op jit(solution)/shard_map/pallas_call | solution.py:507
  157.1 3.9 copy-done.1
  161.1 3.7 copy-done.2
  164.8 3.6 copy-done.3
  174.6 11.5 %convolution_convert_fusion.3.px_ref.tail_ref = bf16[528,3376]{1,0:T(8,128)(2,1)} fusion(bf16[528,1536]{1,0:T(8,128)(2,1)S(1)} %multiply_convert_fusion, bf16[1536,3376]{1,0:T(8,128)(2,1)} %bitcast.81), kind=kOutput, calls=%fused_computation.3 | convolution fusion | flops 5477708800 | bytes 15558144 | tf_op jit(solution)/shard_map/dot_general | solution.py:718
  186.1 20.9 %shard_map.204 = (f32[2,256,3328]{2,1,0:T(8,128)}, f32[2,256,256]{2,1,0:T(8,128)}, f32[2,48,256]{2,1,0:T(8,128)}, f32[2,3072,128]{2,1,0:T(8,128)}) custom-call(bf16[528,3376]{1,0:T(8,128)(2,1)} %convolution_convert_fusion.3.px_ref.tail_ref, bf16[528,3376]{1,0:T(8,128)(2,1)} %convolution_convert_fusion.3.px_ref.tail_ref, f32[8,3328]{1,0:T(8,128)} %pad.46.w_ref, ...), custom_call_target="tpu_custom_call" | custom-call | tf_op jit(solution)/shard_map/pallas_call | solution.py:369
  222.0 7.0 %convolution_bitcast_fusion.dgn_ref = f32[512,3072]{1,0:T(8,128)} fusion(bf16[3072,1536]{1,0:T(8,128)(2,1)S(1)} %bitcast.87, bf16[512,1536]{1,0:T(8,128)(2,1)S(1)} %bitcast.97), kind=kOutput, calls=%fused_computation.6 | convolution fusion | flops 4831838208 | bytes 17301504 | tf_op jit(solution)/shard_map/dot_general | solution.py:739
  230.6 15.4 %shard_map.205.y_ref = f32[2,256,3072]{2,1,0:T(8,128)} custom-call(f32[2,256,3328]{2,1,0:T(8,128)} %get-tuple-element.39.act_ref, f32[2,256,256]{2,1,0:T(8,128)} %get-tuple-element.40.tok_ref, f32[2,48,256]{2,1,0:T(8,128)} %get-tuple-element.41.cst_ref, f32[2,256,128]{2,1,0:T(8,128)} %pad.48.cols_ref, f32[2,8,256]{2,1,0:T(8,128)} %pad.52.rows_ref), custom_call_target="tpu_custom_call" | custom-call | tf_op jit(solution)/shard_map/pallas_call | solution.py:369
  246.1 10.2 %convolution_convert_fusion.4.z_ref = bf16[512,3072]{1,0:T(8,128)(2,1)} fusion(bf16[1536,3072]{1,0:T(8,128)(2,1)} %bitcast.83, bf16[528,1536]{1,0:T(8,128)(2,1)S(1)} %copy-done.11), kind=kOutput, calls=%fused_computation.7 | convolution fusion | flops 4833411072 | bytes 14155776 | tf_op jit(solution)/shard_map/dot_general | solution.py:737
  258.9 31.1 %shard_map.206 = (bf16[512,3072]{1,0:T(8,128)(2,1)}, bf16[512,3072]{1,0:T(8,128)(2,1)}, bf16[2,256,3072]{2,1,0:T(8,128)(2,1)}, f32[2,3072,128]{2,1,0:T(8,128)}, ...) custom-call(bf16[512,3072]{1,0:T(8,128)(2,1)} %convolution_convert_fusion.4.z_ref, ...), custom_call_target="tpu_custom_call" | custom-call | tf_op jit(solution)/shard_map/pallas_call | solution.py:369
  296.4 7.6 %convolution_convert_fusion.2 = bf16[3072,1536]{1,0:T(8,128)(2,1)} fusion(bf16[512,3072]{1,0:T(8,128)(2,1)S(1)} %copy-done.26, bf16[512,1536]{1,0:T(8,128)(2,1)S(1)} %bitcast.98), kind=kOutput, calls=%fused_computation.2 | convolution fusion | flops 4836556800 | bytes 14155776 | tf_op jit(solution)/shard_map/dot_general | solution.py:765
  307.7 6.2 fusion.7
  313.8 17.0 %shard_map.207 = (f32[2,256,3072]{2,1,0:T(8,128)}, f32[2,256,256]{2,1,0:T(8,128)}) custom-call(f32[2,256,3328]{2,1,0:T(8,128)} %get-tuple-element.39.act_ref, f32[2,256,256]{2,1,0:T(8,128)} %get-tuple-element.40.tok_ref, f32[2,48,256]{2,1,0:T(8,128)} %get-tuple-element.41.cst_ref, f32[2,256,128]{2,1,0:T(8,128)} %pad.48.cols_ref, f32[2,8,256]{2,1,0:T(8,128)} %pad.52.rows_ref, ...), custom_call_target="tpu_custom_call" | custom-call | tf_op jit(solution)/shard_map/pallas_call | solution.py:369
  331.2 9.8 %convolution_convert_fusion.1 = bf16[1536,3072]{1,0:T(8,128)(2,1)} fusion(bf16[512,3072]{1,0:T(8,128)(2,1)} %get-tuple-element.53, bf16[528,1536]{1,0:T(8,128)(2,1)} %copy-done.10), kind=kOutput, calls=%fused_computation.1 | convolution fusion | flops 4836556800 | bytes 14155776 | tf_op jit(solution)/shard_map/dot_general | solution.py:766
  341.0 5.7 collective-permute-done.7
  346.6 3.0 add.92.later_ref
  349.6 36.3 %shard_map.208 = (bf16[512,3456]{1,0:T(8,128)(2,1)}, f32[2,8,3456]{2,1,0:T(8,128)}, f32[2,8,3328]{2,1,0:T(8,128)}, f32[2,8,128]{2,1,0:T(8,128)}) custom-call(bf16[528,3376]{1,0:T(8,128)(2,1)} %convolution_convert_fusion.3.px_ref.tail_ref, bf16[528,3376]{1,0:T(8,128)(2,1)} %convolution_convert_fusion.3.px_ref.tail_ref, f32[8,3328]{1,0:T(8,128)} %pad.46.w_ref, ...), custom_call_target="tpu_custom_call" | custom-call | tf_op jit(solution)/shard_map/pallas_call | solution.py:369
  386.8 12.2 %fusion.1 = f32[528,1536]{1,0:T(8,128)} fusion(bf16[1536,3376]{1,0:T(8,128)(2,1)} %bitcast.82, bf16[16,3456]{1,0:T(8,128)(2,1)S(1)} %convert_bitcast_fusion, bf16[512,3456]{1,0:T(8,128)(2,1)} %get-tuple-element.51), kind=kOutput, calls=%fused_computation.9 | convolution fusion | flops 5483056128 | bytes 17264640 | tf_op jit(solution)/shard_map/dot_general | solution.py:797
  399.1 11.3 %convolution_convert_fusion = bf16[1536,3456]{1,0:T(8,128)(2,1)} fusion(bf16[528,1536]{1,0:T(8,128)(2,1)S(1)} %copy-done.12, bf16[16,3456]{1,0:T(8,128)(2,1)S(1)} %convert_bitcast_fusion, bf16[512,3456]{1,0:T(8,128)(2,1)S(1)} %copy-done.25), kind=kOutput, calls=%fused_computation | convolution fusion | flops 5618294784 | bytes 15888384 | tf_op jit(solution)/shard_map/dot_general | solution.py:795
  414.6 30.7 %collective-permute-done.8 = bf16[2,3,1536]{2,1,0:T(4,128)(2,1)S(1)} collective-permute-done((bf16[2,3,1536]{2,1,0:T(4,128)(2,1)S(1)}, bf16[2,3,1536]{2,1,0:T(4,128)(2,1)S(1)}, u32[]{:S(2)}, u32[]{:S(2)}) %collective-permute-start.8) | collective-permute-done | bytes 18464 | tf_op jit(solution)/shard_map/ppermute | solution.py:800
  445.5 12.5 %multiply_reduce_fusion.1 = (f32[1536]{0:T(1024)S(1)}, f32[512]{0:T(512)}, f32[512,1536]{1,0:T(8,128)}) fusion(f32[528,1536]{1,0:T(8,128)S(1)} %maximum_convert_fusion, f32[512]{0:T(512)S(1)} %get-tuple-element.81, f32[1536]{0:T(1024)S(1)} %mul.129, bf16[2,256,1536]{2,1,0:T(8,128)(2,1)S(1)} %pad.54, f32[528,1536]{1,0:T(8,128)} %fusion.1, ...), kind=kOutput, calls=%fused_computation.18 | convolution fusion | flops 4838914048 | bytes 23609344 | tf_op jit(solution)/shard_map/dot_general | solution.py:798
  460.2 164.9 %shard_map.209 = (f32[96,1536]{1,0:T(8,128)}, f32[48,3072]{1,0:T(8,128)}, f32[48,3456]{1,0:T(8,128)}, f32[8,128]{1,0:T(8,128)}) custom-call(bf16[4,2,2,2,96,1536]{5,4,3,2,1,0:T(8,128)(2,1)} %bitcast.95, bf16[4,2,2,2,48,3072]{5,4,3,2,1,0:T(8,128)(2,1)} %bitcast.96, bf16[4,2,2,2,48,3456]{5,4,3,2,1,0:T(8,128)(2,1)} %bitcast.94, f32[4,2,2,2,8,128]{5,4,3,2,1,0:T(8,128)} %bitcast.101), custom_call_target="tpu_custom_call" | custom-call | tf_op jit(solution)/shard_map/pallas_call | solution.py:649
  633.0 4.0 add_convert_fusion
  (170 shorter events, 61.0 us)
Async XLA Ops:
  0.6 170.3 %copy-start.18 = (s32[2,256]{1,0:T(2,128)S(1)}, s32[2,256]{1,0:T(2,128)}, u32[]{:S(2)}) copy-start(s32[2,256]{1,0:T(2,128)} %param.22) | copy-start | bytes 6148
  0.7 169.6 %copy-start.24 = (f32[48]{0:T(128)S(1)}, f32[48]{0:T(128)}, u32[]{:S(2)}) copy-start(f32[48]{0:T(128)} %param.17) | copy-start | bytes 580
  0.7 169.6 %copy-start.23 = (f32[48]{0:T(128)S(1)}, f32[48]{0:T(128)}, u32[]{:S(2)}) copy-start(f32[48]{0:T(128)} %param.18) | copy-start | bytes 580
  1.5 171.0 %collective-permute-start = (bf16[2,3,1536]{2,1,0:T(4,128)(2,1)S(1)}, bf16[2,3,1536]{2,1,0:T(4,128)(2,1)S(1)}, u32[]{:S(2)}, u32[]{:S(2)}) collective-permute-start(bf16[2,3,1536]{2,1,0:T(4,128)(2,1)S(1)} %slice.94), channel_id=1, source_target_pairs={{0,1},{1,2},{2,3},{4,5},{5,6},{6,7},{8,9},{9,10},{10,11},{12,13},{... | collective-permute-start | bytes 55304 | tf_op jit(solution)/shard_map/ppermute | solution.py:696
  4.6 166.3 %collective-permute-start.1 = (s32[2,3]{1,0:T(2,128)S(1)}, s32[2,3]{1,0:T(2,128)S(1)}, u32[]{:S(2)}, u32[]{:S(2)}) collective-permute-start(s32[2,3]{1,0:T(2,128)S(1)} %slice.100), channel_id=1, source_target_pairs={{0,1},{1,2},{2,3},{4,5},{5,6},{6,7},{8,9},{9,10},{10,11},{12,13},{... | collective-permute-start | bytes 80 | tf_op jit(solution)/shard_map/ppermute | solution.py:697
  14.5 158.1 %copy-start.6 = (bf16[2,256,1536]{2,1,0:T(8,128)(2,1)S(1)}, bf16[2,256,1536]{2,1,0:T(8,128)(2,1)}, u32[]{:S(2)}) copy-start(bf16[2,256,1536]{2,1,0:T(8,128)(2,1)} %param.12) | copy-start | bytes 4718596
  208.5 13.5 %slice-start = ((s8[9437184]{0:T(1024)(128)(4,1)}), s8[4194304]{0:T(1024)(128)(4,1)S(1)}, s32[]{:S(2)}) async-start(s8[9437184]{0:T(1024)(128)(4,1)} %bitcast.85), calls=%async_computation | async-start | bytes 8388608
  211.0 5.8 collective-permute-start.2
  217.9 0.9 collective-permute-start.3
  221.1 35.2 %collective-permute-start.4 = (bf16[2,3072,128]{2,1,0:T(8,128)(2,1)}, bf16[2,3072,128]{2,1,0:T(8,128)(2,1)S(1)}, u32[]{:S(2)}, u32[]{:S(2)}) collective-permute-start(bf16[2,3072,128]{2,1,0:T(8,128)(2,1)} %get-tuple-element.70), channel_id=1, source_target_pairs={{2,3},{6,7},{10,11},{14,15},{18,19},{22,23},{26,27},{30,31}} | collective-permute-start | bytes 4718600 | tf_op jit(solution)/shard_map/ppermute | solution.py:384
  230.6 15.4 %copy-start.11 = (bf16[528,1536]{1,0:T(8,128)(2,1)S(1)}, bf16[528,1536]{1,0:T(8,128)(2,1)}, u32[]{:S(2)}) copy-start(bf16[528,1536]{1,0:T(8,128)(2,1)} %copy-done.10) | copy-start | bytes 4866052
  292.6 1.4 collective-permute-start.5
  294.4 13.2 %slice-start.3 = ((s8[9437184]{0:T(1024)(128)(4,1)}), s8[4194304]{0:T(1024)(128)(4,1)S(1)}, s32[]{:S(2)}) async-start(s8[9437184]{0:T(1024)(128)(4,1)} %bitcast.88), calls=%async_computation.3 | async-start | bytes 8388608
  295.4 8.5 %collective-permute-start.6 = (bf16[2,3072,128]{2,1,0:T(8,128)(2,1)S(1)}, bf16[2,3072,128]{2,1,0:T(8,128)(2,1)S(1)}, u32[]{:S(2)}, u32[]{:S(2)}) collective-permute-start(bf16[2,3072,128]{2,1,0:T(8,128)(2,1)S(1)} %add_convert_fusion.2), channel_id=1, source_target_pairs={{2,1},{6,5},{10,9},{14,13},{18,17},{22,21},{26,25},{30,29}} | collective-permute-start | bytes 4718600 | tf_op jit(solution)/shard_map/ppermute | solution.py:384
  296.4 11.2 %slice-start.5 = ((s8[9437184]{0:T(1024)(128)(4,1)}), s8[1048576]{0:T(1024)(128)(4,1)S(1)}, s32[]{:S(2)}) async-start(s8[9437184]{0:T(1024)(128)(4,1)} %bitcast.88), calls=%async_computation.5 | async-start | bytes 2097152
  306.1 40.5 %collective-permute-start.7 = (bf16[2,3072,128]{2,1,0:T(8,128)(2,1)}, bf16[2,3072,128]{2,1,0:T(8,128)(2,1)}, u32[]{:S(2)}, u32[]{:S(2)}) collective-permute-start(bf16[2,3072,128]{2,1,0:T(8,128)(2,1)} %get-tuple-element.68), channel_id=1, source_target_pairs={{1,0},{5,4},{9,8},{13,12},{17,16},{21,20},{25,24},{29,28}} | collective-permute-start | bytes 4718600 | tf_op jit(solution)/shard_map/ppermute | solution.py:384
  313.8 17.0 %copy-start.17 = (f32[2,8,3072]{2,1,0:T(8,128)S(1)}, f32[2,8,3072]{2,1,0:T(8,128)}, u32[]{:S(2)}) copy-start(f32[2,8,3072]{2,1,0:T(8,128)} %get-tuple-element.54) | copy-start | bytes 589828
  331.2 15.4 %copy-start.8 = (bf16[2,3072,128]{2,1,0:T(8,128)(2,1)S(1)}, bf16[2,3072,128]{2,1,0:T(8,128)(2,1)}, u32[]{:S(2)}) copy-start(bf16[2,3072,128]{2,1,0:T(8,128)(2,1)} %get-tuple-element.69) | copy-start | bytes 4718596
  386.8 12.3 %copy-start.12 = (bf16[528,1536]{1,0:T(8,128)(2,1)S(1)}, bf16[528,1536]{1,0:T(8,128)(2,1)}, u32[]{:S(2)}) copy-start(bf16[528,1536]{1,0:T(8,128)(2,1)} %copy-done.10) | copy-start | bytes 4866052
  386.8 12.3 %copy-start.25 = (bf16[512,3456]{1,0:T(8,128)(2,1)S(1)}, bf16[512,3456]{1,0:T(8,128)(2,1)}, u32[]{:S(2)}) copy-start(bf16[512,3456]{1,0:T(8,128)(2,1)} %get-tuple-element.51) | copy-start | bytes 10616836
  399.1 11.3 %copy-start.19 = (f32[2,8,128]{2,1,0:T(8,128)S(1)}, f32[2,8,128]{2,1,0:T(8,128)}, u32[]{:S(2)}) copy-start(f32[2,8,128]{2,1,0:T(8,128)} %get-tuple-element.56) | copy-start | bytes 24580
  411.3 34.0 %collective-permute-start.8 = (bf16[2,3,1536]{2,1,0:T(4,128)(2,1)S(1)}, bf16[2,3,1536]{2,1,0:T(4,128)(2,1)S(1)}, u32[]{:S(2)}, u32[]{:S(2)}) collective-permute-start(bf16[2,3,1536]{2,1,0:T(4,128)(2,1)S(1)} %slice.132), channel_id=1, source_target_pairs={{1,0},{2,1},{3,2},{5,4},{6,5},{7,6},{9,8},{10,9},{11,10},{13,12},{... | collective-permute-start | bytes 55304 | tf_op jit(solution)/shard_map/ppermute | solution.py:800
  445.4 13.2 %copy-start.20 = (f32[144]{0:T(256)S(1)}, f32[144]{0:T(256)}, u32[]{:S(2)}) copy-start(f32[144]{0:T(256)} %pad_maximum_fusion.3) | copy-start | bytes 1732
  460.2 170.3 %copy-start.21 = (f32[512]{0:T(512)S(1)}, f32[512]{0:T(512)}, u32[]{:S(2)}) copy-start(f32[512]{0:T(512)} %get-tuple-element.62) | copy-start | bytes 6148
  (18 other events, 88.4 us)

commit v2 on v1

--- a/solution.py
+++ b/solution.py
@@ -377,12 +377,17 @@
     )(*args)
 
 
-def chain(own, factor, steps):
+def chain(own, factor, steps, beside):
     entered = jnp.zeros(own.shape, bf16)
-    for source, target in steps:
-        sent = (own + factor * entered.astype(f32)).astype(bf16)
-        entered = entered + lax.ppermute(sent, "ctx", [(source, target)])
-    return entered
+    results = []
+    for k, (source, target) in enumerate(steps):
+        sent = own.astype(bf16) if k == 0 else (own + factor * entered.astype(f32)).astype(bf16)
+        came = lax.ppermute(sent, "ctx", [(source, target)])
+        for work in beside[k :: len(steps)]:
+            results.append(work())
+            came, results[-1] = lax.optimization_barrier((came, results[-1]))
+        entered = came if k == 0 else entered + came
+    return entered, results
 
 
 def pad_lanes(v):
@@ -401,13 +406,13 @@
     return {"seq": z * 2 + y, "ctx": x * 2 + c}
 
 
-def greet(z, y, x, c):
+def greet(z, y, x, c, more=0):
     barrier = pltpu.get_barrier_semaphore()
     others = [device(z, y, x, 1 - c), device(z, y, 1 - x, c), device(z, 1 - y, x, c)]
     others += [device(lax.rem(z + d, NZ), y, x, c) for d in range(1, NZ)]
     for other in others:
         pl.semaphore_signal(barrier, inc=1, device_id=other, device_id_type=pl.DeviceIdType.MESH)
-    pl.semaphore_wait(barrier, len(others))
+    pl.semaphore_wait(barrier, len(others) + more)
 
 
 def remote(src, dst, send, recv, target):
@@ -418,105 +423,148 @@
 
 
 def gather_kernel(units, n, *refs):
-    ins, outs, (send, recv, local) = refs[:n], refs[n : 2 * n], refs[2 * n :]
+    ins, outs, land, (tail_land, send, recv, local, store, tail_sem) = (
+        refs[: n + 1], refs[n + 1 : 2 * n + 2], refs[2 * n + 2 : 3 * n + 2], refs[3 * n + 2 :]
+    )
     x_first = [first for _array, _row, _rows, first in units]
     z, y, x, c = place()
-    greet(z, y, x, c)
-    started = []
+    ctx = x * 2 + c
+    after, before = lax.rem(ctx + 1, 4), lax.rem(ctx + 3, 4)
+    barrier = pltpu.get_barrier_semaphore()
+    for other in (after, before):
+        pl.semaphore_signal(
+            barrier, inc=1, device_id={"seq": z * 2 + y, "ctx": other},
+            device_id_type=pl.DeviceIdType.MESH,
+        )
+    greet(z, y, x, c, 2)
+    started, stored = [], []
 
     def shard(u):
         a, row, rows, _first = units[u]
         return ins[a].at[pl.ds(row, rows)]
 
-    def slot_of(u, *at):
+    def slot_of(u, *at, into=None):
         a, row, rows, _first = units[u]
-        return outs[a].at[at + (pl.ds(row, rows),)]
-
-    def push(u, zz, yy, xx, stage, own=False):
-        slot = slot_of(u, zz, yy, xx, c)
-        kind, index = stage
-        target = {
-            "x": device(z, y, 1 - x, c), "y": device(z, 1 - y, x, c), "c": device(z, y, x, 1 - c),
-        }.get(kind)
-        if kind == "z":
-            target = device(lax.rem(z + index, NZ), y, x, c)
-        copy = remote(shard(u) if own else slot, slot, send.at[u, number(u, stage)], recv.at[u, number(u, stage)], target)
-        copy.start()
-        started.append(copy)
-        return copy
-
-    def number(u, stage):
-        kind, index = stage
+        return (land if into is None else into)[a].at[at + (pl.ds(row, rows),)]
+
+    def number(u, kind, index):
         first = "x" if x_first[u] else "y"
         base = 0 if kind == "z" else 3 if kind == first else 15 if kind == "c" else 7
         return base + (index - 1 if kind == "z" else index)
 
-    def came(u, zz, yy, xx, cc, stage):
+    def push(u, zz, yy, xx, kind, index):
+        slot = slot_of(u, zz, yy, xx, c)
+        if kind == "z":
+            target = device(lax.rem(z + index, NZ), y, x, c)
+        else:
+            flip = [1 - v if k == kind else v for k, v in (("y", y), ("x", x), ("c", c))]
+            target = device(z, *flip)
+        k = number(u, kind, index)
+        copy = remote(slot, slot, send.at[u, k], recv.at[u, k], target)
+        copy.start()
+        started.append(copy)
+
+    def came(u, zz, yy, xx, cc, kind, index):
         slot = slot_of(u, zz, yy, xx, cc)
-        k = number(u, stage)
+        k = number(u, kind, index)
         remote(slot, slot, send.at[u, k], recv.at[u, k], device(z, y, x, 1 - c)).wait_recv()
+        keep = pltpu.make_async_copy(slot, slot_of(u, zz, yy, xx, cc, into=outs), store.at[u, k])
+        keep.start()
+        stored.append(keep)
 
     back = [lax.rem(z + NZ - d, NZ) for d in range(NZ)]
-    own_copies = []
-    for u in range(len(units)):
-        a, b = ("x", "y") if x_first[u] else ("y", "x")
-        for d in range(1, NZ):
-            push(u, z, y, x, ("z", d), own=True)
-        push(u, z, y, x, (b, 0), own=True)
-        push(u, z, y, x, (a, 0), own=True)
-        push(u, z, y, x, ("c", 0), own=True)
-        own_copies.append(pltpu.make_async_copy(shard(u), slot_of(u, z, y, x, c), local.at[u]))
-        own_copies[-1].start()
-    for d in range(1, NZ + 1):
-        for u in range(len(units)):
-            a, b = ("x", "y") if x_first[u] else ("y", "x")
+    axes = [("x", "y") if first else ("y", "x") for first in x_first]
+    every = range(len(units))
+    ring = remote(
+        ins[n], tail_land, tail_sem.at[0], tail_sem.at[1], {"seq": z * 2 + y, "ctx": after}
+    )
+    ring.start()
+    for u in every:
+        pltpu.make_async_copy(shard(u), slot_of(u, z, y, x, c), local.at[u]).start()
+
+    def open_unit(u):
+        a, b = axes[u]
+        slot = slot_of(u, z, y, x, c)
+        pltpu.make_async_copy(shard(u), slot, local.at[u]).wait()
+        for d in (1, 3, 2):
+            push(u, z, y, x, "z", d)
+        for kind in (b, a, "c"):
+            push(u, z, y, x, kind, 0)
+        keep = pltpu.make_async_copy(slot, slot_of(u, z, y, x, c, into=outs), local.at[u])
+        keep.start()
+        stored.append(keep)
+
+    def pass_on(u):
+        a, b = axes[u]
+        yy, xx = (y, 1 - x) if a == "x" else (1 - y, x)
+        for d in range(1, NZ + 1):
             if d < NZ:
-                came(u, back[d], y, x, c, ("z", d))
-                push(u, back[d], y, x, (b, d))
-                push(u, back[d], y, x, (a, d))
-                push(u, back[d], y, x, ("c", d))
-            yy, xx = (y, 1 - x) if a == "x" else (1 - y, x)
-            came(u, back[d - 1], yy, xx, c, (a, d - 1))
-            push(u, back[d - 1], yy, xx, (b, NZ + d - 1))
-            push(u, back[d - 1], yy, xx, ("c", NZ + d - 1))
-    for half in range(2):
-        for d in range(NZ):
-            for u in range(len(units)):
-                a, b = ("x", "y") if x_first[u] else ("y", "x")
-                yy, xx = (1 - y, x) if b == "y" else (y, 1 - x)
-                if half:
-                    yy, xx = 1 - y, 1 - x
-                came(u, back[d], yy, xx, c, (b, NZ * half + d))
-                push(u, back[d], yy, xx, ("c", 2 * NZ + NZ * half + d))
-    for u in range(len(units)):
+                came(u, back[d], y, x, c, "z", d)
+                for kind in (b, a, "c"):
+                    push(u, back[d], y, x, kind, d)
+            came(u, back[d - 1], yy, xx, c, a, d - 1)
+            push(u, back[d - 1], yy, xx, b, NZ + d - 1)
+            push(u, back[d - 1], yy, xx, "c", NZ + d - 1)
+
+    def cross(u):
+        a, b = axes[u]
+        for half in range(2):
+            yy, xx = (1 - y, x) if b == "y" else (y, 1 - x)
+            if half:
+                yy, xx = 1 - y, 1 - x
+            for d in range(NZ):
+                came(u, back[d], yy, xx, c, b, NZ * half + d)
+                push(u, back[d], yy, xx, "c", 2 * NZ + NZ * half + d)
+
+    def finish(u):
+        a, b = axes[u]
         for k in range(16):
-            a = "x" if x_first[u] else "y"
-            away_a, away_b = (k // NZ) % 2, k // (2 * NZ)
-            ax, ay = (away_a, away_b) if a == "x" else (away_b, away_a)
-            xx = 1 - x if ax else x
-            yy = 1 - y if ay else y
-            came(u, back[k % NZ], yy, xx, 1 - c, ("c", k))
+            away = {a: (k // NZ) % 2, b: k // (2 * NZ)}
+            came(u, back[k % NZ], 1 - y if away["y"] else y, 1 - x if away["x"] else x, 1 - c, "c", k)
+
+    for t in range(-AHEAD, len(units) + 4):
+        if 0 <= t + AHEAD < len(units):
+            open_unit(t + AHEAD)
+        if 0 <= t < len(units):
+            pass_on(t)
+        if 0 <= t - 2 < len(units):
+            cross(t - 2)
+        if 0 <= t - 4 < len(units):
+            finish(t - 4)
+    ring.wait_recv()
+    keep = pltpu.make_async_copy(tail_land, outs[n], tail_sem.at[2])
+    keep.start()
+    keep.wait()
+    ring.wait_send()
     for copy in started:
         copy.wait_send()
-    for copy in own_copies:
-        copy.wait()
-
-
-def gather_all(shards, units):
+    for keep in stored:
+        keep.wait()
+
+
+def gather_all(shards, tail, units):
     n, m = len(shards), len(units)
+    full = [(NZ, 2, 2, 2) + v.shape for v in shards]
     return pl.pallas_call(
         partial(gather_kernel, tuple(units), n),
-        out_shape=[jax.ShapeDtypeStruct((NZ, 2, 2, 2) + v.shape, v.dtype) for v in shards],
-        in_specs=[pl.BlockSpec(memory_space=pl.ANY)] * n,
-        out_specs=[pl.BlockSpec(memory_space=pl.ANY)] * n,
-        scratch_shapes=[
-            pltpu.SemaphoreType.DMA((m, 31)), pltpu.SemaphoreType.DMA((m, 31)), pltpu.SemaphoreType.DMA((m,)),
+        out_shape=[jax.ShapeDtypeStruct(f, v.dtype) for f, v in zip(full, shards)]
+        + [jax.ShapeDtypeStruct(tail.shape, tail.dtype)],
+        in_specs=[pl.BlockSpec(memory_space=pl.ANY)] * (n + 1),
+        out_specs=[pl.BlockSpec(memory_space=pl.ANY)] * (n + 1),
+        scratch_shapes=[pltpu.VMEM(f, v.dtype) for f, v in zip(full, shards)] + [
+            pltpu.VMEM(tail.shape, tail.dtype),
+            pltpu.SemaphoreType.DMA((m, 31)), pltpu.SemaphoreType.DMA((m, 31)),
+            pltpu.SemaphoreType.DMA((m,)), pltpu.SemaphoreType.DMA((m, 31)),
+            pltpu.SemaphoreType.DMA((3,)),
         ],
-        compiler_params=pltpu.CompilerParams(collective_id=0, has_side_effects=True, vmem_limit_bytes=8 * 1024 * 1024),
-    )(*shards)
+        compiler_params=pltpu.CompilerParams(
+            collective_id=0, has_side_effects=True, vmem_limit_bytes=VMEM
+        ),
+    )(*shards, tail)
 
 
 CUT_ROWS, CUT = 48, 512
+AHEAD = 4
 
 
 def cuts_of(shape):
@@ -667,21 +715,30 @@
     shares = [norm_gain.shape[0], gate_gain.shape[0], CONV * conv_b.shape[0], conv_b.shape[0]]
     cuts = [sum(shares[: i + 1]) for i in range(3)]
     packed = jnp.concatenate([norm_gain, gate_gain, conv_w.reshape(-1), conv_b])
+    onward = [(i, i + 1) for i in range(n_ctx - 1)]
+    tail = jnp.pad(tokens[:, length - (CONV - 1) :], ((0, 0), (8 - (CONV - 1), 0), (0, 0)))
+    tail_ids = jnp.pad(
+        segments[:, length - (CONV - 1) :].astype(bf16), ((0, 0), (0, width - (CONV - 1)))
+    )
+    tail = jnp.concatenate([tail_ids[:, None], tail[:, 1:]], axis=1).reshape(seqs * 8, width)
     torus = lax.axis_size("seq") == 2 * NZ and n_ctx == 4 and norm_gain.shape[0] == CUT_ROWS
     w_z, w_x = input_weight[:, :INNER], input_weight[:, INNER:]
     if torus:
         size = packed.shape[0]
         small = jnp.pad(packed, (0, 16 * LANES - size)).reshape(16, LANES)
-        half = output_weight.shape[0] // 2
-        w_x, w_z, w_out, packed = gather_all(
-            [w_x, w_z, output_weight, small],
-            [(0, 0, CUT_ROWS, True), (1, 0, CUT_ROWS, False), (2, 0, half, True),
-             (2, half, half, False), (3, 0, 16, True)],
+        w_out = lax.all_gather(output_weight, BOTH, axis=0, tiled=True)
+        w_z = lax.all_gather(w_z, BOTH, axis=0, tiled=True)
+        w_x, packed, tail = gather_all(
+            [w_x, small], tail,
+            [(1, 0, 16, True)]
+            + [(0, 16 * k, 16, k % 2 == 0) for k in range(3)]
+,
         )
         w_x, w_z, w_out = (w.reshape(-1, w.shape[-1]) for w in (w_x, w_z, w_out))
         packed = packed.reshape(n_all, -1)[:, :size]
     else:
         packed = lax.all_gather(packed, BOTH, axis=0)
+        tail = lax.ppermute(tail, "ctx", onward)
         w_in, w_out = (
             lax.all_gather(w, BOTH, axis=0, tiled=True) for w in (input_weight, output_weight)
         )
@@ -692,12 +749,13 @@
     conv_b_full = conv_b_full.reshape(1, -1)
     conv_w_full = conv_w_full.reshape(n_all, CONV, -1).transpose(1, 0, 2).reshape(CONV, -1)
 
-    onward = [(i, i + 1) for i in range(n_ctx - 1)]
-    tail_tokens = lax.ppermute(tokens[:, length - (CONV - 1) :], "ctx", onward)
-    tail_ids = lax.ppermute(segments[:, length - (CONV - 1) :], "ctx", onward)
-    tail_ids = jnp.where(lax.axis_index("ctx") == 0, -1, tail_ids)
-    tail_tokens = jnp.pad(tail_tokens, ((0, 0), (8 - (CONV - 1), 0), (0, 0)))
-    x_all = jnp.concatenate([tokens.reshape(count, width), tail_tokens.reshape(seqs * 8, width)])
+    tail = tail.reshape(seqs, 8, width)
+    tail_ids = jnp.where(
+        lax.axis_index("ctx") == 0, -1, tail[:, 0, : CONV - 1].astype(jnp.int32)
+    )
+    tail = jnp.pad(tail[:, 8 - (CONV - 1) :], ((0, 0), (8 - (CONV - 1), 0), (0, 0)))
+    tail = jnp.where(lax.axis_index("ctx") == 0, 0, tail)
+    x_all = jnp.concatenate([tokens.reshape(count, width), tail.reshape(seqs * 8, width)])
     x_all = x_all.astype(f32)
     r_all = lax.rsqrt(jnp.mean(x_all * x_all, axis=-1, keepdims=True) + EPSILON)
     normed = (x_all * r_all * norm_full).astype(bf16)
@@ -732,19 +790,27 @@
     carried = cols[:, length - 1, 3]
     kept = jnp.exp(cst[:, :, length - 1]) * carried[:, None]
     kept = jnp.repeat(kept, HEADDIM, axis=1)[..., None]
-    entering = chain(fresh, kept, onward)
+    g2 = cotangent.reshape(count, width)
+
+    def gate_gradient():
+        return lax.dot_general(g2, w_out, (((1,), (1,)), ((), ())), preferred_element_type=f32)
+
+    def within():
+        [y] = call(
+            within_kernel, seqs,
+            [per_seq(length, CHANNELS), per_seq(length, 2 * LANES), per_seq(HEADS, length),
+             per_seq(length, LANES), per_seq(8, length)],
+            [(per_seq(length, INNER), ((seqs, length, INNER), f32))],
+            [pltpu.VMEM((length, length), f32), pltpu.VMEM((length, length), f32)],
+            act, tok, cst, cols, rows,
+        )
+        return y
+
+    def gates():
+        return MM(normed[:count], w_z).astype(bf16)
+
+    entering, (dgn, y, pz) = chain(fresh, kept, onward, (gate_gradient, within, gates))
     stayed = kept * entering.astype(f32)
-    pz = MM(normed[:count], w_z).astype(bf16)
-    g2 = cotangent.reshape(count, width)
-    dgn = lax.dot_general(g2, w_out, (((1,), (1,)), ((), ())), preferred_element_type=f32)
-    [y] = call(
-        within_kernel, seqs,
-        [per_seq(length, CHANNELS), per_seq(length, 2 * LANES), per_seq(HEADS, length),
-         per_seq(length, LANES), per_seq(8, length)],
-        [(per_seq(length, INNER), ((seqs, length, INNER), f32))],
-        [pltpu.VMEM((length, length), f32), pltpu.VMEM((length, length), f32)],
-        act, tok, cst, cols, rows,
-    )
     gn, dz, dy, dstate, dqueries, ddecay, sums = call(
         gate_kernel, seqs,
         [per_rows(length, INNER), per_seq(length, CHANNELS), per_seq(length, 2 * LANES),
@@ -760,18 +826,28 @@
         [pltpu.VMEM((length, INNER), f32), pltpu.VMEM((length, STATE), f32)],
         pz, act, tok, cols, y, entering, dgn, lanes,
     )
-    later = chain(dstate, kept, [(b, a) for a, b in reversed(onward)])
-    output = (x_all[:count] + MM(gn, w_out)).astype(bf16)
-    dw_out = lax.dot_general(gn, g2, (((0,), (0,)), ((), ())), preferred_element_type=f32)
-    dw_z = lax.dot_general(normed[:count], dz, (((0,), (0,)), ((), ())), preferred_element_type=f32)
-    dx, dbc = call(
-        scan_back_kernel, seqs,
-        [per_seq(length, CHANNELS), per_seq(length, 2 * LANES), per_seq(HEADS, length),
-         per_seq(length, LANES), per_seq(8, length), per_seq(length, INNER)],
-        [(per_seq(length, INNER), ((seqs, length, INNER), f32)),
-         (per_seq(length, 2 * STATE), ((seqs, length, 2 * STATE), f32))],
-        [pltpu.VMEM((length, length), f32)] * 3,
-        act, tok, cst, cols, rows, dy,
+    tn = (((0,), (0,)), ((), ()))
+
+    def products():
+        out = (x_all[:count] + MM(gn, w_out)).astype(bf16)
+        return out, lax.dot_general(gn, g2, tn, preferred_element_type=f32).astype(bf16)
+
+    def scan_back():
+        return call(
+            scan_back_kernel, seqs,
+            [per_seq(length, CHANNELS), per_seq(length, 2 * LANES), per_seq(HEADS, length),
+             per_seq(length, LANES), per_seq(8, length), per_seq(length, INNER)],
+            [(per_seq(length, INNER), ((seqs, length, INNER), f32)),
+             (per_seq(length, 2 * STATE), ((seqs, length, 2 * STATE), f32))],
+            [pltpu.VMEM((length, length), f32)] * 3,
+            act, tok, cst, cols, rows, dy,
+        )
+
+    def gate_weights():
+        return lax.dot_general(normed[:count], dz, tn, preferred_element_type=f32).astype(bf16)
+
+    later, ((output, dw_out), (dx, dbc), dw_z) = chain(
+        dstate, kept, [(b, a) for a, b in reversed(onward)], (products, scan_back, gate_weights)
     )
     dpx, edge, dconv, dheads = call(
         after_kernel, seqs,
@@ -792,17 +868,19 @@
         later, stayed,
     )
     dpx_all = jnp.concatenate([dpx, edge.reshape(seqs * 8, dpx_width).astype(bf16)])
-    dw_x = lax.dot_general(normed, dpx_all, (((0,), (0,)), ((), ())), preferred_element_type=f32)
     nt = (((1,), (1,)), ((), ()))
     dnormed_x = lax.dot_general(dpx_all[:, :px_width], w_x, nt, preferred_element_type=f32)
     dnormed = dnormed_x[:count] + lax.dot_general(dz, w_z, nt, preferred_element_type=f32)
     back = dnormed_x[count:].reshape(seqs, 8, width)[:, 8 - (CONV - 1) :].astype(bf16)
     back = lax.ppermute(back, "ctx", [(b, a) for a, b in onward])
+    dw_x = lax.dot_general(normed, dpx_all, tn, preferred_element_type=f32).astype(bf16)
+    x, r = x_all[:count], r_all[:count]
+    d_gain = jnp.sum(x * r * dnormed, axis=0) + jnp.sum(
+        x_all[count:] * r_all[count:] * dnormed_x[count:], axis=0
+    )
+    back, d_gain, dw_x = lax.optimization_barrier((back, d_gain, dw_x))
     back = jnp.pad(back.astype(f32), ((0, 0), (length - (CONV - 1), 0), (0, 0)))
-    dnormed = dnormed + back.reshape(count, width)
-    x, r = x_all[:count], r_all[:count]
-    d_gain = jnp.sum(x * r * dnormed, axis=0)
-    scaled = norm_full * dnormed
+    scaled = norm_full * (dnormed + back.reshape(count, width))
     dx_in = r * (scaled - x * (r * r) * jnp.mean(x * scaled, axis=-1, keepdims=True))
     input_grad = (g2.astype(f32) + dx_in).astype(bf16)
 
@@ -819,8 +897,9 @@
     if torus:
         fill = 8 * LANES - share - shared.shape[0]
         split = [split, jnp.broadcast_to(shared, (n_all,) + shared.shape), jnp.zeros((n_all, fill), f32)]
-        dw_out, dw_z, dw_x, mine = reduce_all(
-            [v.astype(bf16) for v in (dw_out, dw_z, dw_x)],
+        dw_out = lax.psum_scatter(dw_out, BOTH, scatter_dimension=0, tiled=True).astype(f32)
+        dw_z, dw_x, mine = reduce_all(
+            [dw_z, dw_x],
             jnp.concatenate(split, axis=1).reshape(n_all, 8, LANES),
         )
         dw_in = jnp.concatenate([dw_z, dw_x[:, :px_width]], axis=1)
@@ -829,7 +908,8 @@
     else:
         dw_in = jnp.concatenate([dw_z, dw_x[:, :px_width]], axis=1)
         dw_out, dw_in = (
-            lax.psum_scatter(v, BOTH, scatter_dimension=0, tiled=True) for v in (dw_out, dw_in)
+            lax.psum_scatter(v.astype(f32), BOTH, scatter_dimension=0, tiled=True)
+            for v in (dw_out, dw_in)
         )
         every = lax.psum(jnp.concatenate([split.reshape(-1), shared]), BOTH)
         me = lax.axis_index("seq") * n_ctx + lax.axis_index("ctx")

time: 645 us -> 537 us (0.83)
  Pallas kernels: 428 us -> 329 us
  waiting for transfers between devices: 39.3 us -> 11.4 us
  other arithmetic: 30.1 us -> 46.1 us
  between operations: 1.72 us -> 14.7 us
  local copies, waits for them, and re-layouts: 34.6 us -> 23.2 us
    pallas_call x1, Pallas kernels: 143 us -> 90.8 us  [gather_all(): pl.pallas_call(partial(gather_kernel, tuple(units), n), out_shape=[jax.Sh...]
    pallas_call x1, Pallas kernels: 165 us -> 117 us  [reduce_all(): pl.pallas_call(partial(reduce_kernel, n, tuple(lead)), out_shape=made, in...]
    ppermute x1, waiting for transfers between devices: 30.7 us -> 0.01 us  [local(): back = lax.ppermute(back, 'ctx', [(b, a) for a, b in onward])]
    unnamed x69 -> x48, local copies, waits for them, and re-layouts: 15.6 us -> 2.91 us
    convert_element_type x6 -> x7, other arithmetic: 11.4 us -> 23.6 us  [the longest x4 15.1 us: chain(): (own + factor * entered.astype(f32)).astype(bf16)]
    dot_general x6, matrix products: 51.9 us -> 60.2 us  [the longest x1 13.7 us: local(): lax.dot_general(normed, dpx_all, tn, preferred_element_type=f32)]
    all_gather x0 -> x2, waiting for transfers between devices: none -> 7.57 us  [the longest x1 7.55 us: local(): w_z = lax.all_gather(w_z, BOTH, axis=0, tiled=True)]
    ppermute x8 -> x6, starting transfers between devices: 14.9 us -> 11.7 us  [chain(): came = lax.ppermute(sent, 'ctx', [(source, target)])]
  transfers between devices with their start and end apart: 9 -> 10, of which waited for: 3 -> 2; matrix products, arithmetic and copies ran while one was open for 8% -> 28% of each run, Pallas kernels for 27% -> 56%
where the time goes in v2:
time: 537 us; the launch traced here: 528 us
  Pallas kernels  329 us (61%)
  matrix products  90.7 us (17%)
  other arithmetic  46.1 us (9%)
  local copies, waits for them, and re-layouts  23.2 us (4%)
  between operations  14.7 us (3%)
  starting transfers between devices  13.4 us (2%)
  waiting for transfers between devices  11.4 us (2%)
    pallas_call x5, Pallas kernels, call(): pl.pallas_call(kernel, grid=(count,), in_specs=in_specs, out_specs=[spec...  121 us
    pallas_call x1, Pallas kernels, reduce_all(): pl.pallas_call(partial(reduce_kernel, n, tuple(lead)), out_shape=made, in...  117 us
    pallas_call x1, Pallas kernels, gather_all(): pl.pallas_call(partial(gather_kernel, tuple(units), n), out_shape=[jax.Sh...  90.8 us
    convert_element_type x4, other arithmetic, chain(): (own + factor * entered.astype(f32)).astype(bf16)  15.1 us
    dot_general x1, matrix products, local(): lax.dot_general(normed, dpx_all, tn, preferred_element_type=f32)  13.7 us
    ppermute x6, starting transfers between devices, chain(): came = lax.ppermute(sent, 'ctx', [(source, target)])  11.7 us
    dot_general x1, matrix products, local(): px = MM(normed, w_x).astype(bf16)  11.5 us
  transfers between devices with their start and end apart: 10, of which 2 were waited for; matrix products, arithmetic and copies ran while one was open for 28% of the time, Pallas kernels for 56%

profile of v2, /device:TPU:0, one launch (start us, length us, event | category | flops | bytes accessed | tf_op | source)
XLA Modules:
  0.0 528.2 jit_solution(4934144903352096450)
XLA Ops:
  15.9 90.8 %shard_map.203 = (bf16[4,2,2,2,48,3376]{5,4,3,2,1,0:T(8,128)(2,1)}, bf16[4,2,2,2,16,128]{5,4,3,2,1,0:T(8,128)(2,1)}, bf16[16,1536]{1,0:T(8,128)(2,1)}) custom-call(bf16[48,3376]{1,0:T(8,128)(2,1)} %slice.111.refs_0_, bf16[16,128]{1,0:T(8,128)(2,1)} %fusion.20.refs_1_, bf16[16,1536]{1,0:T(8,128)(2,1)} %maximum_bitcast_fusion.refs_2_), custom_call_target="tpu_custom_call" | custom-call | tf_op jit(solution)/shard_map/pallas_call | solution.py:548
  115.4 11.5 %convolution_convert_fusion.3.px_ref.tail_ref = bf16[528,3376]{1,0:T(8,128)(2,1)} fusion(bf16[528,1536]{1,0:T(8,128)(2,1)S(1)} %multiply_convert_fusion, bf16[1536,3376]{1,0:T(8,128)(2,1)} %bitcast.103), kind=kOutput, calls=%fused_computation.3 | convolution fusion | flops 5477708800 | bytes 15558144 | tf_op jit(solution)/shard_map/dot_general | solution.py:776
  126.9 21.0 %shard_map.204 = (f32[2,256,3328]{2,1,0:T(8,128)}, f32[2,256,256]{2,1,0:T(8,128)}, f32[2,48,256]{2,1,0:T(8,128)}, f32[2,3072,128]{2,1,0:T(8,128)}) custom-call(bf16[528,3376]{1,0:T(8,128)(2,1)} %convolution_convert_fusion.3.px_ref.tail_ref, bf16[528,3376]{1,0:T(8,128)(2,1)} %convolution_convert_fusion.3.px_ref.tail_ref, f32[8,3328]{1,0:T(8,128)} %pad.55.w_ref, ...), custom_call_target="tpu_custom_call" | custom-call | tf_op jit(solution)/shard_map/pallas_call | solution.py:369
  147.9 3.3 convert_element_type.123
  154.4 10.0 %fusion.30.dgn_ref = f32[512,3072]{1,0:T(8,128)} fusion(bf16[512,1536]{1,0:T(8,128)(2,1)} %bitcast.87, bf16[3072,1536]{1,0:T(8,128)(2,1)} %all-gather.3.cloned.1.call-done), kind=kOutput, calls=%fused_computation.100 | convolution fusion | flops 4831838208 | bytes 17301504 | tf_op jit(solution)/shard_map/dot_general | solution.py:796
  169.9 15.2 %shard_map.205.y_ref = f32[2,256,3072]{2,1,0:T(8,128)} custom-call(f32[2,256,3328]{2,1,0:T(8,128)} %get-tuple-element.57.act_ref, f32[2,256,256]{2,1,0:T(8,128)} %get-tuple-element.58.tok_ref, f32[2,48,256]{2,1,0:T(8,128)} %get-tuple-element.55.cst_ref, f32[2,256,128]{2,1,0:T(8,128)} %pad.57.cols_ref, f32[2,8,256]{2,1,0:T(8,128)} %pad.61.rows_ref), custom_call_target="tpu_custom_call" | custom-call | tf_op jit(solution)/shard_map/pallas_call | solution.py:369
  185.1 3.6 add_convert_fusion.3
  192.3 7.6 %all-gather.5.cloned.1.call-done = bf16[1536,3072]{1,0:T(8,128)(2,1)} async-done(((bf16[48,3072]{1,0:T(8,128)(2,1)}), bf16[1536,3072]{1,0:T(8,128)(2,1)}) %all-gather.5.cloned.1.call-update) | async-done | bytes 9437200 | tf_op jit(solution)/shard_map/all_gather | solution.py:730
  199.8 9.4 %convolution_convert_fusion.4.z_ref = bf16[512,3072]{1,0:T(8,128)(2,1)} fusion(bf16[1536,3072]{1,0:T(8,128)(2,1)} %all-gather.5.cloned.1.call-done, bf16[528,1536]{1,0:T(8,128)(2,1)} %copy-done.6), kind=kOutput, calls=%fused_computation.6 | convolution fusion | flops 4833411072 | bytes 14155776 | tf_op jit(solution)/shard_map/dot_general | solution.py:810
  209.2 3.8 convert_multiply_fusion
  213.0 31.0 %shard_map.206 = (bf16[512,3072]{1,0:T(8,128)(2,1)}, bf16[512,3072]{1,0:T(8,128)(2,1)}, bf16[2,256,3072]{2,1,0:T(8,128)(2,1)}, f32[2,3072,128]{2,1,0:T(8,128)}, ...) custom-call(bf16[512,3072]{1,0:T(8,128)(2,1)} %convolution_convert_fusion.4.z_ref, ...), custom_call_target="tpu_custom_call" | custom-call | tf_op jit(solution)/shard_map/pallas_call | solution.py:369
  244.1 3.4 convert_element_type.129
  249.3 9.9 %fusion.7 = bf16[512,1536]{1,0:T(8,128)(2,1)} fusion(bf16[512,3072]{1,0:T(8,128)(2,1)S(1)} %copy-done.22, bf16[3072,1536]{1,0:T(8,128)(2,1)} %all-gather.3.cloned.1.call-done, f32[528,1536]{1,0:T(8,128)S(1)} %maximum_convert_fusion), kind=kOutput, calls=%fused_computation.26 | convolution fusion | flops 4833411072 | bytes 17301504 | tf_op jit(solution)/shard_map/dot_general | solution.py:832
  259.2 7.4 %convolution_convert_fusion.2 = bf16[3072,1536]{1,0:T(8,128)(2,1)} fusion(bf16[512,3072]{1,0:T(8,128)(2,1)S(1)} %copy-done.22, bf16[512,1536]{1,0:T(8,128)(2,1)S(1)} %bitcast.88), kind=kOutput, calls=%fused_computation.2 | convolution fusion | flops 4836556800 | bytes 14155776 | tf_op jit(solution)/shard_map/dot_general | solution.py:833
  266.6 3.7 add_convert_fusion.2
  272.2 17.0 %shard_map.207 = (f32[2,256,3072]{2,1,0:T(8,128)}, f32[2,256,256]{2,1,0:T(8,128)}) custom-call(f32[2,256,3328]{2,1,0:T(8,128)} %get-tuple-element.57.act_ref, f32[2,256,256]{2,1,0:T(8,128)} %get-tuple-element.58.tok_ref, f32[2,48,256]{2,1,0:T(8,128)} %get-tuple-element.55.cst_ref, f32[2,256,128]{2,1,0:T(8,128)} %pad.57.cols_ref, f32[2,8,256]{2,1,0:T(8,128)} %pad.61.rows_ref, ...), custom_call_target="tpu_custom_call" | custom-call | tf_op jit(solution)/shard_map/pallas_call | solution.py:369
  289.2 4.8 add_convert_fusion.1
  297.4 9.8 %convolution_convert_fusion.1 = bf16[1536,3072]{1,0:T(8,128)(2,1)} fusion(bf16[512,3072]{1,0:T(8,128)(2,1)} %get-tuple-element.76, bf16[528,1536]{1,0:T(8,128)(2,1)} %copy-done.6), kind=kOutput, calls=%fused_computation.1 | convolution fusion | flops 4836556800 | bytes 14155776 | tf_op jit(solution)/shard_map/dot_general | solution.py:847
  307.2 3.1 collective-permute-done.5
  313.3 37.0 %shard_map.208 = (bf16[512,3456]{1,0:T(8,128)(2,1)}, f32[2,8,3456]{2,1,0:T(8,128)}, f32[2,8,3328]{2,1,0:T(8,128)}, f32[2,8,128]{2,1,0:T(8,128)}) custom-call(bf16[528,3376]{1,0:T(8,128)(2,1)} %convolution_convert_fusion.3.px_ref.tail_ref, bf16[528,3376]{1,0:T(8,128)(2,1)} %convolution_convert_fusion.3.px_ref.tail_ref, f32[8,3328]{1,0:T(8,128)} %pad.55.w_ref, ...), custom_call_target="tpu_custom_call" | custom-call | tf_op jit(solution)/shard_map/pallas_call | solution.py:369
  351.3 10.0 %fusion.1 = f32[528,1536]{1,0:T(8,128)S(1)} fusion(bf16[1536,3376]{1,0:T(8,128)(2,1)} %bitcast.104, bf16[16,3456]{1,0:T(8,128)(2,1)S(1)} %convert_bitcast_fusion, bf16[512,3456]{1,0:T(8,128)(2,1)} %get-tuple-element.78), kind=kOutput, calls=%fused_computation.8 | convolution fusion | flops 5483056128 | bytes 17264640 | tf_op jit(solution)/shard_map/dot_general | solution.py:872
  365.7 13.7 %convolution_convert_fusion = bf16[1536,3456]{1,0:T(8,128)(2,1)} fusion(bf16[528,1536]{1,0:T(8,128)(2,1)} %copy-done.6, bf16[16,3456]{1,0:T(8,128)(2,1)S(1)} %convert_bitcast_fusion, bf16[512,3456]{1,0:T(8,128)(2,1)} %get-tuple-element.78), kind=kOutput, calls=%fused_computation | convolution fusion | flops 5618294784 | bytes 15888384 | tf_op jit(solution)/shard_map/dot_general | solution.py:876
  379.4 8.9 %multiply_reduce_fusion.2 = (f32[1536]{0:T(1024)S(1)}, f32[512,1536]{1,0:T(8,128)}) fusion(f32[528,1536]{1,0:T(8,128)S(1)} %maximum_convert_fusion, f32[512]{0:T(512)S(1)} %get-tuple-element.108, bf16[512,3072]{1,0:T(8,128)(2,1)S(1)} %copy-done.21, bf16[1536,3072]{1,0:T(8,128)(2,1)} %all-gather.5.cloned.1.call-done, f32[528,1536]{1,0:T(8,128)S(1)} %copy-done.16), kind=kOutput, calls=%fused_computation.20 | convolution fusion | flops 4834982400 | bytes 22028288 | tf_op jit(solution)/shard_map/dot_general | solution.py:873
  391.0 116.7 %shard_map.209 = (f32[48,3072]{1,0:T(8,128)}, f32[48,3456]{1,0:T(8,128)}, f32[8,128]{1,0:T(8,128)}) custom-call(bf16[4,2,2,2,48,3072]{5,4,3,2,1,0:T(8,128)(2,1)} %bitcast.86, bf16[4,2,2,2,48,3456]{5,4,3,2,1,0:T(8,128)(2,1)} %bitcast.85, f32[4,2,2,2,8,128]{5,4,3,2,1,0:T(8,128)} %bitcast.91), custom_call_target="tpu_custom_call" | custom-call | tf_op jit(solution)/shard_map/pallas_call | solution.py:697
  (162 shorter events, 60.8 us)
Async XLA Ops:
  7.2 105.6 %copy-start.1 = (bf16[2,256,1536]{2,1,0:T(8,128)(2,1)S(1)}, bf16[2,256,1536]{2,1,0:T(8,128)(2,1)}, u32[]{:S(2)}) copy-start(bf16[2,256,1536]{2,1,0:T(8,128)(2,1)} %param.12) | copy-start | bytes 4718596
  7.2 103.9 %copy-start.13 = (s32[2,256]{1,0:T(2,128)S(1)}, s32[2,256]{1,0:T(2,128)}, u32[]{:S(2)}) copy-start(s32[2,256]{1,0:T(2,128)} %param.22) | copy-start | bytes 6148
  7.2 106.0 %copy-start.19 = (f32[48]{0:T(128)S(1)}, f32[48]{0:T(128)}, u32[]{:S(2)}) copy-start(f32[48]{0:T(128)} %param.18) | copy-start | bytes 580
  7.2 106.0 %copy-start.20 = (f32[48]{0:T(128)S(1)}, f32[48]{0:T(128)}, u32[]{:S(2)}) copy-start(f32[48]{0:T(128)} %param.17) | copy-start | bytes 580
  7.2 147.2 %all-gather.3.cloned.1.call-start = ((), (), s32[]{:S(2)}) async-start(), calls=%async_computation.1 | async-start | bytes 9732096 | tf_op jit(solution)/shard_map/all_gather | solution.py:729
  8.0 191.9 %all-gather.5.cloned.1.call-start = ((), (), s32[]{:S(2)}) async-start(), calls=%async_computation.2 | async-start | bytes 9732096 | tf_op jit(solution)/shard_map/all_gather | solution.py:730
  9.7 509.7 %reduce-scatter.2.cloned.1.call-start = ((), (), s32[]{:S(2)}) async-start(), calls=%async_computation.3 | async-start | bytes 9732096 | tf_op jit(solution)/shard_map/reduce_scatter | solution.py:900
  147.9 6.1 %copy-start.10 = (f32[2,48,256]{2,1,0:T(8,128)S(1)}, f32[2,48,256]{2,1,0:T(8,128)}, u32[]{:S(2)}) copy-start(f32[2,48,256]{2,1,0:T(8,128)} %get-tuple-element.55.cst_ref) | copy-start | bytes 294916
  151.2 13.3 %collective-permute-start = (bf16[2,3072,128]{2,1,0:T(8,128)(2,1)}, bf16[2,3072,128]{2,1,0:T(8,128)(2,1)}, u32[]{:S(2)}, u32[]{:S(2)}) collective-permute-start(bf16[2,3072,128]{2,1,0:T(8,128)(2,1)} %convert_element_type.123), channel_id=1, source_target_pairs={{0,1},{4,5},{8,9},{12,13},{16,17},{20,21},{24,25},{28,29}} | collective-permute-start | bytes 4718600 | tf_op jit(solution)/shard_map/ppermute | solution.py:385
  154.4 10.0 %copy-start = (f32[2,3072,128]{2,1,0:T(8,128)S(1)}, f32[2,3072,128]{2,1,0:T(8,128)}, u32[]{:S(2)}) copy-start(f32[2,3072,128]{2,1,0:T(8,128)} %get-tuple-element.54) | copy-start | bytes 9437188
  167.4 17.7 %collective-permute-start.1 = (bf16[2,3072,128]{2,1,0:T(8,128)(2,1)}, bf16[2,3072,128]{2,1,0:T(8,128)(2,1)}, u32[]{:S(2)}, u32[]{:S(2)}) collective-permute-start(bf16[2,3072,128]{2,1,0:T(8,128)(2,1)} %add_convert_fusion.4), channel_id=1, source_target_pairs={{1,2},{5,6},{9,10},{13,14},{17,18},{21,22},{25,26},{29,30}} | collective-permute-start | bytes 4718600 | tf_op jit(solution)/shard_map/ppermute | solution.py:385
  185.1 5.8 %copy-start.2 = (bf16[2,256,1536]{2,1,0:T(8,128)(2,1)S(1)}, bf16[2,256,1536]{2,1,0:T(8,128)(2,1)}, u32[]{:S(2)}) copy-start(bf16[2,256,1536]{2,1,0:T(8,128)(2,1)} %param.12) | copy-start | bytes 4718596
  188.7 20.5 %collective-permute-start.2 = (bf16[2,3072,128]{2,1,0:T(8,128)(2,1)}, bf16[2,3072,128]{2,1,0:T(8,128)(2,1)}, u32[]{:S(2)}, u32[]{:S(2)}) collective-permute-start(bf16[2,3072,128]{2,1,0:T(8,128)(2,1)} %get-tuple-element.97), channel_id=1, source_target_pairs={{2,3},{6,7},{10,11},{14,15},{18,19},{22,23},{26,27},{30,31}} | collective-permute-start | bytes 4718600 | tf_op jit(solution)/shard_map/ppermute | solution.py:385
  199.8 9.4 %copy-start.5 = (bf16[2,3072,128]{2,1,0:T(8,128)(2,1)S(1)}, bf16[2,3072,128]{2,1,0:T(8,128)(2,1)}, u32[]{:S(2)}) copy-start(bf16[2,3072,128]{2,1,0:T(8,128)(2,1)} %get-tuple-element.98) | copy-start | bytes 4718596
  247.4 19.2 %collective-permute-start.3 = (bf16[2,3072,128]{2,1,0:T(8,128)(2,1)}, bf16[2,3072,128]{2,1,0:T(8,128)(2,1)}, u32[]{:S(2)}, u32[]{:S(2)}) collective-permute-start(bf16[2,3072,128]{2,1,0:T(8,128)(2,1)} %convert_element_type.129), channel_id=1, source_target_pairs={{3,2},{7,6},{11,10},{15,14},{19,18},{23,22},{27,26},{31,30}} | collective-permute-start | bytes 4718600 | tf_op jit(solution)/shard_map/ppermute | solution.py:385
  249.3 9.9 %copy-start.7 = (bf16[2,256,1536]{2,1,0:T(8,128)(2,1)S(1)}, bf16[2,256,1536]{2,1,0:T(8,128)(2,1)}, u32[]{:S(2)}) copy-start(bf16[2,256,1536]{2,1,0:T(8,128)(2,1)} %param.23) | copy-start | bytes 4718596
  270.3 18.8 %collective-permute-start.4 = (bf16[2,3072,128]{2,1,0:T(8,128)(2,1)}, bf16[2,3072,128]{2,1,0:T(8,128)(2,1)}, u32[]{:S(2)}, u32[]{:S(2)}) collective-permute-start(bf16[2,3072,128]{2,1,0:T(8,128)(2,1)} %add_convert_fusion.2), channel_id=1, source_target_pairs={{2,1},{6,5},{10,9},{14,13},{18,17},{22,21},{26,25},{30,29}} | collective-permute-start | bytes 4718600 | tf_op jit(solution)/shard_map/ppermute | solution.py:385
  289.1 6.3 %copy-start.12 = (f32[2,8,3072]{2,1,0:T(8,128)S(1)}, f32[2,8,3072]{2,1,0:T(8,128)}, u32[]{:S(2)}) copy-start(f32[2,8,3072]{2,1,0:T(8,128)} %get-tuple-element.84) | copy-start | bytes 589828
  293.9 16.4 %collective-permute-start.5 = (bf16[2,3072,128]{2,1,0:T(8,128)(2,1)}, bf16[2,3072,128]{2,1,0:T(8,128)(2,1)}, u32[]{:S(2)}, u32[]{:S(2)}) collective-permute-start(bf16[2,3072,128]{2,1,0:T(8,128)(2,1)} %get-tuple-element.95), channel_id=1, source_target_pairs={{1,0},{5,4},{9,8},{13,12},{17,16},{21,20},{25,24},{29,28}} | collective-permute-start | bytes 4718600 | tf_op jit(solution)/shard_map/ppermute | solution.py:385
  297.4 12.9 %copy-start.4 = (bf16[2,3072,128]{2,1,0:T(8,128)(2,1)S(1)}, bf16[2,3072,128]{2,1,0:T(8,128)(2,1)}, u32[]{:S(2)}) copy-start(bf16[2,3072,128]{2,1,0:T(8,128)(2,1)} %get-tuple-element.96) | copy-start | bytes 4718596
  351.3 13.3 %copy-start.14 = (f32[2,8,128]{2,1,0:T(8,128)S(1)}, f32[2,8,128]{2,1,0:T(8,128)}, u32[]{:S(2)}) copy-start(f32[2,8,128]{2,1,0:T(8,128)} %get-tuple-element.86) | copy-start | bytes 24580
  362.0 26.8 %collective-permute-start.6 = (bf16[2,3,1536]{2,1,0:T(4,128)(2,1)}, bf16[2,3,1536]{2,1,0:T(4,128)(2,1)}, u32[]{:S(2)}, u32[]{:S(2)}) collective-permute-start(bf16[2,3,1536]{2,1,0:T(4,128)(2,1)} %slice.157), channel_id=1, source_target_pairs={{1,0},{2,1},{3,2},{5,4},{6,5},{7,6},{9,8},{10,9},{11,10},{13,12},{... | collective-permute-start | bytes 55304 | tf_op jit(solution)/shard_map/ppermute | solution.py:875
  365.7 13.7 %copy-start.16 = (f32[528,1536]{1,0:T(8,128)S(1)}, f32[528,1536]{1,0:T(8,128)}, u32[]{:S(2)}) copy-start(f32[528,1536]{1,0:T(8,128)} %copy-done.15) | copy-start | bytes 9732100
  365.7 13.7 %copy-start.21 = (bf16[512,3072]{1,0:T(8,128)(2,1)S(1)}, bf16[512,3072]{1,0:T(8,128)(2,1)}, u32[]{:S(2)}) copy-start(bf16[512,3072]{1,0:T(8,128)(2,1)} %get-tuple-element.76) | copy-start | bytes 9437188
  (9 other events, 26.8 us)
Sparse Core Ops, SparseCore 0:
  11.0 102.9 all-gather.2
  117.4 82.3 all-gather.4
  272.3 146.6 reduce-scatter.1

commit v3 on v2

--- a/solution.py
+++ b/solution.py
@@ -19,6 +19,7 @@
 LANES = 128
 EPSILON = 1e-05
 VMEM = 60 * 1024 * 1024
+FINISH_VMEM = 62 * 1024 * 1024 - 512 * 1024
 BOTH = ("seq", "ctx")
 FAR = -1e30
 f32 = jnp.float32
@@ -567,65 +568,76 @@
 AHEAD = 4
 
 
-def cuts_of(shape):
-    rows, columns = shape[-2:]
-    return [(r, k, min(CUT, columns - k)) for k in range(0, columns, CUT) for r in range(0, rows, CUT_ROWS)]
-
-
-def reduce_kernel(n, lead, *refs):
-    ins, outs, scratch = refs[: n + 1], refs[n + 1 : 2 * n + 2], refs[2 * n + 2 :]
-    (own, core, first, second, last, own_s, core_s, first_s, second_s, last_s, sem, semz) = scratch
+def finish_kernel(lead, dwz_ref, small_ref, dpx_ref, normed_ref, dz_ref, wx_ref, wz_ref, x_ref, tail_ref, gain_ref, g_ref,
+                  oz_ref, ox_ref, os_ref, grad_ref,
+                  own_z, own, core, first, second, last, own_s, core_s, first_s, second_s, last_s,
+                  wbuf, total, back, spare, sem, semz, wsem, tail_sem):
     z, y, x, c = place()
-    greet(z, y, x, c)
-    pieces = [(a, cut) for a in range(n) for cut in cuts_of(ins[a].shape)]
-    total = len(pieces) + 1
+    ctx = x * 2 + c
+    after, before = lax.rem(ctx + 1, 4), lax.rem(ctx + 3, 4)
+    barrier = pltpu.get_barrier_semaphore()
+    for other in (after, before):
+        pl.semaphore_signal(
+            barrier, inc=1, device_id={"seq": z * 2 + y, "ctx": other},
+            device_id_type=pl.DeviceIdType.MESH,
+        )
+    greet(z, y, x, c, 2)
+    count = g_ref.shape[0]
+    nz = dwz_ref.shape[-1] // CUT
+    widths = [CUT] * nz + [
+        min(CUT, dpx_ref.shape[1] - k) for k in range(0, dpx_ref.shape[1], CUT)
+    ]
+    pieces = len(widths)
     sent = []
 
-    def begin(i):
-        own_i, core_i = view(i, 0), view(i, 1)
-        if i == total - 1:
-            src_out, src_own = ins[n].at[:, :, :, 1 - c], ins[n].at[:, :, :, c]
-        else:
-            a, (r, k, w) = pieces[i]
-            rows, cols = pl.ds(r, CUT_ROWS), pl.ds(k, w)
-            src_out = ins[a].at[:, :, :, 1 - c, rows, cols]
-            src_own = ins[a].at[:, :, :, c, rows, cols]
-        go = remote(src_out, core_i, sem.at[0, i], sem.at[1, i], device(z, y, x, 1 - c))
-        go.start()
-        sent.append(go)
-        pltpu.make_async_copy(src_own, own_i, sem.at[2, i]).start()
-
     def view(i, k):
-        if i == total - 1:
+        if i == pieces:
             return (own_s, core_s, first_s, second_s, last_s)[k]
         v = (own, core, first, second, last)[k]
-        w = pieces[i][1][2]
-        if w == CUT:
-            return v.at[i]
-        free = len(v.shape) - 2
-        return v.at[(i,) + (slice(None),) * free + (pl.ds(0, w),)]
+        j = i - nz if k == 0 else i
+        if widths[i] == CUT:
+            return v.at[j]
+        return v.at[(j,) + (slice(None),) * (len(v.shape) - 2) + (pl.ds(0, widths[i]),)]
+
+    def fetch(i):
+        if i == pieces:
+            return pltpu.make_async_copy(small_ref, own_s, sem.at[2, i])
+        return pltpu.make_async_copy(
+            dwz_ref.at[:, :, :, c, :, pl.ds(i * CUT, CUT)], own_z.at[i], sem.at[2, i]
+        )
+
+    def begin(i):
+        if i < nz:
+            src = dwz_ref.at[:, :, :, 1 - c, :, pl.ds(i * CUT, CUT)]
+        else:
+            src = view(i, 0).at[:, :, :, 1 - c]
+        copy = remote(src, view(i, 1), sem.at[0, i], sem.at[1, i], device(z, y, x, 1 - c))
+        copy.start()
+        sent.append(copy)
 
     def x_goes_first(i):
         return i % 2 == 0
 
     def after_core(i):
-        own_i, core_i = view(i, 0), view(i, 1)
+        core_i = view(i, 1)
+        if i < nz:
+            fetch(i).wait()
         remote(core_i, core_i, sem.at[0, i], sem.at[1, i], device(z, y, x, 1 - c)).wait_recv()
-        pltpu.make_async_copy(own_i, own_i, sem.at[2, i]).wait()
 
         @pl.loop(0, NZ)
         def _(zz):
             for yy in range(2):
                 for xx in range(2):
-                    core_i[zz, yy, xx] = core_i[zz, yy, xx] + own_i[zz, yy, xx]
+                    mine = own_z[i, zz, yy, xx] if i < nz else view(i, 0)[zz, yy, xx, c]
+                    core_i[zz, yy, xx] = core_i[zz, yy, xx] + mine
 
         if x_goes_first(i):
             src, to = core_i.at[:, :, 1 - x], device(z, y, 1 - x, c)
         else:
             src, to = core_i.at[:, 1 - y], device(z, 1 - y, x, c)
-        go = remote(src, view(i, 2), sem.at[3, i], sem.at[4, i], to)
-        go.start()
-        sent.append(go)
+        copy = remote(src, view(i, 2), sem.at[3, i], sem.at[4, i], to)
+        copy.start()
+        sent.append(copy)
 
     def after_first(i):
         core_i, first_i = view(i, 1), view(i, 2)
@@ -641,9 +653,9 @@
             src, to = first_i.at[:, 1 - y], device(z, 1 - y, x, c)
         else:
             src, to = first_i.at[:, 1 - x], device(z, y, 1 - x, c)
-        go = remote(src, view(i, 3), sem.at[5, i], sem.at[6, i], to)
-        go.start()
-        sent.append(go)
+        copy = remote(src, view(i, 3), sem.at[5, i], sem.at[6, i], to)
+        copy.start()
+        sent.append(copy)
 
     def after_second(i):
         first_i, second_i, last_i = view(i, 2), view(i, 3), view(i, 4)
@@ -655,55 +667,174 @@
 
         for d in range(1, NZ):
             zz = lax.rem(z + d, NZ)
-            go = remote(second_i.at[zz], last_i.at[z], semz.at[0, d, i], semz.at[1, d, i], device(zz, y, x, c))
-            go.start()
-            sent.append(go)
+            copy = remote(
+                second_i.at[zz], last_i.at[z], semz.at[0, d, i], semz.at[1, d, i],
+                device(zz, y, x, c),
+            )
+            copy.start()
+            sent.append(copy)
         last_i[z] = second_i[z]
 
     def after_last(i):
         last_i = view(i, 4)
         for d in range(1, NZ):
             zz = lax.rem(z + NZ - d, NZ)
-            remote(last_i.at[zz], last_i.at[zz], semz.at[0, d, i], semz.at[1, d, i], device(z, y, x, 1 - c)).wait_recv()
+            remote(
+                last_i.at[zz], last_i.at[zz], semz.at[0, d, i], semz.at[1, d, i],
+                device(z, y, x, 1 - c),
+            ).wait_recv()
         value = last_i[0].astype(f32)
         for zz in range(1, NZ):
             value = value + last_i[zz].astype(f32)
-        if i == total - 1:
-            outs[n][...] = value
+        if i == pieces:
+            os_ref[...] = value
+        elif i < nz:
+            oz_ref[:, i * CUT : i * CUT + CUT] = value
         else:
-            a, (r, k, w) = pieces[i]
-            outs[a][r : r + CUT_ROWS, k : k + w] = value
-
-    order = [total - 1] + list(range(total - 1))
-    for i in order:
+            k = (i - nz) * CUT
+            ox_ref[:, k : k + widths[i]] = value
+
+    def weight_piece(j):
+        k, w = j * CUT, widths[nz + j]
+        own_i = view(nz + j, 0)
+        depth = normed_ref.shape[1] // NZ
+
+        @pl.loop(0, NZ)
+        def _(zz):
+            value = mm_tn(normed_ref[:, at(zz, depth)], dpx_ref[:, k : k + w])
+            if nz + j == pieces - 1:
+                lane = lax.broadcasted_iota(jnp.int32, (depth, w), 1)
+                column = jnp.concatenate([spare[pl.ds(zz * depth, depth), :]] * (w // LANES), axis=1)
+                value = jnp.where(lane + k < CHANNELS + HEADS, value, column)
+            own_i[zz] = value.astype(bf16).reshape(2, 2, 2, CUT_ROWS, w)
+
+    def weight_and_send(j):
+        weight_piece(j)
+        begin(nz + j)
+
+    chunks = [(wz_ref, dz_ref, k, CUT) for k in range(0, wz_ref.shape[1], CUT)]
+    chunks += [
+        (wx_ref, dpx_ref, k, min(CUT, dpx_ref.shape[1] - k)) for k in range(0, dpx_ref.shape[1], CUT)
+    ]
+
+    def stream(q):
+        w_ref, _left, k, w = chunks[q]
+        return pltpu.make_async_copy(
+            w_ref.at[:, pl.ds(k, w)], wbuf.at[q % 2, :, pl.ds(0, w)], wsem.at[q % 2]
+        )
+
+    def input_chunk(q):
+        _w, left, k, w = chunks[q]
+        stream(q).wait()
+        weights = wbuf[q % 2, :, :w]
+        rows = left.shape[0]
+        value = mm_nt(left[:, k : k + w], weights)
+        if q == 0:
+            total[...] = jnp.zeros_like(total)
+        total[:rows] += value
+        if q + 2 < len(chunks):
+            stream(q + 2).start()
+
+    def tail_copy():
+        return remote(
+            total.at[pl.ds(count, 16)], back, tail_sem.at[0], tail_sem.at[1],
+            {"seq": z * 2 + y, "ctx": before},
+        )
+
+    def scaled_rows(rows_ref, lo, hi):
+        v = rows_ref[lo:hi].astype(f32)
+        r = lax.rsqrt(jnp.mean(v * v, axis=1, keepdims=True) + EPSILON)
+        return v, r
+
+    def norm_weights():
+        tail_copy().start()
+        sums = jnp.zeros((normed_ref.shape[1], LANES), f32)
+        ones = jnp.ones((LANES, LANES), bf16)
+        for lo in range(0, count, LANES):
+            v, r = scaled_rows(x_ref, lo, lo + LANES)
+            product = v * r * total[lo : lo + LANES]
+            high = product.astype(bf16)
+            rest = (product - high.astype(f32)).astype(bf16)
+            sums = sums + mm_tn(high, ones) + mm_tn(rest, ones)
+        v, r = scaled_rows(tail_ref, 0, 16)
+        product = v * r * total[count : count + 16]
+        high = product.astype(bf16)
+        rest = (product - high.astype(f32)).astype(bf16)
+        sums = sums + mm_tn(high, ones[:16]) + mm_tn(rest, ones[:16])
+        spare[...] = sums
+
+    def norm_rows():
+        tail_copy().wait()
+        seqs = tail_ref.shape[0] // 8
+        length = count // seqs
+        for s in range(seqs):
+            total[(s + 1) * length - 8 : (s + 1) * length] += back[8 * s : 8 * s + 8]
+        for lo in range(0, count, LANES):
+            v, r = scaled_rows(x_ref, lo, lo + LANES)
+            scaled = gain_ref[0:1] * total[lo : lo + LANES]
+            mean = jnp.mean(v * scaled, axis=1, keepdims=True)
+            value = g_ref[lo : lo + LANES].astype(f32) + r * (scaled - v * (r * r) * mean)
+            grad_ref[lo : lo + LANES] = value.astype(bf16)
+
+    for i in range(nz):
+        fetch(i).start()
+    fetch(pieces).start()
+    stream(0).start()
+    stream(1).start()
+    order = [pieces, *range(pieces)]
+    for i in range(nz):
         begin(i)
-    stages = (after_core, after_first, after_second, after_last)
-    for t in range(total + lead[-1]):
-        for stage, skew in reversed(list(zip(stages, lead))):
-            if 0 <= t - skew < total:
+    fetch(pieces).wait()
+    begin(pieces)
+    work = [[partial(weight_and_send, j)] for j in range(pieces - nz - 1)]
+    step = -(-len(chunks) // 5)
+    work += [
+        [partial(input_chunk, q) for q in range(k, min(k + step, len(chunks)))]
+        for k in range(0, len(chunks), step)
+    ]
+    work += [[norm_weights, partial(weight_and_send, pieces - nz - 1)], [norm_rows]]
+    stages = list(zip((after_core, after_first, after_second, after_last), lead))
+    for t in range(len(order) + lead[-1]):
+        for job in work[t] if t < len(work) else []:
+            job()
+        for stage, skew in reversed(stages):
+            if 0 <= t - skew < len(order):
                 stage(order[t - skew])
-    for go in sent:
-        go.wait_send()
-
-
-def reduce_all(arrays, small, lead=(0, 4, 6, 8)):
-    n = len(arrays)
-    arrays = [v.reshape((NZ, 2, 2, 2, -1, v.shape[-1])) for v in arrays]
+    for copy in sent:
+        copy.wait_send()
+
+
+def finish(dw_z, small, dpx, normed, dz, w_x, w_z, x, tail, gain, g, lead=(0, 5, 7, 9)):
+    dw_z = dw_z.reshape((NZ, 2, 2, 2, -1, dw_z.shape[-1]))
     small = small.reshape((NZ, 2, 2, 2, -1, small.shape[-1]))
-    p = sum(len(cuts_of(v.shape)) for v in arrays)
+    nz = dw_z.shape[-1] // CUT
+    p = nz + pl.cdiv(dpx.shape[1], CUT)
     ss = small.shape[-2:]
-    made = [jax.ShapeDtypeStruct(v.shape[-2:], f32) for v in arrays + [small]]
-    dims = [(NZ, 2, 2), (NZ, 2, 2), (NZ, 2), (NZ,), (NZ,)]
+    dims = [(NZ, 2, 2, 2), (NZ, 2, 2), (NZ, 2), (NZ,), (NZ,)]
+    far, near = pl.BlockSpec(memory_space=pl.ANY), pl.BlockSpec(memory_space=pltpu.VMEM)
     return pl.pallas_call(
-        partial(reduce_kernel, n, tuple(lead)),
-        out_shape=made,
-        in_specs=[pl.BlockSpec(memory_space=pl.ANY)] * (n + 1),
-        out_specs=[pl.BlockSpec(memory_space=pltpu.VMEM)] * (n + 1),
-        scratch_shapes=[pltpu.VMEM((p,) + d + (CUT_ROWS, CUT), bf16) for d in dims]
+        partial(finish_kernel, tuple(lead)),
+        out_shape=[
+            jax.ShapeDtypeStruct((CUT_ROWS, dw_z.shape[-1]), f32),
+            jax.ShapeDtypeStruct((CUT_ROWS, dpx.shape[1]), f32),
+            jax.ShapeDtypeStruct(ss, f32),
+            jax.ShapeDtypeStruct(g.shape, bf16),
+        ],
+        in_specs=[far, far, near, near, near, far, far, near, near, near, near],
+        out_specs=[near] * 4,
+        scratch_shapes=[pltpu.VMEM((nz,) + dims[1] + (CUT_ROWS, CUT), bf16)]
+        + [pltpu.VMEM((n,) + d + (CUT_ROWS, CUT), bf16) for n, d in zip((p - nz, p, p, p, p), dims)]
         + [pltpu.VMEM(d + ss, f32) for d in dims]
-        + [pltpu.SemaphoreType.DMA((7, p + 1)), pltpu.SemaphoreType.DMA((2, NZ, p + 1))],
-        compiler_params=pltpu.CompilerParams(collective_id=1, has_side_effects=True, vmem_limit_bytes=VMEM),
-    )(*arrays, small)
+        + [
+            pltpu.VMEM((2, w_x.shape[0], CUT), bf16), pltpu.VMEM(normed.shape, f32),
+            pltpu.VMEM(tail.shape, f32), pltpu.VMEM((normed.shape[1], LANES), f32),
+            pltpu.SemaphoreType.DMA((7, p + 1)), pltpu.SemaphoreType.DMA((2, NZ, p + 1)),
+            pltpu.SemaphoreType.DMA((2,)), pltpu.SemaphoreType.DMA((2,)),
+        ],
+        compiler_params=pltpu.CompilerParams(
+            collective_id=1, has_side_effects=True, vmem_limit_bytes=FINISH_VMEM
+        ),
+    )(dw_z, small, dpx, normed, dz, w_x, w_z, x, tail, gain, g)
 
 
 def local(tokens, norm_gain, input_weight, conv_w, conv_b, dt_bias, a_log, d_skip, gate_gain,
@@ -722,7 +853,8 @@
     )
     tail = jnp.concatenate([tail_ids[:, None], tail[:, 1:]], axis=1).reshape(seqs * 8, width)
     torus = lax.axis_size("seq") == 2 * NZ and n_ctx == 4 and norm_gain.shape[0] == CUT_ROWS
-    w_z, w_x = input_weight[:, :INNER], input_weight[:, INNER:]
+    spare = ((0, 0), (0, LANES - HEADS))
+    w_z, w_x = input_weight[:, :INNER], jnp.pad(input_weight[:, INNER:], spare)
     if torus:
         size = packed.shape[0]
         small = jnp.pad(packed, (0, 16 * LANES - size)).reshape(16, LANES)
@@ -742,7 +874,7 @@
         w_in, w_out = (
             lax.all_gather(w, BOTH, axis=0, tiled=True) for w in (input_weight, output_weight)
         )
-        w_z, w_x = w_in[:, :INNER], w_in[:, INNER:]
+        w_z, w_x = w_in[:, :INNER], jnp.pad(w_in[:, INNER:], spare)
     norm_full, gate_full, conv_w_full, conv_b_full = jnp.split(packed.astype(f32), cuts, axis=1)
     norm_full = norm_full.reshape(1, -1)
     gate_full = gate_full.reshape(1, -1)
@@ -755,7 +887,8 @@
     )
     tail = jnp.pad(tail[:, 8 - (CONV - 1) :], ((0, 0), (8 - (CONV - 1), 0), (0, 0)))
     tail = jnp.where(lax.axis_index("ctx") == 0, 0, tail)
-    x_all = jnp.concatenate([tokens.reshape(count, width), tail.reshape(seqs * 8, width)])
+    tail = tail.reshape(seqs * 8, width)
+    x_all = jnp.concatenate([tokens.reshape(count, width), tail])
     x_all = x_all.astype(f32)
     r_all = lax.rsqrt(jnp.mean(x_all * x_all, axis=-1, keepdims=True) + EPSILON)
     normed = (x_all * r_all * norm_full).astype(bf16)
@@ -774,7 +907,7 @@
     conv_b8 = jnp.pad(conv_b_full, ((0, 7), (0, 0)))
 
     px = MM(normed, w_x).astype(bf16)
-    px_width, dpx_width = CHANNELS + HEADS, CHANNELS + LANES
+    px_width, used = CHANNELS + LANES, CHANNELS + HEADS
     tail_spec = pl.BlockSpec((16, px_width), lambda s: (count // 16, 0))
     act, tok, cst, fresh = call(
         before_kernel, seqs,
@@ -856,8 +989,8 @@
          per_seq(length, 2 * LANES), whole((8, INNER)), per_seq(length, INNER),
          per_seq(length, INNER), per_seq(length, 2 * STATE), per_seq(length, STATE),
          per_seq(length, LANES), per_seq(INNER, STATE), per_seq(INNER, STATE)],
-        [(per_rows(length, dpx_width), ((count, dpx_width), bf16)),
-         (per_seq(8, dpx_width), ((seqs, 8, dpx_width), f32)),
+        [(per_rows(length, px_width), ((count, px_width), bf16)),
+         (per_seq(8, px_width), ((seqs, 8, px_width), f32)),
          (per_seq(8, CHANNELS), ((seqs, 8, CHANNELS), f32)),
          (per_seq(8, LANES), ((seqs, 8, LANES), f32))],
         [pltpu.VMEM((length + 8, LANES), f32), pltpu.VMEM((CONV - 1, length + 16, LANES), f32),
@@ -867,54 +1000,56 @@
         px, px, conv_w8, conv_b8, cols, heads, act, tok, lanes, dy, dx, dbc, dqueries, ddecay,
         later, stayed,
     )
-    dpx_all = jnp.concatenate([dpx, edge.reshape(seqs * 8, dpx_width).astype(bf16)])
-    nt = (((1,), (1,)), ((), ()))
-    dnormed_x = lax.dot_general(dpx_all[:, :px_width], w_x, nt, preferred_element_type=f32)
-    dnormed = dnormed_x[:count] + lax.dot_general(dz, w_z, nt, preferred_element_type=f32)
-    back = dnormed_x[count:].reshape(seqs, 8, width)[:, 8 - (CONV - 1) :].astype(bf16)
-    back = lax.ppermute(back, "ctx", [(b, a) for a, b in onward])
-    dw_x = lax.dot_general(normed, dpx_all, tn, preferred_element_type=f32).astype(bf16)
-    x, r = x_all[:count], r_all[:count]
-    d_gain = jnp.sum(x * r * dnormed, axis=0) + jnp.sum(
-        x_all[count:] * r_all[count:] * dnormed_x[count:], axis=0
-    )
-    back, d_gain, dw_x = lax.optimization_barrier((back, d_gain, dw_x))
-    back = jnp.pad(back.astype(f32), ((0, 0), (length - (CONV - 1), 0), (0, 0)))
-    scaled = norm_full * (dnormed + back.reshape(count, width))
-    dx_in = r * (scaled - x * (r * r) * jnp.mean(x * scaled, axis=-1, keepdims=True))
-    input_grad = (g2.astype(f32) + dx_in).astype(bf16)
-
+    dpx_all = jnp.concatenate([dpx, edge.reshape(seqs * 8, px_width).astype(bf16)])
     sums = jnp.sum(sums, axis=0)
     dconv = jnp.sum(dconv, axis=0)
     dheads = jnp.sum(dheads, axis=0)
     d_skip_sum = jnp.sum(sums[1].reshape(HEADS, HEADDIM), axis=1)
-    split = [d_gain.reshape(n_all, -1), sums[0].reshape(n_all, -1),
+    split = [sums[0].reshape(n_all, -1),
              dconv[:CONV].reshape(CONV, n_all, -1).transpose(1, 0, 2).reshape(n_all, -1),
              dconv[CONV].reshape(n_all, -1)]
     shared = jnp.concatenate([dheads[0, :HEADS], dheads[1, :HEADS], d_skip_sum])
     split = jnp.concatenate(split, axis=1)
-    share = sum(shares)
+    share = split.shape[1]
     if torus:
         fill = 8 * LANES - share - shared.shape[0]
         split = [split, jnp.broadcast_to(shared, (n_all,) + shared.shape), jnp.zeros((n_all, fill), f32)]
+        dw_z, dw_x, mine, input_grad = finish(
+            dw_z, jnp.concatenate(split, axis=1).reshape(n_all, 8, LANES), dpx_all, normed, dz,
+            w_x, w_z, tokens.reshape(count, width), tail, jnp.pad(norm_full, ((0, 7), (0, 0))), g2,
+        )
         dw_out = lax.psum_scatter(dw_out, BOTH, scatter_dimension=0, tiled=True).astype(f32)
-        dw_z, dw_x, mine = reduce_all(
-            [dw_z, dw_x],
-            jnp.concatenate(split, axis=1).reshape(n_all, 8, LANES),
-        )
-        dw_in = jnp.concatenate([dw_z, dw_x[:, :px_width]], axis=1)
+        dw_in = jnp.concatenate([dw_z, dw_x[:, :used]], axis=1)
+        d_norm = dw_x[:, used]
         mine = mine.reshape(-1)
         mine, shared = mine[:share], mine[share : share + shared.shape[0]]
     else:
-        dw_in = jnp.concatenate([dw_z, dw_x[:, :px_width]], axis=1)
+        nt = (((1,), (1,)), ((), ()))
+        dnormed_x = lax.dot_general(dpx_all, w_x, nt, preferred_element_type=f32)
+        dnormed = dnormed_x[:count] + lax.dot_general(dz, w_z, nt, preferred_element_type=f32)
+        back = dnormed_x[count:].reshape(seqs, 8, width)[:, 8 - (CONV - 1) :].astype(bf16)
+        back = lax.ppermute(back, "ctx", [(b, a) for a, b in onward])
+        dw_x = lax.dot_general(normed, dpx_all, tn, preferred_element_type=f32).astype(bf16)
+        x, r = x_all[:count], r_all[:count]
+        d_gain = jnp.sum(x * r * dnormed, axis=0) + jnp.sum(
+            x_all[count:] * r_all[count:] * dnormed_x[count:], axis=0
+        )
+        back, d_gain, dw_x = lax.optimization_barrier((back, d_gain, dw_x))
+        back = jnp.pad(back.astype(f32), ((0, 0), (length - (CONV - 1), 0), (0, 0)))
+        scaled = norm_full * (dnormed + back.reshape(count, width))
+        dx_in = r * (scaled - x * (r * r) * jnp.mean(x * scaled, axis=-1, keepdims=True))
+        input_grad = (g2.astype(f32) + dx_in).astype(bf16)
+        dw_in = jnp.concatenate([dw_z, dw_x[:, :used]], axis=1)
         dw_out, dw_in = (
             lax.psum_scatter(v.astype(f32), BOTH, scatter_dimension=0, tiled=True)
             for v in (dw_out, dw_in)
         )
-        every = lax.psum(jnp.concatenate([split.reshape(-1), shared]), BOTH)
+        every = lax.psum(jnp.concatenate([split.reshape(-1), shared, d_gain]), BOTH)
         me = lax.axis_index("seq") * n_ctx + lax.axis_index("ctx")
-        mine, shared = lax.dynamic_slice(every, (me * share,), (share,)), every[n_all * share :]
-    d_norm, d_gate, d_conv_w, d_conv_b = jnp.split(mine, cuts)
+        d_norm = lax.dynamic_slice(every[-width:], (me * shares[0],), (shares[0],))
+        mine = lax.dynamic_slice(every, (me * share,), (share,))
+        shared = every[n_all * share : n_all * share + shared.shape[0]]
+    d_gate, d_conv_w, d_conv_b = jnp.split(mine, [v - cuts[0] for v in cuts[1:]])
     d_bias, d_alog, d_skips = jnp.split(shared, 3)
     return (
         output.reshape(tokens.shape), input_grad.reshape(tokens.shape), d_norm, dw_in,

time: 537 us -> 516 us (0.961)
  matrix products: 90.7 us -> 59.5 us
  Pallas kernels: 329 us -> 340 us
    dot_general x3 -> x0, matrix products: 32.7 us -> none  [the longest x1 13.7 us: local(): lax.dot_general(normed, dpx_all, tn, preferred_element_type=f32)]
    pallas_call x1, Pallas kernels: 117 us -> 128 us  [finish(): pl.pallas_call(partial(finish_kernel, tuple(lead)), out_shape=[jax.ShapeD...]
    concatenate x1 -> x2, other arithmetic: 1.12 us -> 6.5 us  [the longest x1 4.12 us: local(): jnp.concatenate([dpx, edge.reshape(seqs * 8, px_width).astype(bf16)])]
  transfers between devices with their start and end apart: 10 -> 9, of which waited for: 2 -> 2; matrix products, arithmetic and copies ran while one was open for 28% -> 23% of each run, Pallas kernels for 56% -> 61%
where the time goes in v3:
time: 516 us; the launch traced here: 507 us
  Pallas kernels  340 us (66%)
  matrix products  59.5 us (12%)
  other arithmetic  44 us (9%)
  local copies, waits for them, and re-layouts  25.2 us (5%)
  between operations  14.6 us (3%)
  waiting for transfers between devices  12.2 us (2%)
  starting transfers between devices  11.7 us (2%)
    pallas_call x1, Pallas kernels, finish(): pl.pallas_call(partial(finish_kernel, tuple(lead)), out_shape=[jax.ShapeD...  128 us
    pallas_call x5, Pallas kernels, call(): pl.pallas_call(kernel, grid=(count,), in_specs=in_specs, out_specs=[spec...  121 us
    pallas_call x1, Pallas kernels, gather_all(): pl.pallas_call(partial(gather_kernel, tuple(units), n), out_shape=[jax.Sh...  90.9 us
    convert_element_type x4, other arithmetic, chain(): (own + factor * entered.astype(f32)).astype(bf16)  13.3 us
    ppermute x6, starting transfers between devices, chain(): came = lax.ppermute(sent, 'ctx', [(source, target)])  11.5 us
    dot_general x1, matrix products, local(): px = MM(normed, w_x).astype(bf16)  11.5 us
    dot_general x1, matrix products, products(): out = (x_all[:count] + MM(gn, w_out)).astype(bf16)  10.4 us
  transfers between devices with their start and end apart: 9, of which 2 were waited for; matrix products, arithmetic and copies ran while one was open for 23% of the time, Pallas kernels for 61%

profile of v3, /device:TPU:0, one launch (start us, length us, event | category | flops | bytes accessed | tf_op | source)
XLA Modules:
  0.0 507.0 jit_solution(12301047778058862692)
XLA Ops:
  15.9 90.9 %shard_map.203 = (bf16[4,2,2,2,48,3456]{5,4,3,2,1,0:T(8,128)(2,1)}, bf16[4,2,2,2,16,128]{5,4,3,2,1,0:T(8,128)(2,1)}, bf16[16,1536]{1,0:T(8,128)(2,1)}) custom-call(bf16[48,3456]{1,0:T(8,128)(2,1)} %pad.54.refs_0_, bf16[16,128]{1,0:T(8,128)(2,1)} %fusion.10.refs_1_, bf16[16,1536]{1,0:T(8,128)(2,1)} %maximum_bitcast_fusion.refs_2_), custom_call_target="tpu_custom_call" | custom-call | tf_op jit(solution)/shard_map/pallas_call | solution.py:549
  115.6 11.5 %convolution_convert_fusion.2.px_ref.tail_ref = bf16[528,3456]{1,0:T(8,128)(2,1)} fusion(bf16[528,1536]{1,0:T(8,128)(2,1)S(1)} %multiply_convert_fusion.normed_ref, bf16[1536,3456]{1,0:T(8,128)(2,1)} %bitcast.74), kind=kOutput, calls=%fused_computation.2 | convolution fusion | flops 5607512064 | bytes 15888384 | tf_op jit(solution)/shard_map/dot_general | solution.py:909
  127.0 21.0 %shard_map.204 = (f32[2,256,3328]{2,1,0:T(8,128)}, f32[2,256,256]{2,1,0:T(8,128)}, f32[2,48,256]{2,1,0:T(8,128)}, f32[2,3072,128]{2,1,0:T(8,128)}) custom-call(bf16[528,3456]{1,0:T(8,128)(2,1)} %convolution_convert_fusion.2.px_ref.tail_ref, bf16[528,3456]{1,0:T(8,128)(2,1)} %convolution_convert_fusion.2.px_ref.tail_ref, f32[8,3328]{1,0:T(8,128)} %pad.59.w_ref, ...), custom_call_target="tpu_custom_call" | custom-call | tf_op jit(solution)/shard_map/pallas_call | solution.py:370
  148.0 3.3 convert_element_type.114
  151.3 2.6 collective-permute-start
  154.5 10.0 %fusion.18.dgn_ref = f32[512,3072]{1,0:T(8,128)} fusion(bf16[512,1536]{1,0:T(8,128)(2,1)} %bitcast.77, bf16[3072,1536]{1,0:T(8,128)(2,1)} %all-gather.3.cloned.1.call-done), kind=kOutput, calls=%fused_computation.79 | convolution fusion | flops 4831838208 | bytes 17301504 | tf_op jit(solution)/shard_map/dot_general | solution.py:929
  164.6 3.0 add_convert_fusion.3
  170.0 15.2 %shard_map.205.y_ref = f32[2,256,3072]{2,1,0:T(8,128)} custom-call(f32[2,256,3328]{2,1,0:T(8,128)} %get-tuple-element.55.act_ref, f32[2,256,256]{2,1,0:T(8,128)} %get-tuple-element.56.tok_ref, f32[2,48,256]{2,1,0:T(8,128)} %get-tuple-element.53.cst_ref, f32[2,256,128]{2,1,0:T(8,128)} %pad.61.cols_ref, f32[2,8,256]{2,1,0:T(8,128)} %pad.65.rows_ref), custom_call_target="tpu_custom_call" | custom-call | tf_op jit(solution)/shard_map/pallas_call | solution.py:370
  185.2 3.6 add_convert_fusion.2
  194.2 5.5 %all-gather.5.cloned.1.call-done.wz_ref = bf16[1536,3072]{1,0:T(8,128)(2,1)} async-done(((bf16[48,3072]{1,0:T(8,128)(2,1)}), bf16[1536,3072]{1,0:T(8,128)(2,1)}) %all-gather.5.cloned.1.call-update) | async-done | bytes 9437200 | tf_op jit(solution)/shard_map/all_gather | solution.py:862
  199.7 10.1 %convolution_convert_fusion.3.z_ref = bf16[512,3072]{1,0:T(8,128)(2,1)} fusion(bf16[1536,3072]{1,0:T(8,128)(2,1)} %all-gather.5.cloned.1.call-done.wz_ref, bf16[528,1536]{1,0:T(8,128)(2,1)S(1)} %copy-done.5), kind=kOutput, calls=%fused_computation.3 | convolution fusion | flops 4833411072 | bytes 14155776 | tf_op jit(solution)/shard_map/dot_general | solution.py:943
  209.8 3.8 convert_multiply_fusion
  213.5 31.0 %shard_map.206 = (bf16[512,3072]{1,0:T(8,128)(2,1)}, bf16[512,3072]{1,0:T(8,128)(2,1)}, bf16[2,256,3072]{2,1,0:T(8,128)(2,1)}, f32[2,3072,128]{2,1,0:T(8,128)}, ...) custom-call(bf16[512,3072]{1,0:T(8,128)(2,1)} %convolution_convert_fusion.3.z_ref, ...), custom_call_target="tpu_custom_call" | custom-call | tf_op jit(solution)/shard_map/pallas_call | solution.py:370
  244.6 3.4 convert_element_type.120
  249.8 10.4 %fusion = bf16[512,1536]{1,0:T(8,128)(2,1)} fusion(bf16[512,3072]{1,0:T(8,128)(2,1)} %get-tuple-element.63, bf16[3072,1536]{1,0:T(8,128)(2,1)} %all-gather.3.cloned.1.call-done, f32[528,1536]{1,0:T(8,128)S(1)} %copy-done.8), kind=kOutput, calls=%fused_computation.13 | convolution fusion | flops 4833411072 | bytes 17301504 | tf_op jit(solution)/shard_map/dot_general | solution.py:965
  260.3 7.5 %convolution_convert_fusion.1 = bf16[3072,1536]{1,0:T(8,128)(2,1)} fusion(bf16[512,3072]{1,0:T(8,128)(2,1)S(1)} %copy-done.18, bf16[512,1536]{1,0:T(8,128)(2,1)S(1)} %bitcast.79), kind=kOutput, calls=%fused_computation.1 | convolution fusion | flops 4836556800 | bytes 14155776 | tf_op jit(solution)/shard_map/dot_general | solution.py:966
  269.7 3.0 add_convert_fusion.1
  274.5 17.0 %shard_map.207 = (f32[2,256,3072]{2,1,0:T(8,128)}, f32[2,256,256]{2,1,0:T(8,128)}) custom-call(f32[2,256,3328]{2,1,0:T(8,128)} %get-tuple-element.55.act_ref, f32[2,256,256]{2,1,0:T(8,128)} %get-tuple-element.56.tok_ref, f32[2,48,256]{2,1,0:T(8,128)} %get-tuple-element.53.cst_ref, f32[2,256,128]{2,1,0:T(8,128)} %pad.61.cols_ref, f32[2,8,256]{2,1,0:T(8,128)} %pad.65.rows_ref, ...), custom_call_target="tpu_custom_call" | custom-call | tf_op jit(solution)/shard_map/pallas_call | solution.py:370
  291.4 3.7 add_convert_fusion
  297.5 10.0 %convolution_convert_fusion = bf16[1536,3072]{1,0:T(8,128)(2,1)} fusion(bf16[512,3072]{1,0:T(8,128)(2,1)} %get-tuple-element.70.dz_ref, bf16[528,1536]{1,0:T(8,128)(2,1)} %copy-done.4), kind=kOutput, calls=%fused_computation | convolution fusion | flops 4836556800 | bytes 14155776 | tf_op jit(solution)/shard_map/dot_general | solution.py:980
  307.5 5.9 %collective-permute-done.5 = bf16[2,3072,128]{2,1,0:T(8,128)(2,1)S(1)} collective-permute-done((bf16[2,3072,128]{2,1,0:T(8,128)(2,1)}, bf16[2,3072,128]{2,1,0:T(8,128)(2,1)S(1)}, u32[]{:S(2)}, u32[]{:S(2)}) %collective-permute-start.5) | collective-permute-done | bytes 1572896 | tf_op jit(solution)/shard_map/ppermute | solution.py:386
  314.9 37.0 %shard_map.208 = (bf16[512,3456]{1,0:T(8,128)(2,1)}, f32[2,8,3456]{2,1,0:T(8,128)}, f32[2,8,3328]{2,1,0:T(8,128)}, f32[2,8,128]{2,1,0:T(8,128)}) custom-call(bf16[528,3456]{1,0:T(8,128)(2,1)} %convolution_convert_fusion.2.px_ref.tail_ref, bf16[528,3456]{1,0:T(8,128)(2,1)} %convolution_convert_fusion.2.px_ref.tail_ref, f32[8,3328]{1,0:T(8,128)} %pad.59.w_ref, ...), custom_call_target="tpu_custom_call" | custom-call | tf_op jit(solution)/shard_map/pallas_call | solution.py:370
  355.9 4.1 pad_maximum_fusion.dpx_ref
  360.0 127.9 %shard_map.209 = (f32[48,3072]{1,0:T(8,128)}, f32[48,3456]{1,0:T(8,128)}, f32[8,128]{1,0:T(8,128)}, bf16[512,1536]{1,0:T(8,128)(2,1)}) custom-call(bf16[4,2,2,2,48,3072]{5,4,3,2,1,0:T(8,128)(2,1)} %bitcast.76, f32[4,2,2,2,8,128]{5,4,3,2,1,0:T(8,128)} %bitcast.82, bf16[528,3456]{1,0:T(8,128)(2,1)} %pad_maximum_fusion.dpx_ref, bf16[528,1536]{1,0:T(8,128)(2,1)} %copy-done.4, ...), custom_call_target="tpu_custom_call" | custom-call | tf_op jit(solution)/shard_map/pallas_call | solution.py:815
  (144 shorter events, 51.1 us)
Async XLA Ops:
  7.2 105.7 %copy-start.2 = (bf16[2,256,1536]{2,1,0:T(8,128)(2,1)S(1)}, bf16[2,256,1536]{2,1,0:T(8,128)(2,1)}, u32[]{:S(2)}) copy-start(bf16[2,256,1536]{2,1,0:T(8,128)(2,1)} %param.12) | copy-start | bytes 4718596
  7.2 103.9 %copy-start.14 = (s32[2,256]{1,0:T(2,128)S(1)}, s32[2,256]{1,0:T(2,128)}, u32[]{:S(2)}) copy-start(s32[2,256]{1,0:T(2,128)} %param.22) | copy-start | bytes 6148
  7.2 147.3 %all-gather.3.cloned.1.call-start = ((), (), s32[]{:S(2)}) async-start(), calls=%async_computation.1 | async-start | bytes 9732096 | tf_op jit(solution)/shard_map/all_gather | solution.py:861
  7.9 191.8 %all-gather.5.cloned.1.call-start = ((), (), s32[]{:S(2)}) async-start(), calls=%async_computation.2 | async-start | bytes 9732096 | tf_op jit(solution)/shard_map/all_gather | solution.py:862
  9.7 103.6 %copy-start.16 = (f32[48]{0:T(128)S(1)}, f32[48]{0:T(128)}, u32[]{:S(2)}) copy-start(f32[48]{0:T(128)} %param.18) | copy-start | bytes 580
  9.7 103.6 %copy-start.17 = (f32[48]{0:T(128)S(1)}, f32[48]{0:T(128)}, u32[]{:S(2)}) copy-start(f32[48]{0:T(128)} %param.17) | copy-start | bytes 580
  9.7 487.3 %reduce-scatter.2.cloned.1.call-start = ((), (), s32[]{:S(2)}) async-start(), calls=%async_computation.3 | async-start | bytes 9732096 | tf_op jit(solution)/shard_map/reduce_scatter | solution.py:1021
  112.8 78.2 %copy-start.11 = (bf16[16,1536]{1,0:T(8,128)(2,1)}, bf16[16,1536]{1,0:T(8,128)(2,1)S(1)}, u32[]{:S(2)}) copy-start(bf16[16,1536]{1,0:T(8,128)(2,1)S(1)} %select_bitcast_fusion.tail_ref) | copy-start | bytes 147460
  148.0 6.1 %copy-start.12 = (f32[2,48,256]{2,1,0:T(8,128)S(1)}, f32[2,48,256]{2,1,0:T(8,128)}, u32[]{:S(2)}) copy-start(f32[2,48,256]{2,1,0:T(8,128)} %get-tuple-element.53.cst_ref) | copy-start | bytes 294916
  151.3 13.3 %collective-permute-start = (bf16[2,3072,128]{2,1,0:T(8,128)(2,1)}, bf16[2,3072,128]{2,1,0:T(8,128)(2,1)}, u32[]{:S(2)}, u32[]{:S(2)}) collective-permute-start(bf16[2,3072,128]{2,1,0:T(8,128)(2,1)} %convert_element_type.114), channel_id=1, source_target_pairs={{0,1},{4,5},{8,9},{12,13},{16,17},{20,21},{24,25},{28,29}} | collective-permute-start | bytes 4718600 | tf_op jit(solution)/shard_map/ppermute | solution.py:386
  154.5 10.0 %copy-start.1 = (f32[2,3072,128]{2,1,0:T(8,128)S(1)}, f32[2,3072,128]{2,1,0:T(8,128)}, u32[]{:S(2)}) copy-start(f32[2,3072,128]{2,1,0:T(8,128)} %get-tuple-element.52) | copy-start | bytes 9437188
  167.6 17.7 %collective-permute-start.1 = (bf16[2,3072,128]{2,1,0:T(8,128)(2,1)}, bf16[2,3072,128]{2,1,0:T(8,128)(2,1)}, u32[]{:S(2)}, u32[]{:S(2)}) collective-permute-start(bf16[2,3072,128]{2,1,0:T(8,128)(2,1)} %add_convert_fusion.3), channel_id=1, source_target_pairs={{1,2},{5,6},{9,10},{13,14},{17,18},{21,22},{25,26},{29,30}} | collective-permute-start | bytes 4718600 | tf_op jit(solution)/shard_map/ppermute | solution.py:386
  185.2 5.8 %copy-start.3 = (bf16[2,256,1536]{2,1,0:T(8,128)(2,1)S(1)}, bf16[2,256,1536]{2,1,0:T(8,128)(2,1)}, u32[]{:S(2)}) copy-start(bf16[2,256,1536]{2,1,0:T(8,128)(2,1)} %param.12) | copy-start | bytes 4718596
  188.9 10.8 %copy-start.5 = (bf16[528,1536]{1,0:T(8,128)(2,1)S(1)}, bf16[528,1536]{1,0:T(8,128)(2,1)}, u32[]{:S(2)}) copy-start(bf16[528,1536]{1,0:T(8,128)(2,1)} %copy-done.4) | copy-start | bytes 4866052
  188.9 20.9 %collective-permute-start.2 = (bf16[2,3072,128]{2,1,0:T(8,128)(2,1)}, bf16[2,3072,128]{2,1,0:T(8,128)(2,1)}, u32[]{:S(2)}, u32[]{:S(2)}) collective-permute-start(bf16[2,3072,128]{2,1,0:T(8,128)(2,1)} %get-tuple-element.93), channel_id=1, source_target_pairs={{2,3},{6,7},{10,11},{14,15},{18,19},{22,23},{26,27},{30,31}} | collective-permute-start | bytes 4718600 | tf_op jit(solution)/shard_map/ppermute | solution.py:386
  194.1 15.6 %copy-start.7 = (bf16[2,3072,128]{2,1,0:T(8,128)(2,1)S(1)}, bf16[2,3072,128]{2,1,0:T(8,128)(2,1)}, u32[]{:S(2)}) copy-start(bf16[2,3072,128]{2,1,0:T(8,128)(2,1)} %get-tuple-element.94) | copy-start | bytes 4718596
  248.0 19.8 %collective-permute-start.3 = (bf16[2,3072,128]{2,1,0:T(8,128)(2,1)}, bf16[2,3072,128]{2,1,0:T(8,128)(2,1)}, u32[]{:S(2)}, u32[]{:S(2)}) collective-permute-start(bf16[2,3072,128]{2,1,0:T(8,128)(2,1)} %convert_element_type.120), channel_id=1, source_target_pairs={{3,2},{7,6},{11,10},{15,14},{19,18},{23,22},{27,26},{31,30}} | collective-permute-start | bytes 4718600 | tf_op jit(solution)/shard_map/ppermute | solution.py:386
  249.8 10.4 %copy-start.9 = (bf16[2,256,1536]{2,1,0:T(8,128)(2,1)S(1)}, bf16[2,256,1536]{2,1,0:T(8,128)(2,1)}, u32[]{:S(2)}) copy-start(bf16[2,256,1536]{2,1,0:T(8,128)(2,1)} %param.23) | copy-start | bytes 4718596
  249.8 10.4 %copy-start.18 = (bf16[512,3072]{1,0:T(8,128)(2,1)S(1)}, bf16[512,3072]{1,0:T(8,128)(2,1)}, u32[]{:S(2)}) copy-start(bf16[512,3072]{1,0:T(8,128)(2,1)} %get-tuple-element.63) | copy-start | bytes 9437188
  272.6 18.8 %collective-permute-start.4 = (bf16[2,3072,128]{2,1,0:T(8,128)(2,1)}, bf16[2,3072,128]{2,1,0:T(8,128)(2,1)}, u32[]{:S(2)}, u32[]{:S(2)}) collective-permute-start(bf16[2,3072,128]{2,1,0:T(8,128)(2,1)} %add_convert_fusion.1), channel_id=1, source_target_pairs={{2,1},{6,5},{10,9},{14,13},{18,17},{22,21},{26,25},{30,29}} | collective-permute-start | bytes 4718600 | tf_op jit(solution)/shard_map/ppermute | solution.py:386
  291.4 5.7 %copy-start.13 = (f32[2,8,3072]{2,1,0:T(8,128)S(1)}, f32[2,8,3072]{2,1,0:T(8,128)}, u32[]{:S(2)}) copy-start(f32[2,8,3072]{2,1,0:T(8,128)} %get-tuple-element.72) | copy-start | bytes 589828
  295.1 18.2 %collective-permute-start.5 = (bf16[2,3072,128]{2,1,0:T(8,128)(2,1)}, bf16[2,3072,128]{2,1,0:T(8,128)(2,1)S(1)}, u32[]{:S(2)}, u32[]{:S(2)}) collective-permute-start(bf16[2,3072,128]{2,1,0:T(8,128)(2,1)} %get-tuple-element.91), channel_id=1, source_target_pairs={{1,0},{5,4},{9,8},{13,12},{17,16},{21,20},{25,24},{29,28}} | collective-permute-start | bytes 4718600 | tf_op jit(solution)/shard_map/ppermute | solution.py:386
  297.5 15.9 %copy-start.6 = (bf16[2,3072,128]{2,1,0:T(8,128)(2,1)S(1)}, bf16[2,3072,128]{2,1,0:T(8,128)(2,1)}, u32[]{:S(2)}) copy-start(bf16[2,3072,128]{2,1,0:T(8,128)(2,1)} %get-tuple-element.92) | copy-start | bytes 4718596
  487.9 11.0 %copy-start.10 = (bf16[512,1536]{1,0:T(8,128)(2,1)S(1)}, bf16[512,1536]{1,0:T(8,128)(2,1)}, u32[]{:S(2)}) copy-start(bf16[512,1536]{1,0:T(8,128)(2,1)} %get-tuple-element.82) | copy-start | bytes 4718596
  (4 other events, 12.7 us)
Sparse Core Ops, SparseCore 0:
  10.9 102.9 all-gather.2
  117.4 82.2 all-gather.4
  267.9 157.4 reduce-scatter.1

commit v4 on v1

v4 whole, which is shorter than its diff:
```python
from functools import partial

import jax
import jax.numpy as jnp
from jax import lax
from jax.experimental import pallas as pl
from jax.experimental.pallas import tpu as pltpu
from jax.sharding import PartitionSpec as P

HEADS = 48
STATE = 128
HEADDIM = 64
CONV = 4
INNER = HEADS * HEADDIM
CHANNELS = INNER + 2 * STATE
GROUP = 8
GROUPS = HEADS // GROUP
WIDTH = GROUP * HEADDIM
LANES = 128
EPSILON = 1e-05
VMEM = 60 * 1024 * 1024
FINISH_VMEM = 62 * 1024 * 1024 - 512 * 1024
BOTH = ("seq", "ctx")
FAR = -1e30
f32 = jnp.float32
bf16 = jnp.bfloat16
MM = partial(jnp.dot, preferred_element_type=f32)


def mm_nt(a, b):
    return lax.dot_general(a, b, (((1,), (1,)), ((), ())), preferred_element_type=f32)


def mm_tn(a, b):
    return lax.dot_general(a, b, (((0,), (0,)), ((), ())), preferred_element_type=f32)


def sigmoid(v):
    return 0.5 + 0.5 * jnp.tanh(0.5 * v)


def at(j, width):
    return pl.ds(pl.multiple_of(j * width, width), width)


def low_half(rows):
    return lax.broadcasted_iota(jnp.int32, (rows, LANES), 1) < HEADDIM


def to_front(columns, g):
    return pltpu.roll(columns, lax.rem(LANES - GROUP * g, LANES), 1)


def spread(front, pair, low):
    return jnp.where(low, front[:, 2 * pair : 2 * pair + 1], front[:, 2 * pair + 1 : 2 * pair + 2])


def head_sums(product, g):
    lane = lax.broadcasted_iota(jnp.int32, (WIDTH, LANES), 1)
    row = lax.broadcasted_iota(jnp.int32, (WIDTH, LANES), 0)
    pick = jnp.where(lane == row // HEADDIM, 1.0, 0.0).astype(bf16)
    high = product.astype(bf16)
    rest = (product - high.astype(f32)).astype(bf16)
    return pltpu.roll(MM(high, pick) + MM(rest, pick), GROUP * g, 1)


def taps(px_ref, tail, j, w_ref, b_ref, masks, ext):
    here = at(j, LANES)
    length = px_ref.shape[0]
    own = px_ref[:, here].astype(f32)
    ext[0:8, :] = tail
    ext[8 : 8 + length, :] = own
    inputs = [own] + [
        masks[k - 1] * ext[8 - k : 8 - k + length, :] for k in range(1, CONV)
    ]
    out = b_ref[0:1, here]
    for k in range(CONV):
        out = out + w_ref[k : k + 1, here] * inputs[k]
    return out, inputs


def tail_of(tail_ref, s, here):
    both = tail_ref[:, here].astype(f32)
    return jnp.where(s == 0, both[0:8], both[8:16])


def lane_masks(cols_ref, length):
    return [
        jnp.broadcast_to(cols_ref[0, :, k : k + 1], (length, LANES)) for k in range(CONV - 1)
    ]


NZ = 4


def place():
    seq, ctx = lax.axis_index("seq"), lax.axis_index("ctx")
    return seq // 2, lax.rem(seq, 2), ctx // 2, lax.rem(ctx, 2)


def device(z, y, x, c):
    return {"seq": z * 2 + y, "ctx": x * 2 + c}


def greet(z, y, x, c, more=0):
    barrier = pltpu.get_barrier_semaphore()
    others = [device(z, y, x, 1 - c), device(z, y, 1 - x, c), device(z, 1 - y, x, c)]
    others += [device(lax.rem(z + d, NZ), y, x, c) for d in range(1, NZ)]
    for other in others:
        pl.semaphore_signal(barrier, inc=1, device_id=other, device_id_type=pl.DeviceIdType.MESH)
    pl.semaphore_wait(barrier, len(others) + more)


def remote(src, dst, send, recv, target):
    return pltpu.make_async_remote_copy(
        src_ref=src, dst_ref=dst, send_sem=send, recv_sem=recv, device_id=target,
        device_id_type=pl.DeviceIdType.MESH,
    )


def gather_kernel(units, n, *refs):
    ins, outs, land, (tail_land, send, recv, local, store, tail_sem) = (
        refs[: n + 1], refs[n + 1 : 2 * n + 2], refs[2 * n + 2 : 3 * n + 2], refs[3 * n + 2 :]
    )
    x_first = [first for _array, _row, _rows, first in units]
    z, y, x, c = place()
    ctx = x * 2 + c
    after, before = lax.rem(ctx + 1, 4), lax.rem(ctx + 3, 4)
    barrier = pltpu.get_barrier_semaphore()
    for other in (after, before):
        pl.semaphore_signal(
            barrier, inc=1, device_id={"seq": z * 2 + y, "ctx": other},
            device_id_type=pl.DeviceIdType.MESH,
        )
    greet(z, y, x, c, 2)
    started, stored = [], []

    def shard(u):
        a, row, rows, _first = units[u]
        return ins[a].at[pl.ds(row, rows)]

    def slot_of(u, *at, into=None):
        a, row, rows, _first = units[u]
        return (land if into is None else into)[a].at[at + (pl.ds(row, rows),)]

    def number(u, kind, index):
        first = "x" if x_first[u] else "y"
        base = 0 if kind == "z" else 3 if kind == first else 15 if kind == "c" else 7
        return base + (index - 1 if kind == "z" else index)

    def push(u, zz, yy, xx, kind, index):
        slot = slot_of(u, zz, yy, xx, c)
        if kind == "z":
            target = device(lax.rem(z + index, NZ), y, x, c)
        else:
            flip = [1 - v if k == kind else v for k, v in (("y", y), ("x", x), ("c", c))]
            target = device(z, *flip)
        k = number(u, kind, index)
        copy = remote(slot, slot, send.at[u, k], recv.at[u, k], target)
        copy.start()
        started.append(copy)

    def came(u, zz, yy, xx, cc, kind, index):
        slot = slot_of(u, zz, yy, xx, cc)
        k = number(u, kind, index)
        remote(slot, slot, send.at[u, k], recv.at[u, k], device(z, y, x, 1 - c)).wait_recv()
        keep = pltpu.make_async_copy(slot, slot_of(u, zz, yy, xx, cc, into=outs), store.at[u, k])
        keep.start()
        stored.append(keep)

    back = [lax.rem(z + NZ - d, NZ) for d in range(NZ)]
    axes = [("x", "y") if first else ("y", "x") for first in x_first]
    every = range(len(units))
    ring = remote(
        ins[n], tail_land, tail_sem.at[0], tail_sem.at[1], {"seq": z * 2 + y, "ctx": after}
    )
    ring.start()
    for u in every:
        pltpu.make_async_copy(shard(u), slot_of(u, z, y, x, c), local.at[u]).start()

    def open_unit(u):
        a, b = axes[u]
        slot = slot_of(u, z, y, x, c)
        pltpu.make_async_copy(shard(u), slot, local.at[u]).wait()
        for d in (1, 3, 2):
            push(u, z, y, x, "z", d)
        for kind in (b, a, "c"):
            push(u, z, y, x, kind, 0)
        keep = pltpu.make_async_copy(slot, slot_of(u, z, y, x, c, into=outs), local.at[u])
        keep.start()
        stored.append(keep)

    def pass_on(u):
        a, b = axes[u]
        yy, xx = (y, 1 - x) if a == "x" else (1 - y, x)
        for d in range(1, NZ + 1):
            if d < NZ:
                came(u, back[d], y, x, c, "z", d)
                for kind in (b, a, "c"):
                    push(u, back[d], y, x, kind, d)
            came(u, back[d - 1], yy, xx, c, a, d - 1)
            push(u, back[d - 1], yy, xx, b, NZ + d - 1)
            push(u, back[d - 1], yy, xx, "c", NZ + d - 1)

    def cross(u):
        a, b = axes[u]
        for half in range(2):
            yy, xx = (1 - y, x) if b == "y" else (y, 1 - x)
            if half:
                yy, xx = 1 - y, 1 - x
            for d in range(NZ):
                came(u, back[d], yy, xx, c, b, NZ * half + d)
                push(u, back[d], yy, xx, "c", 2 * NZ + NZ * half + d)

    def finish(u):
        a, b = axes[u]
        for k in range(16):
            away = {a: (k // NZ) % 2, b: k // (2 * NZ)}
            came(u, back[k % NZ], 1 - y if away["y"] else y, 1 - x if away["x"] else x, 1 - c, "c", k)

    for t in range(-AHEAD, len(units) + 4):
        if 0 <= t + AHEAD < len(units):
            open_unit(t + AHEAD)
        if 0 <= t < len(units):
            pass_on(t)
        if 0 <= t - 2 < len(units):
            cross(t - 2)
        if 0 <= t - 4 < len(units):
            finish(t - 4)
    ring.wait_recv()
    keep = pltpu.make_async_copy(tail_land, outs[n], tail_sem.at[2])
    keep.start()
    keep.wait()
    ring.wait_send()
    for copy in started:
        copy.wait_send()
    for keep in stored:
        keep.wait()


def gather_all(shards, tail, units):
    n, m = len(shards), len(units)
    full = [(NZ, 2, 2, 2) + v.shape for v in shards]
    return pl.pallas_call(
        partial(gather_kernel, tuple(units), n),
        out_shape=[jax.ShapeDtypeStruct(f, v.dtype) for f, v in zip(full, shards)]
        + [jax.ShapeDtypeStruct(tail.shape, tail.dtype)],
        in_specs=[pl.BlockSpec(memory_space=pl.ANY)] * (n + 1),
        out_specs=[pl.BlockSpec(memory_space=pl.ANY)] * (n + 1),
        scratch_shapes=[pltpu.VMEM(f, v.dtype) for f, v in zip(full, shards)] + [
            pltpu.VMEM(tail.shape, tail.dtype),
            pltpu.SemaphoreType.DMA((m, 31)), pltpu.SemaphoreType.DMA((m, 31)),
            pltpu.SemaphoreType.DMA((m,)), pltpu.SemaphoreType.DMA((m, 31)),
            pltpu.SemaphoreType.DMA((3,)),
        ],
        compiler_params=pltpu.CompilerParams(
            collective_id=0, has_side_effects=True, vmem_limit_bytes=VMEM
        ),
    )(*shards, tail)


CUT_ROWS, CUT = 48, 512
SLOTS = 3
LEAD = (0, 5, 7, 9)
AHEAD = 4


def meet(place_of, ring):
    z, y, x, c = place_of
    if ring:
        barrier = pltpu.get_barrier_semaphore()
        for step in (1, 3):
            pl.semaphore_signal(
                barrier, inc=1, device_id={"seq": z * 2 + y, "ctx": lax.rem(x * 2 + c + step, 4)},
                device_id_type=pl.DeviceIdType.MESH,
            )
    greet(z, y, x, c, 2 if ring else 0)


class Reduction:
    def __init__(self, place_of, source, own, buffers, result, sem, semz):
        self.place, self.source, self.own, self.buffers = place_of, source, own, buffers
        self.result, self.sem, self.semz = result, sem, semz

    def copies(self, i, stage):
        z, y, x, c = self.place
        core, first, second, last = self.buffers(i)
        x_first = i % 2 == 0
        along_x, along_y = device(z, y, 1 - x, c), device(z, 1 - y, x, c)
        if stage == 0:
            moves = [(self.source(i, 1 - c), core, device(z, y, x, 1 - c))]
        elif stage == 1:
            src = core.at[:, :, 1 - x] if x_first else core.at[:, 1 - y]
            moves = [(src, first, along_x if x_first else along_y)]
        elif stage == 2:
            src = first.at[:, 1 - y] if x_first else first.at[:, 1 - x]
            moves = [(src, second, along_y if x_first else along_x)]
        else:
            moves = []
            for d in range(1, NZ):
                zz = lax.rem(z + d, NZ)
                moves.append((second.at[zz], last.at[z], device(zz, y, x, c)))
        made = []
        for d, (src, dst, to) in enumerate(moves):
            if stage < 3:
                sems = self.sem.at[2 * stage, i], self.sem.at[2 * stage + 1, i]
            else:
                sems = self.semz.at[0, d, i], self.semz.at[1, d, i]
            made.append(remote(src, dst, *sems, to))
        return made

    def send(self, i, stage):
        for copy in self.copies(i, stage):
            copy.start()

    def drain(self, i):
        for stage in range(4):
            for copy in self.copies(i, stage):
                copy.wait_send()

    def arrive(self, i, stage):
        z, y, x, c = self.place
        core, first, second, last = self.buffers(i)
        x_first = i % 2 == 0
        if stage < 3:
            landed = (core, first, second)[stage]
            remote(
                landed, landed, self.sem.at[2 * stage, i], self.sem.at[2 * stage + 1, i],
                device(z, y, x, 1 - c),
            ).wait_recv()
        if stage == 0:
            own = self.own(i)

            @pl.loop(0, NZ)
            def _(zz):
                for yy in range(2):
                    for xx in range(2):
                        core[zz, yy, xx] = core[zz, yy, xx] + own(zz, yy, xx)

        elif stage == 1:

            @pl.loop(0, NZ)
            def _(zz):
                for o in range(2):
                    first[zz, o] = first[zz, o] + (core[zz, o, x] if x_first else core[zz, y, o])

        elif stage == 2:

            @pl.loop(0, NZ)
            def _(zz):
                second[zz] = second[zz] + (first[zz, y] if x_first else first[zz, x])

            last[z] = second[z]
        else:
            for d in range(1, NZ):
                landed = last.at[lax.rem(z + NZ - d, NZ)]
                remote(
                    landed, landed, self.semz.at[0, d - 1, i], self.semz.at[1, d - 1, i],
                    device(z, y, x, 1 - c),
                ).wait_recv()
            value = last[0].astype(f32)
            for zz in range(1, NZ):
                value = value + last[zz].astype(f32)
            self.result(i, value)
        if stage < 3:
            self.send(i, stage + 1)


def reduction_buffers(count, shape, dtype):
    return [pltpu.VMEM((count,) + d + shape, dtype) for d in ((NZ, 2, 2), (NZ, 2), (NZ,), (NZ,))]


def reduction_semaphores(count):
    return [pltpu.SemaphoreType.DMA((6, count)), pltpu.SemaphoreType.DMA((2, NZ - 1, count))]


def cut_to(width, ref):
    if ref.shape[-1] == width:
        return ref
    return ref.at[(slice(None),) * (len(ref.shape) - 1) + (pl.ds(0, width),)]


def before_kernel(px_ref, tail_ref, w_ref, b_ref, cols_ref, heads_ref,
                  act_ref, tok_ref, cst_ref, fresh_ref, ext):
    s = pl.program_id(0)
    length = px_ref.shape[0]
    masks = lane_masks(cols_ref, length)

    @pl.loop(0, CHANNELS // LANES)
    def _(j):
        here = at(j, LANES)
        conv, _unused = taps(px_ref, tail_of(tail_ref, s, here), j, w_ref, b_ref, masks, ext)
        act_ref[0, :, here] = conv * sigmoid(conv)

    raw = px_ref[:, CHANNELS : CHANNELS + HEADS].astype(f32) + heads_ref[0:1, :HEADS]
    step = jnp.maximum(raw, 0.0) + jnp.log1p(jnp.exp(-jnp.abs(raw)))
    step = jnp.concatenate([step, jnp.zeros((length, LANES - HEADS), f32)], axis=1)
    rate = -step * jnp.exp(heads_ref[1:2, :])
    before = (
        lax.broadcasted_iota(jnp.int32, (length, length), 0)
        >= lax.broadcasted_iota(jnp.int32, (length, length), 1)
    ).astype(f32)
    decay = jnp.dot(before, rate, precision=lax.Precision.HIGHEST, preferred_element_type=f32)
    tok_ref[0, :, 0:LANES] = step
    tok_ref[0, :, LANES : 2 * LANES] = decay
    cst_ref[0] = decay.T[:HEADS]
    toward = jnp.exp(decay[length - 1 : length] - decay) * step * cols_ref[0, :, 4:5]
    keys = act_ref[0, :, INNER : INNER + STATE].astype(bf16)
    low = low_half(length)

    @pl.loop(0, GROUPS)
    def _(g):
        front = to_front(toward, g)
        scaled = []
        for pair in range(GROUP // 2):
            here = pl.ds(pl.multiple_of(g * WIDTH + pair * LANES, LANES), LANES)
            scaled.append((act_ref[0, :, here] * spread(front, pair, low)).astype(bf16))
        fresh_ref[0, at(g, WIDTH), :] = mm_tn(jnp.concatenate(scaled, axis=1), keys)


def bias_of(ids_col, ids_row, transposed):
    shape = (ids_col.shape[0], ids_row.shape[1])
    down = lax.broadcasted_iota(jnp.int32, shape, 0)
    across = lax.broadcasted_iota(jnp.int32, shape, 1)
    order = (down <= across) if transposed else (down >= across)
    return jnp.where(order & (ids_col == ids_row), 0.0, FAR)


def within_kernel(act_ref, tok_ref, cst_ref, cols_ref, rows_ref, y_ref, cross, bias):
    length = act_ref.shape[1]
    half = length // 2
    cross[...] = mm_nt(
        act_ref[0, :, INNER + STATE :].astype(bf16),
        act_ref[0, :, INNER : INNER + STATE].astype(bf16),
    )
    bias[...] = bias_of(cols_ref[0, :, 5:6], rows_ref[0, 0:1, :], False)
    low = low_half(length)

    @pl.loop(0, GROUPS)
    def _(g):
        step = to_front(tok_ref[0, :, 0:LANES], g)
        decay = to_front(tok_ref[0, :, LANES : 2 * LANES], g)
        rows = cst_ref[0, at(g, GROUP), :]
        for pair in range(GROUP // 2):
            here = pl.ds(pl.multiple_of(g * WIDTH + pair * LANES, LANES), LANES)
            scaled = act_ref[0, :, here] * spread(step, pair, low)
            top, bottom = 0.0, 0.0
            for which in range(2):
                h = 2 * pair + which
                mine = jnp.where(low == (which == 0), scaled, 0.0).astype(bf16)
                col, row = decay[:, h : h + 1], rows[h : h + 1, :]
                w = jnp.exp(col[:half] - row[:, :half] + bias[:half, :half])
                top = top + MM((cross[:half, :half] * w).astype(bf16), mine[:half])
                w = jnp.exp(col[half:] - row + bias[half:, :])
                bottom = bottom + MM((cross[half:, :] * w).astype(bf16), mine)
            y_ref[0, :half, here] = top
            y_ref[0, half:, here] = bottom


def gate_kernel(z_ref, act_ref, tok_ref, cols_ref, y_ref, state_ref, dgn_ref, lanes_ref,
                gn_ref, dz_ref, dy_ref, dstate_ref, q_ref, dq_ref, sums_ref, total, queries_acc):
    length = act_ref.shape[1]
    low = low_half(length)
    enter = jnp.exp(tok_ref[0, :, LANES : 2 * LANES]) * cols_ref[0, :, 3:4]
    queries = act_ref[0, :, INNER + STATE :].astype(bf16)

    def first(g, carry):
        square, inner = carry
        front = to_front(enter, g)
        group_far = mm_nt(queries, state_ref[0, at(g, WIDTH), :])
        for pair in range(GROUP // 2):
            here = pl.ds(pl.multiple_of(g * WIDTH + pair * LANES, LANES), LANES)
            far = group_far[:, pair * LANES : (pair + 1) * LANES]
            y = y_ref[0, :, here] + spread(front, pair, low) * far
            total[:, here] = y
            y = y + lanes_ref[1:2, here] * act_ref[0, :, here]
            z = z_ref[:, here].astype(f32)
            gated = y * (z * sigmoid(z))
            square = square + gated * gated
            inner = inner + lanes_ref[0:1, here] * dgn_ref[:, here] * gated
        return square, inner

    zero = jnp.zeros((length, LANES), f32)
    square, inner = lax.fori_loop(0, GROUPS, first, (zero, zero))
    scale = lax.rsqrt(jnp.sum(square, axis=1, keepdims=True) * (1.0 / INNER) + EPSILON)
    back = scale * scale * scale * (jnp.sum(inner, axis=1, keepdims=True) * (1.0 / INNER))
    scale = jnp.broadcast_to(scale, (length, LANES))
    back = jnp.broadcast_to(back, (length, LANES))
    queries_acc[...] = jnp.zeros_like(queries_acc)
    dq_ref[0] = jnp.zeros_like(dq_ref[0])

    @pl.loop(0, GROUPS)
    def _(g):
        front = to_front(enter, g)
        products, entered = [], []
        for pair in range(GROUP // 2):
            here = pl.ds(pl.multiple_of(g * WIDTH + pair * LANES, LANES), LANES)
            xs = act_ref[0, :, here]
            inside = total[:, here]
            y = inside + lanes_ref[1:2, here] * xs
            z = z_ref[:, here].astype(f32)
            sg = sigmoid(z)
            gate = z * sg
            gated = y * gate
            gain = lanes_ref[0:1, here]
            dgn = dgn_ref[:, here]
            gn = gated * scale
            gn_ref[:, here] = (gn * gain).astype(bf16)
            dgated = scale * (gain * dgn) - gated * back
            dy = dgated * gate
            dz_ref[:, here] = (dgated * y * (sg * (1.0 + z * (1.0 - sg)))).astype(bf16)
            rounded = dy.astype(bf16)
            dy_ref[0, :, here] = rounded
            sums_ref[0, 0:1, here] = jnp.sum(dgn * gn, axis=0, keepdims=True)
            sums_ref[0, 1:2, here] = jnp.sum(dy * xs, axis=0, keepdims=True)
            rounded = rounded.astype(f32)
            entered.append((rounded * spread(front, pair, low)).astype(bf16))
            products.append(rounded * inside)
        entered = jnp.concatenate(entered, axis=1)
        dstate_ref[0, at(g, WIDTH), :] = mm_tn(entered, queries)
        queries_acc[...] += MM(entered, state_ref[0, at(g, WIDTH), :])
        dq_ref[0] += head_sums(jnp.concatenate(products, axis=1), g)

    q_ref[0] = queries_acc[...]


def scan_back_kernel(act_ref, tok_ref, cst_ref, cols_ref, rows_ref, dy_ref,
                     dx_ref, dbc_ref, cross, bias, dcross):
    length = act_ref.shape[1]
    half = length // 2
    keys = act_ref[0, :, INNER : INNER + STATE].astype(bf16)
    queries = act_ref[0, :, INNER + STATE :].astype(bf16)
    cross[...] = mm_nt(keys, queries)
    bias[...] = bias_of(cols_ref[0, :, 5:6], rows_ref[0, 0:1, :], True)
    dcross[...] = jnp.zeros_like(dcross)
    low = low_half(length)

    @pl.loop(0, GROUPS)
    def _(g):
        step = to_front(tok_ref[0, :, 0:LANES], g)
        decay = to_front(tok_ref[0, :, LANES : 2 * LANES], g)
        rows = cst_ref[0, at(g, GROUP), :]
        for pair in range(GROUP // 2):
            here = pl.ds(pl.multiple_of(g * WIDTH + pair * LANES, LANES), LANES)
            scaled = (act_ref[0, :, here] * spread(step, pair, low)).astype(bf16)
            dy = dy_ref[0, :, here].astype(f32)
            top, bottom = 0.0, 0.0
            for which in range(2):
                h = 2 * pair + which
                mine = jnp.where(low == (which == 0), dy, 0.0).astype(bf16)
                col, row = decay[:, h : h + 1], rows[h : h + 1, :]
                w = jnp.exp(row - col[:half] + bias[:half, :])
                dcross[:half, :] += mm_nt(scaled[:half], mine) * w
                top = top + MM((cross[:half, :] * w).astype(bf16), mine)
                w = jnp.exp(row[:, half:] - col[half:] + bias[half:, half:])
                dcross[half:, half:] += mm_nt(scaled[half:], mine[half:]) * w
                bottom = bottom + MM((cross[half:, half:] * w).astype(bf16), mine[half:])
            dx_ref[0, :half, here] = top
            dx_ref[0, half:, here] = bottom

    d = dcross[...].astype(bf16)
    dbc_ref[0, :, :STATE] = MM(d, queries)
    dbc_ref[0, :, STATE:] = mm_tn(d, keys)


def after_kernel(px_ref, tail_ref, w_ref, b_ref, cols_ref, heads_ref, act_ref, tok_ref, lanes_ref,
                 dy_ref, dx_ref, dbc_ref, q_ref, dq_ref, later_ref, kept_ref,
                 dpx_ref, dconv_ref, dheads_ref, ext, moved, grad, dstep_acc, dcol_acc, keys_acc, ends, sent, edges):
    s = pl.program_id(0)
    length = act_ref.shape[1]
    low = low_half(length)
    step = tok_ref[0, :, 0:LANES]
    decay = tok_ref[0, :, LANES : 2 * LANES]
    leave = jnp.exp(decay[length - 1 : length] - decay) * cols_ref[0, :, 4:5]
    keys = act_ref[0, :, INNER : INNER + STATE].astype(bf16)
    dstep_acc[...] = jnp.zeros_like(dstep_acc)
    dcol_acc[...] = jnp.zeros_like(dcol_acc)
    sent[...] = jnp.zeros_like(sent)
    keys_acc[...] = dbc_ref[0, :, :STATE]
    ends[...] = jnp.zeros_like(ends)

    @pl.loop(0, GROUPS)
    def _(g):
        step_front, leave_front = to_front(step, g), to_front(leave, g)
        products, columns, leaves = [], [], []
        group_through = mm_nt(keys, later_ref[0, at(g, WIDTH), :])
        for pair in range(GROUP // 2):
            here = pl.ds(pl.multiple_of(g * WIDTH + pair * LANES, LANES), LANES)
            later = later_ref[0, here, :]
            xs = act_ref[0, :, here]
            steps = spread(step_front, pair, low)
            leaving = spread(leave_front, pair, low)
            through = leaving * group_through[:, pair * LANES : (pair + 1) * LANES]
            dscaled = dx_ref[0, :, here] + through
            scaled = steps * xs
            rounded = scaled.astype(bf16).astype(f32)
            leaves.append((leaving * scaled).astype(bf16))
            products.append(xs * dscaled)
            columns.append(rounded * dscaled)
            sent[0:1, here] = jnp.sum(rounded * through, axis=0, keepdims=True)
            grad[:, here] = steps * dscaled + lanes_ref[1:2, here] * dy_ref[0, :, here].astype(f32)
            both = later.astype(f32) * kept_ref[0, here, :]
            at_row = GROUP * g + 2 * pair
            ends[pl.ds(at_row, 1), :] = jnp.sum(both[:HEADDIM], axis=0, keepdims=True)
            ends[pl.ds(at_row + 1, 1), :] = jnp.sum(both[HEADDIM:], axis=0, keepdims=True)
        keys_acc[...] += MM(jnp.concatenate(leaves, axis=1), later_ref[0, at(g, WIDTH), :])
        dstep_acc[...] += head_sums(jnp.concatenate(products, axis=1), g)
        dcol_acc[...] += head_sums(jnp.concatenate(columns, axis=1), g)

    grad[:, INNER : INNER + STATE] = keys_acc[...]
    grad[:, INNER + STATE :] = dbc_ref[0, :, STATE:] + q_ref[0]
    dstep = dstep_acc[...]
    at_end = jnp.sum(ends[...].T, axis=0, keepdims=True)
    for g in range(GROUPS):
        at_end = at_end + head_sums(sent[:, g * WIDTH : (g + 1) * WIDTH], g)[0:1]
    row = lax.broadcasted_iota(jnp.int32, (length, LANES), 0)
    ddecay = dq_ref[0] - dcol_acc[...] + jnp.where(row == length - 1, at_end, 0.0)
    onward = (
        lax.broadcasted_iota(jnp.int32, (length, length), 0)
        <= lax.broadcasted_iota(jnp.int32, (length, length), 1)
    ).astype(f32)
    drate = jnp.dot(onward, ddecay, precision=lax.Precision.HIGHEST, preferred_element_type=f32)
    speed = jnp.exp(heads_ref[1:2, :])
    raw = px_ref[:, CHANNELS : CHANNELS + HEADS].astype(f32) + heads_ref[0:1, :HEADS]
    draw = (dstep - drate * speed)[:, :HEADS] * sigmoid(raw)
    mine = pl.ds(pl.multiple_of(s * length, length), length)
    dpx_ref[mine, CHANNELS:] = jnp.concatenate(
        [draw, jnp.zeros((length, LANES - HEADS), f32)], axis=1
    ).astype(bf16)
    edges[s, :, CHANNELS:] = jnp.zeros((8, LANES), f32)
    dheads_ref[0] = jnp.zeros((8, LANES), f32)
    dheads_ref[0, 0:1, :HEADS] = jnp.sum(draw, axis=0, keepdims=True)
    dheads_ref[0, 1:2, :] = jnp.sum(drate * (-step * speed), axis=0, keepdims=True)

    masks = lane_masks(cols_ref, length)
    moved[...] = jnp.zeros_like(moved)
    dconv_ref[0] = jnp.zeros((8, CHANNELS), f32)

    @pl.loop(0, CHANNELS // LANES)
    def _(j):
        here = at(j, LANES)
        conv, inputs = taps(px_ref, tail_of(tail_ref, s, here), j, w_ref, b_ref, masks, ext)
        sg = sigmoid(conv)
        dconv = grad[:, here] * (sg * (1.0 + conv * (1.0 - sg)))
        for k in range(CONV):
            dconv_ref[0, k : k + 1, here] = jnp.sum(dconv * inputs[k], axis=0, keepdims=True)
        dconv_ref[0, CONV : CONV + 1, here] = jnp.sum(dconv, axis=0, keepdims=True)
        dx = w_ref[0:1, here] * dconv
        edge = jnp.zeros((8, LANES), f32)
        for k in range(1, CONV):
            moved[k - 1, 8 : 8 + length, :] = dconv * masks[k - 1]
            dx = dx + w_ref[k : k + 1, here] * moved[k - 1, 8 + k : 8 + k + length, :]
            edge = edge + w_ref[k : k + 1, here] * moved[k - 1, k : 8 + k, :]
        dpx_ref[mine, here] = dx.astype(bf16)
        edges[s, :, here] = edge

    @pl.when(s == pl.num_programs(0) - 1)
    def _():
        rows = edges.shape[0] * 8
        dpx_ref[dpx_ref.shape[0] - rows :, :] = edges[...].reshape(rows, edges.shape[2]).astype(bf16)


def whole(shape):
    return pl.BlockSpec(shape, lambda s: (0,) * len(shape))


def per_seq(*tail):
    return pl.BlockSpec((1,) + tail, lambda s: (s,) + (0,) * len(tail))


def per_rows(rows, width):
    return pl.BlockSpec((rows, width), lambda s: (s, 0))


def call(kernel, count, in_specs, outs, scratch, *args):
    return pl.pallas_call(
        kernel,
        grid=(count,),
        in_specs=in_specs,
        out_specs=[spec for spec, _unused in outs],
        out_shape=[jax.ShapeDtypeStruct(*made) for _unused, made in outs],
        scratch_shapes=scratch,
        compiler_params=pltpu.CompilerParams(vmem_limit_bytes=VMEM),
    )(*args)


def chain(own, factor, steps, beside):
    entered = jnp.zeros(own.shape, bf16)
    results = []
    for k, (source, target) in enumerate(steps):
        sent = own.astype(bf16) if k == 0 else (own + factor * entered.astype(f32)).astype(bf16)
        came = lax.ppermute(sent, "ctx", [(source, target)])
        for work in beside[k :: len(steps)]:
            results.append(work())
            came, results[-1] = lax.optimization_barrier((came, results[-1]))
        entered = came if k == 0 else entered + came
    return entered, results


def pad_lanes(v):
    return jnp.pad(v, (0, LANES - v.shape[0]))


def finish_kernel(lead, small_ref, dwz_ref, dpx_ref, normed_ref, dz_ref, wx_ref, wz_ref, x_ref, tail_ref, gain_ref, g_ref,
                  gn_ref, wo_ref, oz_ref, ox_ref, os_ref, og_ref, grad_ref, out_ref, *scratch):
    own_z, own, buffers, own_s, buffers_s = scratch[0], scratch[1], scratch[2:6], scratch[6], scratch[7:11]
    own_g, buffers_g = scratch[11], scratch[12:16]
    rows, wbuf, total, back, sem, semz, zsem, wsem, rsem, tail_sem, own_sem = scratch[16:]
    place_of = place()
    z, y, x, c = place_of
    meet(place_of, True)
    count = g_ref.shape[0]
    nz = dwz_ref.shape[-1] // CUT
    widths = [CUT] * nz + [
        min(CUT, dpx_ref.shape[1] - k) for k in range(0, dpx_ref.shape[1], CUT)
    ]
    small, gain = len(widths), len(widths) + 1

    def whole_own(i):
        return {small: own_s, gain: own_g}[i] if i >= small else cut_to(widths[i], own.at[i - nz])

    def own_of(i):
        if i < nz:
            return lambda zz, yy, xx: own_z[i % SLOTS, zz, yy, xx]
        ref = whole_own(i)
        return lambda zz, yy, xx: ref[zz, yy, xx, c]

    def source(i, core):
        if i < nz:
            return dwz_ref.at[:, :, :, core, :, pl.ds(i * CUT, CUT)]
        return whole_own(i).at[:, :, :, core]

    def result(i, value):
        if i >= small:
            {small: os_ref, gain: og_ref}[i][...] = value
        elif i < nz:
            oz_ref[:, i * CUT : (i + 1) * CUT] = value
        else:
            k = (i - nz) * CUT
            ox_ref[:, k : k + widths[i]] = value

    def buffers_of(i):
        if i >= small:
            return [v.at[0] for v in (buffers_s if i == small else buffers_g)]
        return [cut_to(widths[i], v.at[i]) for v in buffers]

    red = Reduction(place_of, source, own_of, buffers_of, result, sem, semz)

    def fetch(i):
        return pltpu.make_async_copy(
            dwz_ref.at[:, :, :, c, :, pl.ds(i * CUT, CUT)], own_z.at[i % SLOTS], zsem.at[i % SLOTS]
        )

    def arrive(i, stage):
        if stage == 0 and i < nz:
            fetch(i).wait()
        red.arrive(i, stage)
        if stage == 0 and i + SLOTS < nz:
            fetch(i + SLOTS).start()

    def weight_and_send(j):
        k, w = j * CUT, widths[nz + j]
        own_j = whole_own(nz + j)
        depth = normed_ref.shape[1] // NZ

        @pl.loop(0, NZ)
        def _(zz):
            value = mm_tn(normed_ref[:, at(zz, depth)], dpx_ref[:, k : k + w])
            own_j[zz] = value.astype(bf16).reshape(2, 2, 2, CUT_ROWS, w)

        red.send(nz + j, 0)

    chunks = [(wz_ref, rows, k, CUT) for k in range(0, wz_ref.shape[1], CUT)]
    chunks += [(wx_ref, dpx_ref, k * CUT, w) for k, w in enumerate(widths[nz:])]

    def stream(q):
        w_ref, _left, k, w = chunks[q]
        return pltpu.make_async_copy(
            w_ref.at[:, pl.ds(k, w)], wbuf.at[q % 2, :, pl.ds(0, w)], wsem.at[q % 2]
        )

    depth_out = wo_ref.shape[0] // 2
    outs = wo_ref.shape[1] // CUT

    def stream_out(q, half):
        return pltpu.make_async_copy(
            wo_ref.at[pl.ds(half * depth_out, depth_out), pl.ds(q * CUT, CUT)], wbuf.at[half],
            wsem.at[half],
        )

    def load_rows(source_ref):
        return pltpu.make_async_copy(source_ref, rows, rsem.at[0])

    def input_chunk(q):
        _w, left, k, w = chunks[q]
        if q == 0:
            load_rows(dz_ref).wait()
            total[...] = jnp.zeros_like(total)
        stream(q).wait()
        total[: left.shape[0]] += mm_nt(left[:, k : k + w], wbuf[q % 2, :, :w])
        if q + 2 < len(chunks):
            stream(q + 2).start()
        if q == nz - 1:
            load_rows(gn_ref).start()

    def output_chunk(q):
        here = slice(q * CUT, (q + 1) * CUT)
        if q == 0:
            load_rows(gn_ref).wait()
            for half in range(2):
                stream_out(q, half).start()
        value = x_ref[:, here].astype(f32)
        for half in range(2):
            stream_out(q, half).wait()
            value = value + MM(rows[:, half * depth_out : (half + 1) * depth_out], wbuf[half])
            if q + 1 < outs:
                stream_out(q + 1, half).start()
        out_ref[:, here] = value.astype(bf16)

    def tail_copy():
        return remote(
            total.at[pl.ds(count, 16)], back, tail_sem.at[0], tail_sem.at[1],
            {"seq": z * 2 + y, "ctx": lax.rem(x * 2 + c + 3, 4)},
        )

    def scaled_rows(rows_ref, lo, hi):
        v = rows_ref[lo:hi].astype(f32)
        return v, lax.rsqrt(jnp.mean(v * v, axis=1, keepdims=True) + EPSILON)

    def norm_weights():
        tail_copy().start()
        sums = jnp.zeros((normed_ref.shape[1], LANES), f32)
        ones = jnp.ones((LANES, LANES), bf16)
        for lo in range(0, count + 16, LANES):
            size = min(LANES, count + 16 - lo)
            v, r = scaled_rows(x_ref, lo, lo + LANES) if lo < count else scaled_rows(tail_ref, 0, 16)
            product = v * r * total[lo : lo + size]
            high = product.astype(bf16)
            rest = (product - high.astype(f32)).astype(bf16)
            sums = sums + mm_tn(high, ones[:size]) + mm_tn(rest, ones[:size])
        own_g[...] = sums.astype(bf16).reshape(own_g.shape)
        red.send(gain, 0)

    def norm_rows():
        tail_copy().wait()
        seqs = tail_ref.shape[0] // 8
        length = count // seqs
        for s in range(seqs):
            total[(s + 1) * length - 8 : (s + 1) * length] += back[8 * s : 8 * s + 8]
        for lo in range(0, count, LANES):
            v, r = scaled_rows(x_ref, lo, lo + LANES)
            scaled = gain_ref[0:1] * total[lo : lo + LANES]
            mean = jnp.mean(v * scaled, axis=1, keepdims=True)
            value = g_ref[lo : lo + LANES].astype(f32) + r * (scaled - v * (r * r) * mean)
            grad_ref[lo : lo + LANES] = value.astype(bf16)

    for i in range(nz):
        red.send(i, 0)
    for i in range(SLOTS):
        fetch(i).start()
    small_copy = pltpu.make_async_copy(small_ref, own_s, own_sem.at[0])
    small_copy.start()
    load_rows(dz_ref).start()
    for q in range(2):
        stream(q).start()
    order = [*range(gain + 1)]
    work = [[partial(weight_and_send, j)] for j in range(small - nz)]
    step = -(-len(chunks) // 5)
    work += [
        [partial(input_chunk, q) for q in range(k, min(k + step, len(chunks)))]
        for k in range(0, len(chunks), step)
    ]
    work += [[norm_weights], [norm_rows]] + [[partial(output_chunk, q)] for q in range(outs)]
    work[1] = work[1] + [small_copy.wait, partial(red.send, small, 0)]
    for t in range(max(len(order) + lead[-1], len(work))):
        for job in work[t] if t < len(work) else []:
            job()
        for stage in reversed(range(4)):
            if 0 <= t - lead[stage] < len(order):
                arrive(order[t - lead[stage]], stage)
    for i in order:
        red.drain(i)


def finish(small, dw_z, dpx, normed, dz, w_x, w_z, x, tail, gain, g, gn, w_out, lead=LEAD):
    small = small.reshape((NZ, 2, 2, 2, -1, small.shape[-1]))
    dw_z = dw_z.reshape((NZ, 2, 2, 2, -1, dw_z.shape[-1]))
    nx = pl.cdiv(dpx.shape[1], CUT)
    p = nx + dw_z.shape[-1] // CUT
    ss = small.shape[-2:]
    far, near = pl.BlockSpec(memory_space=pl.ANY), pl.BlockSpec(memory_space=pltpu.VMEM)
    return pl.pallas_call(
        partial(finish_kernel, tuple(lead)),
        out_shape=[
            jax.ShapeDtypeStruct((CUT_ROWS, dw_z.shape[-1]), f32),
            jax.ShapeDtypeStruct((CUT_ROWS, dpx.shape[1]), f32),
            jax.ShapeDtypeStruct(ss, f32),
            jax.ShapeDtypeStruct((CUT_ROWS, LANES), f32),
            jax.ShapeDtypeStruct(g.shape, bf16),
            jax.ShapeDtypeStruct(g.shape, bf16),
        ],
        in_specs=[far, far, near, near, far, far, far, near, near, near, near, far, far],
        out_specs=[near] * 6,
        scratch_shapes=[
            pltpu.VMEM((SLOTS, NZ, 2, 2, CUT_ROWS, CUT), bf16),
            pltpu.VMEM((nx, NZ, 2, 2, 2, CUT_ROWS, CUT), bf16),
        ]
        + reduction_buffers(p, (CUT_ROWS, CUT), bf16)
        + [pltpu.VMEM(small.shape, f32)] + reduction_buffers(1, ss, f32)
        + [pltpu.VMEM((NZ, 2, 2, 2, CUT_ROWS, LANES), bf16)]
        + reduction_buffers(1, (CUT_ROWS, LANES), bf16)
        + [
            pltpu.VMEM(dz.shape, bf16), pltpu.VMEM((2, w_x.shape[0], CUT), bf16),
            pltpu.VMEM(normed.shape, f32), pltpu.VMEM(tail.shape, f32),
        ]
        + reduction_semaphores(p + 2)
        + [pltpu.SemaphoreType.DMA((SLOTS,)), pltpu.SemaphoreType.DMA((2,)),
           pltpu.SemaphoreType.DMA((1,)), pltpu.SemaphoreType.DMA((2,)), pltpu.SemaphoreType.DMA((1,))],
        compiler_params=pltpu.CompilerParams(
            collective_id=1, has_side_effects=True, vmem_limit_bytes=FINISH_VMEM
        ),
    )(small, dw_z, dpx, normed, dz, w_x, w_z, x, tail, gain, g, gn, w_out)


def local(tokens, norm_gain, input_weight, conv_w, conv_b, dt_bias, a_log, d_skip, gate_gain,
          output_weight, segments, cotangent):
    seqs, length, width = tokens.shape
    n_ctx = lax.axis_size("ctx")
    n_all = n_ctx * lax.axis_size("seq")
    count = seqs * length
    shares = [norm_gain.shape[0], gate_gain.shape[0], CONV * conv_b.shape[0], conv_b.shape[0]]
    cuts = [sum(shares[: i + 1]) for i in range(3)]
    packed = jnp.concatenate([norm_gain, gate_gain, conv_w.reshape(-1), conv_b])
    onward = [(i, i + 1) for i in range(n_ctx - 1)]
    tail = jnp.pad(tokens[:, length - (CONV - 1) :], ((0, 0), (8 - (CONV - 1), 0), (0, 0)))
    tail_ids = jnp.pad(
        segments[:, length - (CONV - 1) :].astype(bf16), ((0, 0), (0, width - (CONV - 1)))
    )
    tail = jnp.concatenate([tail_ids[:, None], tail[:, 1:]], axis=1).reshape(seqs * 8, width)
    torus = lax.axis_size("seq") == 2 * NZ and n_ctx == 4 and norm_gain.shape[0] == CUT_ROWS
    spare = ((0, 0), (0, LANES - HEADS))
    w_z, w_x = input_weight[:, :INNER], jnp.pad(input_weight[:, INNER:], spare)
    if torus:
        size = packed.shape[0]
        small = jnp.pad(packed, (0, 16 * LANES - size)).reshape(16, LANES)
        w_out = lax.all_gather(output_weight, BOTH, axis=0, tiled=True)
        w_z = lax.all_gather(w_z, BOTH, axis=0, tiled=True)
        w_x, packed, tail = gather_all(
            [w_x, small], tail,
            [(1, 0, 16, True)]
            + [(0, 16 * k, 16, k % 2 == 0) for k in range(3)]
,
        )
        w_x, w_z, w_out = (w.reshape(-1, w.shape[-1]) for w in (w_x, w_z, w_out))
        packed = packed.reshape(n_all, -1)[:, :size]
    else:
        packed = lax.all_gather(packed, BOTH, axis=0)
        tail = lax.ppermute(tail, "ctx", onward)
        w_in, w_out = (
            lax.all_gather(w, BOTH, axis=0, tiled=True) for w in (input_weight, output_weight)
        )
        w_z, w_x = w_in[:, :INNER], jnp.pad(w_in[:, INNER:], spare)
    norm_full, gate_full, conv_w_full, conv_b_full = jnp.split(packed.astype(f32), cuts, axis=1)
    norm_full = norm_full.reshape(1, -1)
    gate_full = gate_full.reshape(1, -1)
    conv_b_full = conv_b_full.reshape(1, -1)
    conv_w_full = conv_w_full.reshape(n_all, CONV, -1).transpose(1, 0, 2).reshape(CONV, -1)

    tail = tail.reshape(seqs, 8, width)
    tail_ids = jnp.where(
        lax.axis_index("ctx") == 0, -1, tail[:, 0, : CONV - 1].astype(jnp.int32)
    )
    tail = jnp.pad(tail[:, 8 - (CONV - 1) :], ((0, 0), (8 - (CONV - 1), 0), (0, 0)))
    tail = jnp.where(lax.axis_index("ctx") == 0, 0, tail)
    tail = tail.reshape(seqs * 8, width)
    x_all = jnp.concatenate([tokens.reshape(count, width), tail])
    x_all = x_all.astype(f32)
    r_all = lax.rsqrt(jnp.mean(x_all * x_all, axis=-1, keepdims=True) + EPSILON)
    normed = (x_all * r_all * norm_full).astype(bf16)

    ids_ext = jnp.concatenate([tail_ids, segments], axis=1)
    flags = [
        segments == ids_ext[:, CONV - 1 - k : CONV - 1 - k + length] for k in range(1, CONV)
    ] + [segments == ids_ext[:, CONV - 2 : CONV - 1], segments == segments[:, -1:]]
    cols = jnp.stack([f.astype(f32) for f in flags] + [segments.astype(f32)], axis=-1)
    cols = jnp.pad(cols, ((0, 0), (0, 0), (0, LANES - cols.shape[-1])))
    rows = jnp.pad(segments.astype(f32)[:, None], ((0, 0), (0, 7), (0, 0)))
    heads = jnp.pad(jnp.stack([pad_lanes(dt_bias), pad_lanes(a_log)]), ((0, 6), (0, 0)))
    lanes = jnp.concatenate([gate_full, jnp.repeat(d_skip, HEADDIM)[None]])
    lanes = jnp.pad(lanes, ((0, 6), (0, 0)))
    conv_w8 = jnp.pad(conv_w_full, ((0, 8 - CONV), (0, 0)))
    conv_b8 = jnp.pad(conv_b_full, ((0, 7), (0, 0)))

    px = MM(normed, w_x).astype(bf16)
    px_width, used = CHANNELS + LANES, CHANNELS + HEADS
    tail_spec = pl.BlockSpec((16, px_width), lambda s: (count // 16, 0))
    act, tok, cst, fresh = call(
        before_kernel, seqs,
        [per_rows(length, px_width), tail_spec, whole((8, CHANNELS)), whole((8, CHANNELS)),
         per_seq(length, LANES), whole((8, LANES))],
        [(per_seq(length, CHANNELS), ((seqs, length, CHANNELS), f32)),
         (per_seq(length, 2 * LANES), ((seqs, length, 2 * LANES), f32)),
         (per_seq(HEADS, length), ((seqs, HEADS, length), f32)),
         (per_seq(INNER, STATE), ((seqs, INNER, STATE), f32))],
        [pltpu.VMEM((length + 8, LANES), f32)],
        px, px, conv_w8, conv_b8, cols, heads,
    )
    carried = cols[:, length - 1, 3]
    kept = jnp.exp(cst[:, :, length - 1]) * carried[:, None]
    kept = jnp.repeat(kept, HEADDIM, axis=1)[..., None]
    g2 = cotangent.reshape(count, width)

    def gate_gradient():
        return lax.dot_general(g2, w_out, (((1,), (1,)), ((), ())), preferred_element_type=f32)

    def within():
        [y] = call(
            within_kernel, seqs,
            [per_seq(length, CHANNELS), per_seq(length, 2 * LANES), per_seq(HEADS, length),
             per_seq(length, LANES), per_seq(8, length)],
            [(per_seq(length, INNER), ((seqs, length, INNER), f32))],
            [pltpu.VMEM((length, length), f32), pltpu.VMEM((length, length), f32)],
            act, tok, cst, cols, rows,
        )
        return y

    def gates():
        return MM(normed[:count], w_z).astype(bf16)

    entering, (dgn, y, pz) = chain(fresh, kept, onward, (gate_gradient, within, gates))
    stayed = kept * entering.astype(f32)
    gn, dz, dy, dstate, dqueries, ddecay, sums = call(
        gate_kernel, seqs,
        [per_rows(length, INNER), per_seq(length, CHANNELS), per_seq(length, 2 * LANES),
         per_seq(length, LANES), per_seq(length, INNER), per_seq(INNER, STATE),
         per_rows(length, INNER), whole((8, INNER))],
        [(per_rows(length, INNER), ((count, INNER), bf16)),
         (per_rows(length, INNER), ((count, INNER), bf16)),
         (per_seq(length, INNER), ((seqs, length, INNER), bf16)),
         (per_seq(INNER, STATE), ((seqs, INNER, STATE), f32)),
         (per_seq(length, STATE), ((seqs, length, STATE), f32)),
         (per_seq(length, LANES), ((seqs, length, LANES), f32)),
         (per_seq(8, INNER), ((seqs, 8, INNER), f32))],
        [pltpu.VMEM((length, INNER), f32), pltpu.VMEM((length, STATE), f32)],
        pz, act, tok, cols, y, entering, dgn, lanes,
    )
    tn = (((0,), (0,)), ((), ()))

    def output_weights():
        return lax.dot_general(gn, g2, tn, preferred_element_type=f32).astype(bf16)

    def scan_back():
        return call(
            scan_back_kernel, seqs,
            [per_seq(length, CHANNELS), per_seq(length, 2 * LANES), per_seq(HEADS, length),
             per_seq(length, LANES), per_seq(8, length), per_seq(length, INNER)],
            [(per_seq(length, INNER), ((seqs, length, INNER), f32)),
             (per_seq(length, 2 * STATE), ((seqs, length, 2 * STATE), f32))],
            [pltpu.VMEM((length, length), f32)] * 3,
            act, tok, cst, cols, rows, dy,
        )

    def gate_weights():
        return lax.dot_general(normed[:count], dz, tn, preferred_element_type=f32).astype(bf16)

    later, (dw_out, (dx, dbc), dw_z) = chain(
        dstate, kept, [(b, a) for a, b in reversed(onward)], (output_weights, scan_back, gate_weights)
    )
    dpx, dconv, dheads = call(
        after_kernel, seqs,
        [per_rows(length, px_width), tail_spec, whole((8, CHANNELS)), whole((8, CHANNELS)),
         per_seq(length, LANES), whole((8, LANES)), per_seq(length, CHANNELS),
         per_seq(length, 2 * LANES), whole((8, INNER)), per_seq(length, INNER),
         per_seq(length, INNER), per_seq(length, 2 * STATE), per_seq(length, STATE),
         per_seq(length, LANES), per_seq(INNER, STATE), per_seq(INNER, STATE)],
        [(whole((count + seqs * 8, px_width)), ((count + seqs * 8, px_width), bf16)),
         (per_seq(8, CHANNELS), ((seqs, 8, CHANNELS), f32)),
         (per_seq(8, LANES), ((seqs, 8, LANES), f32))],
        [pltpu.VMEM((length + 8, LANES), f32), pltpu.VMEM((CONV - 1, length + 16, LANES), f32),
         pltpu.VMEM((length, CHANNELS), f32), pltpu.VMEM((length, LANES), f32),
         pltpu.VMEM((length, LANES), f32), pltpu.VMEM((length, STATE), f32), pltpu.VMEM((LANES, LANES), f32),
         pltpu.VMEM((8, INNER), f32), pltpu.VMEM((seqs, 8, px_width), f32)],
        px, px, conv_w8, conv_b8, cols, heads, act, tok, lanes, dy, dx, dbc, dqueries, ddecay,
        later, stayed,
    )
    sums = jnp.sum(sums, axis=0)
    dconv = jnp.sum(dconv, axis=0)
    dheads = jnp.sum(dheads, axis=0)
    d_skip_sum = jnp.sum(sums[1].reshape(HEADS, HEADDIM), axis=1)
    split = [sums[0].reshape(n_all, -1),
             dconv[:CONV].reshape(CONV, n_all, -1).transpose(1, 0, 2).reshape(n_all, -1),
             dconv[CONV].reshape(n_all, -1)]
    shared = jnp.concatenate([dheads[0, :HEADS], dheads[1, :HEADS], d_skip_sum])
    split = jnp.concatenate(split, axis=1)
    share = split.shape[1]
    if torus:
        fill = 8 * LANES - share - shared.shape[0]
        split = [split, jnp.broadcast_to(shared, (n_all,) + shared.shape), jnp.zeros((n_all, fill), f32)]
        dw_z, dw_x, mine, d_norm, input_grad, output = finish(
            jnp.concatenate(split, axis=1).reshape(n_all, 8, LANES), dw_z, dpx, normed, dz,
            w_x, w_z, tokens.reshape(count, width), tail, jnp.pad(norm_full, ((0, 7), (0, 0))), g2,
            gn, w_out,
        )
        d_norm = d_norm[:, 0]
        dw_out = lax.psum_scatter(dw_out, BOTH, scatter_dimension=0, tiled=True).astype(f32)
        dw_in = jnp.concatenate([dw_z, dw_x[:, :used]], axis=1)
        mine = mine.reshape(-1)
        mine, shared = mine[:share], mine[share : share + shared.shape[0]]
    else:
        nt = (((1,), (1,)), ((), ()))
        dnormed_x = lax.dot_general(dpx, w_x, nt, preferred_element_type=f32)
        dnormed = dnormed_x[:count] + lax.dot_general(dz, w_z, nt, preferred_element_type=f32)
        back = dnormed_x[count:].reshape(seqs, 8, width)[:, 8 - (CONV - 1) :].astype(bf16)
        back = lax.ppermute(back, "ctx", [(b, a) for a, b in onward])
        dw_x = lax.dot_general(normed, dpx, tn, preferred_element_type=f32).astype(bf16)
        x, r = x_all[:count], r_all[:count]
        d_gain = jnp.sum(x * r * dnormed, axis=0) + jnp.sum(
            x_all[count:] * r_all[count:] * dnormed_x[count:], axis=0
        )
        back, d_gain, dw_x = lax.optimization_barrier((back, d_gain, dw_x))
        back = jnp.pad(back.astype(f32), ((0, 0), (length - (CONV - 1), 0), (0, 0)))
        scaled = norm_full * (dnormed + back.reshape(count, width))
        dx_in = r * (scaled - x * (r * r) * jnp.mean(x * scaled, axis=-1, keepdims=True))
        input_grad = (g2.astype(f32) + dx_in).astype(bf16)
        output = (x_all[:count] + MM(gn, w_out)).astype(bf16)
        dw_in = jnp.concatenate([dw_z, dw_x[:, :used]], axis=1)
        dw_out, dw_in = (
            lax.psum_scatter(v.astype(f32), BOTH, scatter_dimension=0, tiled=True)
            for v in (dw_out, dw_in)
        )
        every = lax.psum(jnp.concatenate([split.reshape(-1), shared, d_gain]), BOTH)
        me = lax.axis_index("seq") * n_ctx + lax.axis_index("ctx")
        d_norm = lax.dynamic_slice(every[-width:], (me * shares[0],), (shares[0],))
        mine = lax.dynamic_slice(every, (me * share,), (share,))
        shared = every[n_all * share : n_all * share + shared.shape[0]]
    d_gate, d_conv_w, d_conv_b = jnp.split(mine, [v - cuts[0] for v in cuts[1:]])
    d_bias, d_alog, d_skips = jnp.split(shared, 3)
    return (
        output.reshape(tokens.shape), input_grad.reshape(tokens.shape), d_norm, dw_in,
        d_conv_w.reshape(CONV, -1), d_conv_b, d_bias, d_alog, d_skips, d_gate, dw_out,
    )


def solution(mesh):
    split = P(BOTH)
    rows = P(BOTH, None)
    seq = P("seq", "ctx", None)
    in_specs = (seq, split, rows, P(None, BOTH), split, P(), P(), P(), split, rows,
                P("seq", "ctx"), seq)
    out_specs = (seq, seq, split, rows, P(None, BOTH), split, P(), P(), P(), split, rows)
    return jax.shard_map(local, mesh=mesh, in_specs=in_specs, out_specs=out_specs, check_vma=False)
```

time: 645 us -> 502 us (0.78)
  Pallas kernels: 428 us -> 343 us
  matrix products: 88.1 us -> 48 us
  waiting for transfers between devices: 39.3 us -> 15 us
  between operations: 1.72 us -> 14.6 us
  local copies, waits for them, and re-layouts: 34.6 us -> 26.2 us
    pallas_call x1, Pallas kernels: 143 us -> 90.8 us  [gather_all(): pl.pallas_call(partial(gather_kernel, tuple(units), n), out_shape=[jax.Sh...]
    dot_general x8 -> x4, matrix products: 76.6 us -> 36.5 us  [the longest x1 10 us: gate_gradient(): lax.dot_general(g2, w_out, (((1,), (1,)), ((), ())), preferred_element_ty...]
    ppermute x9 -> x6, waiting for transfers between devices: 39.3 us -> 4.16 us  [chain(): came = lax.ppermute(sent, 'ctx', [(source, target)])]
    pallas_call x1, Pallas kernels: 165 us -> 130 us  [finish(): pl.pallas_call(partial(finish_kernel, tuple(lead)), out_shape=[jax.ShapeD...]
    all_gather x0 -> x2, waiting for transfers between devices: none -> 10.2 us  [the longest x1 10.2 us: local(): w_z = lax.all_gather(w_z, BOTH, axis=0, tiled=True)]
    unnamed x69 -> x38, local copies, waits for them, and re-layouts: 15.6 us -> 6.99 us
    ppermute x9 -> x6, starting transfers between devices: 16.1 us -> 10.8 us  [chain(): came = lax.ppermute(sent, 'ctx', [(source, target)])]
    convert_element_type x9 -> x7, other arithmetic: 16.8 us -> 21.7 us  [the longest x4 13.2 us: chain(): (own + factor * entered.astype(f32)).astype(bf16)]
  transfers between devices with their start and end apart: 9 -> 9, of which waited for: 3 -> 2; matrix products, arithmetic and copies ran while one was open for 8% -> 20% of each run, Pallas kernels for 27% -> 63%
where the time goes in v4:
time: 502 us; the launch traced here: 494 us
  Pallas kernels  343 us (68%)
  matrix products  48 us (10%)
  other arithmetic  35.7 us (7%)
  local copies, waits for them, and re-layouts  26.2 us (5%)
  waiting for transfers between devices  15 us (3%)
  between operations  14.6 us (3%)
  starting transfers between devices  10.9 us (2%)
    pallas_call x1, Pallas kernels, finish(): pl.pallas_call(partial(finish_kernel, tuple(lead)), out_shape=[jax.ShapeD...  130 us
    pallas_call x5, Pallas kernels, call(): pl.pallas_call(kernel, grid=(count,), in_specs=in_specs, out_specs=[spec...  122 us
    pallas_call x1, Pallas kernels, gather_all(): pl.pallas_call(partial(gather_kernel, tuple(units), n), out_shape=[jax.Sh...  90.8 us
    convert_element_type x4, other arithmetic, chain(): (own + factor * entered.astype(f32)).astype(bf16)  13.2 us
    dot_general x1, matrix products, local(): px = MM(normed, w_x).astype(bf16)  11.5 us
    ppermute x6, starting transfers between devices, chain(): came = lax.ppermute(sent, 'ctx', [(source, target)])  10.8 us
    all_gather x1, waiting for transfers between devices, local(): w_z = lax.all_gather(w_z, BOTH, axis=0, tiled=True)  10.2 us
  transfers between devices with their start and end apart: 9, of which 2 were waited for; matrix products, arithmetic and copies ran while one was open for 20% of the time, Pallas kernels for 63%

profile of v4, /device:TPU:0, one launch (start us, length us, event | category | flops | bytes accessed | tf_op | source)
XLA Modules:
  0.0 493.5 jit_solution(14926262749806615014)
XLA Ops:
  15.9 90.8 %shard_map.203 = (bf16[4,2,2,2,48,3456]{5,4,3,2,1,0:T(8,128)(2,1)}, bf16[4,2,2,2,16,128]{5,4,3,2,1,0:T(8,128)(2,1)}, bf16[16,1536]{1,0:T(8,128)(2,1)}) custom-call(bf16[48,3456]{1,0:T(8,128)(2,1)} %pad.54.refs_0_, bf16[16,128]{1,0:T(8,128)(2,1)} %fusion.12.refs_1_, bf16[16,1536]{1,0:T(8,128)(2,1)} %maximum_bitcast_fusion.refs_2_), custom_call_target="tpu_custom_call" | custom-call | tf_op jit(solution)/shard_map/pallas_call | solution.py:244
  115.4 11.5 %convolution_convert_fusion.2.px_ref.tail_ref = bf16[528,3456]{1,0:T(8,128)(2,1)} fusion(bf16[528,1536]{1,0:T(8,128)(2,1)S(1)} %fusion.2.normed_ref, bf16[1536,3456]{1,0:T(8,128)(2,1)} %bitcast.69), kind=kOutput, calls=%fused_computation.2 | convolution fusion | flops 5607512064 | bytes 15888384 | tf_op jit(solution)/shard_map/dot_general | solution.py:994
  126.9 19.5 %shard_map.204 = (f32[2,256,3328]{2,1,0:T(8,128)}, f32[2,256,256]{2,1,0:T(8,128)}, f32[2,48,256]{2,1,0:T(8,128)}, f32[2,3072,128]{2,1,0:T(8,128)}) custom-call(bf16[528,3456]{1,0:T(8,128)(2,1)} %convolution_convert_fusion.2.px_ref.tail_ref, bf16[528,3456]{1,0:T(8,128)(2,1)} %convolution_convert_fusion.2.px_ref.tail_ref, f32[8,3328]{1,0:T(8,128)} %pad.59.w_ref, ...), custom_call_target="tpu_custom_call" | custom-call | tf_op jit(solution)/shard_map/pallas_call | solution.py:676
  146.5 3.3 convert_element_type.105
  149.7 2.7 collective-permute-start
  153.0 10.0 %fusion.20.dgn_ref = f32[512,3072]{1,0:T(8,128)} fusion(bf16[512,1536]{1,0:T(8,128)(2,1)} %bitcast.72, bf16[3072,1536]{1,0:T(8,128)(2,1)} %all-gather.3.cloned.1.call-done.wo_ref), kind=kOutput, calls=%fused_computation.78 | convolution fusion | flops 4831838208 | bytes 17301504 | tf_op jit(solution)/shard_map/dot_general | solution.py:1014
  163.1 3.0 add_convert_fusion.3
  166.1 1.9 collective-permute-start.1
  168.6 15.2 %shard_map.205.y_ref = f32[2,256,3072]{2,1,0:T(8,128)} custom-call(f32[2,256,3328]{2,1,0:T(8,128)} %get-tuple-element.55.act_ref, f32[2,256,256]{2,1,0:T(8,128)} %get-tuple-element.56.tok_ref, f32[2,48,256]{2,1,0:T(8,128)} %get-tuple-element.53.cst_ref, f32[2,256,128]{2,1,0:T(8,128)} %pad.61.cols_ref, f32[2,8,256]{2,1,0:T(8,128)} %pad.65.rows_ref), custom_call_target="tpu_custom_call" | custom-call | tf_op jit(solution)/shard_map/pallas_call | solution.py:676
  183.8 3.5 add_convert_fusion.2
  189.6 10.2 %all-gather.5.cloned.1.call-done.wz_ref = bf16[1536,3072]{1,0:T(8,128)(2,1)} async-done(((bf16[48,3072]{1,0:T(8,128)(2,1)}), bf16[1536,3072]{1,0:T(8,128)(2,1)}) %all-gather.5.cloned.1.call-update) | async-done | bytes 9437200 | tf_op jit(solution)/shard_map/all_gather | solution.py:947
  199.7 9.2 %convolution_convert_fusion.3.z_ref = bf16[512,3072]{1,0:T(8,128)(2,1)} fusion(bf16[1536,3072]{1,0:T(8,128)(2,1)} %all-gather.5.cloned.1.call-done.wz_ref, bf16[528,1536]{1,0:T(8,128)(2,1)} %copy-done.3), kind=kOutput, calls=%fused_computation.3 | convolution fusion | flops 4833411072 | bytes 14155776 | tf_op jit(solution)/shard_map/dot_general | solution.py:1028
  208.9 2.7 convert_multiply_fusion.2
  211.6 31.3 %shard_map.206 = (bf16[512,3072]{1,0:T(8,128)(2,1)}, bf16[512,3072]{1,0:T(8,128)(2,1)}, bf16[2,256,3072]{2,1,0:T(8,128)(2,1)}, f32[2,3072,128]{2,1,0:T(8,128)}, ...) custom-call(bf16[512,3072]{1,0:T(8,128)(2,1)} %convolution_convert_fusion.3.z_ref, ...), custom_call_target="tpu_custom_call" | custom-call | tf_op jit(solution)/shard_map/pallas_call | solution.py:676
  243.0 3.4 convert_element_type.111
  248.2 7.5 %convolution_convert_fusion.1 = bf16[3072,1536]{1,0:T(8,128)(2,1)} fusion(bf16[512,3072]{1,0:T(8,128)(2,1)S(1)} %copy-done.6, bf16[512,1536]{1,0:T(8,128)(2,1)S(1)} %bitcast.74), kind=kOutput, calls=%fused_computation.1 | convolution fusion | flops 4836556800 | bytes 14155776 | tf_op jit(solution)/shard_map/dot_general | solution.py:1050
  257.6 3.0 add_convert_fusion.1
  262.4 17.0 %shard_map.207 = (f32[2,256,3072]{2,1,0:T(8,128)}, f32[2,256,256]{2,1,0:T(8,128)}) custom-call(f32[2,256,3328]{2,1,0:T(8,128)} %get-tuple-element.55.act_ref, f32[2,256,256]{2,1,0:T(8,128)} %get-tuple-element.56.tok_ref, f32[2,48,256]{2,1,0:T(8,128)} %get-tuple-element.53.cst_ref, f32[2,256,128]{2,1,0:T(8,128)} %pad.61.cols_ref, f32[2,8,256]{2,1,0:T(8,128)} %pad.65.rows_ref, ...), custom_call_target="tpu_custom_call" | custom-call | tf_op jit(solution)/shard_map/pallas_call | solution.py:676
  279.4 3.7 add_convert_fusion
  285.6 9.8 %convolution_convert_fusion = bf16[1536,3072]{1,0:T(8,128)(2,1)} fusion(bf16[512,3072]{1,0:T(8,128)(2,1)} %get-tuple-element.74.dz_ref, bf16[528,1536]{1,0:T(8,128)(2,1)} %copy-done.3), kind=kOutput, calls=%fused_computation | convolution fusion | flops 4836556800 | bytes 14155776 | tf_op jit(solution)/shard_map/dot_general | solution.py:1064
  295.3 4.1 collective-permute-done.5
  301.0 39.0 %shard_map.208 = (bf16[528,3456]{1,0:T(8,128)(2,1)}, f32[2,8,3328]{2,1,0:T(8,128)}, f32[2,8,128]{2,1,0:T(8,128)}) custom-call(bf16[528,3456]{1,0:T(8,128)(2,1)} %convolution_convert_fusion.2.px_ref.tail_ref, bf16[528,3456]{1,0:T(8,128)(2,1)} %convolution_convert_fusion.2.px_ref.tail_ref, f32[8,3328]{1,0:T(8,128)} %pad.59.w_ref, f32[8,3328]{1,0:T(8,128)} %pad.60.b_ref, ...), custom_call_target="tpu_custom_call" | custom-call | tf_op jit(solution)/shard_map/pallas_call | solution.py:676
  343.1 130.2 %shard_map.209 = (f32[48,3072]{1,0:T(8,128)}, f32[48,3456]{1,0:T(8,128)}, f32[8,128]{1,0:T(8,128)}, f32[48,128]{1,0:T(8,128)}, bf16[512,1536]{1,0:T(8,128)(2,1)}, /*index=5*/bf16[512,1536]{1,0:T(8,128)(2,1)}) custom-call(f32[4,2,2,2,8,128]{5,4,3,2,1,0:T(8,128)} %bitcast.78, bf16[4,2,2,2,48,3072]{5,4,3,2,1,0:T(8,128)(2,1)} %bitcast.71, ...), custom_call_target="tpu_custom_call" | custom-call | tf_op jit(solution)/shard_map/pallas_call | solution.py:892
  479.9 2.5 pad_maximum_fusion.1
  (137 shorter events, 44.0 us)
Async XLA Ops:
  7.2 103.9 %copy-start.13 = (s32[2,256]{1,0:T(2,128)S(1)}, s32[2,256]{1,0:T(2,128)}, u32[]{:S(2)}) copy-start(s32[2,256]{1,0:T(2,128)} %param.22) | copy-start | bytes 6148
  7.2 105.6 %copy-start.2 = (bf16[2,256,1536]{2,1,0:T(8,128)(2,1)S(1)}, bf16[2,256,1536]{2,1,0:T(8,128)(2,1)}, u32[]{:S(2)}) copy-start(bf16[2,256,1536]{2,1,0:T(8,128)(2,1)} %param.12) | copy-start | bytes 4718596
  7.2 145.8 %all-gather.3.cloned.1.call-start = ((), (), s32[]{:S(2)}) async-start(), calls=%async_computation.1 | async-start | bytes 9732096 | tf_op jit(solution)/shard_map/all_gather | solution.py:946
  7.9 191.8 %all-gather.5.cloned.1.call-start = ((), (), s32[]{:S(2)}) async-start(), calls=%async_computation.2 | async-start | bytes 9732096 | tf_op jit(solution)/shard_map/all_gather | solution.py:947
  9.7 103.5 %copy-start.15 = (f32[48]{0:T(128)S(1)}, f32[48]{0:T(128)}, u32[]{:S(2)}) copy-start(f32[48]{0:T(128)} %param.18) | copy-start | bytes 580
  9.7 103.5 %copy-start.16 = (f32[48]{0:T(128)S(1)}, f32[48]{0:T(128)}, u32[]{:S(2)}) copy-start(f32[48]{0:T(128)} %param.17) | copy-start | bytes 580
  9.7 472.7 %reduce-scatter.2.cloned.1.call-start = ((), (), s32[]{:S(2)}) async-start(), calls=%async_computation.3 | async-start | bytes 9732096 | tf_op jit(solution)/shard_map/reduce_scatter | solution.py:1105
  112.8 14.1 %copy-start.10 = (bf16[16,1536]{1,0:T(8,128)(2,1)}, bf16[16,1536]{1,0:T(8,128)(2,1)S(1)}, u32[]{:S(2)}) copy-start(bf16[16,1536]{1,0:T(8,128)(2,1)S(1)} %select_bitcast_fusion.tail_ref) | copy-start | bytes 147460
  146.4 6.1 %copy-start.11 = (f32[2,48,256]{2,1,0:T(8,128)S(1)}, f32[2,48,256]{2,1,0:T(8,128)}, u32[]{:S(2)}) copy-start(f32[2,48,256]{2,1,0:T(8,128)} %get-tuple-element.53.cst_ref) | copy-start | bytes 294916
  149.7 13.4 %collective-permute-start = (bf16[2,3072,128]{2,1,0:T(8,128)(2,1)}, bf16[2,3072,128]{2,1,0:T(8,128)(2,1)}, u32[]{:S(2)}, u32[]{:S(2)}) collective-permute-start(bf16[2,3072,128]{2,1,0:T(8,128)(2,1)} %convert_element_type.105), channel_id=1, source_target_pairs={{0,1},{4,5},{8,9},{12,13},{16,17},{20,21},{24,25},{28,29}} | collective-permute-start | bytes 4718600 | tf_op jit(solution)/shard_map/ppermute | solution.py:692
  153.0 10.1 %copy-start.1 = (f32[2,3072,128]{2,1,0:T(8,128)S(1)}, f32[2,3072,128]{2,1,0:T(8,128)}, u32[]{:S(2)}) copy-start(f32[2,3072,128]{2,1,0:T(8,128)} %get-tuple-element.52) | copy-start | bytes 9437188
  166.1 17.7 %collective-permute-start.1 = (bf16[2,3072,128]{2,1,0:T(8,128)(2,1)}, bf16[2,3072,128]{2,1,0:T(8,128)(2,1)}, u32[]{:S(2)}, u32[]{:S(2)}) collective-permute-start(bf16[2,3072,128]{2,1,0:T(8,128)(2,1)} %add_convert_fusion.3), channel_id=1, source_target_pairs={{1,2},{5,6},{9,10},{13,14},{17,18},{21,22},{25,26},{29,30}} | collective-permute-start | bytes 4718600 | tf_op jit(solution)/shard_map/ppermute | solution.py:692
  183.8 4.8 copy-start.14
  187.3 21.6 %collective-permute-start.2 = (bf16[2,3072,128]{2,1,0:T(8,128)(2,1)}, bf16[2,3072,128]{2,1,0:T(8,128)(2,1)S(1)}, u32[]{:S(2)}, u32[]{:S(2)}) collective-permute-start(bf16[2,3072,128]{2,1,0:T(8,128)(2,1)} %get-tuple-element.93), channel_id=1, source_target_pairs={{2,3},{6,7},{10,11},{14,15},{18,19},{22,23},{26,27},{30,31}} | collective-permute-start | bytes 4718600 | tf_op jit(solution)/shard_map/ppermute | solution.py:692
  189.6 19.4 %copy-start.5 = (bf16[2,3072,128]{2,1,0:T(8,128)(2,1)S(1)}, bf16[2,3072,128]{2,1,0:T(8,128)(2,1)}, u32[]{:S(2)}) copy-start(bf16[2,3072,128]{2,1,0:T(8,128)(2,1)} %get-tuple-element.94) | copy-start | bytes 4718596
  243.0 5.2 %copy-start.6 = (bf16[512,3072]{1,0:T(8,128)(2,1)S(1)}, bf16[512,3072]{1,0:T(8,128)(2,1)}, u32[]{:S(2)}) copy-start(bf16[512,3072]{1,0:T(8,128)(2,1)} %get-tuple-element.65.gn_ref) | copy-start | bytes 9437188
  243.0 5.2 %copy-start.7 = (bf16[2,256,1536]{2,1,0:T(8,128)(2,1)S(1)}, bf16[2,256,1536]{2,1,0:T(8,128)(2,1)}, u32[]{:S(2)}) copy-start(bf16[2,256,1536]{2,1,0:T(8,128)(2,1)} %param.23) | copy-start | bytes 4718596
  246.4 9.4 %collective-permute-start.3 = (bf16[2,3072,128]{2,1,0:T(8,128)(2,1)}, bf16[2,3072,128]{2,1,0:T(8,128)(2,1)}, u32[]{:S(2)}, u32[]{:S(2)}) collective-permute-start(bf16[2,3072,128]{2,1,0:T(8,128)(2,1)} %convert_element_type.111), channel_id=1, source_target_pairs={{3,2},{7,6},{11,10},{15,14},{19,18},{23,22},{27,26},{31,30}} | collective-permute-start | bytes 4718600 | tf_op jit(solution)/shard_map/ppermute | solution.py:692
  260.6 18.8 %collective-permute-start.4 = (bf16[2,3072,128]{2,1,0:T(8,128)(2,1)}, bf16[2,3072,128]{2,1,0:T(8,128)(2,1)}, u32[]{:S(2)}, u32[]{:S(2)}) collective-permute-start(bf16[2,3072,128]{2,1,0:T(8,128)(2,1)} %add_convert_fusion.1), channel_id=1, source_target_pairs={{2,1},{6,5},{10,9},{14,13},{18,17},{22,21},{26,25},{30,29}} | collective-permute-start | bytes 4718600 | tf_op jit(solution)/shard_map/ppermute | solution.py:692
  279.4 5.9 %copy-start.12 = (f32[2,8,3072]{2,1,0:T(8,128)S(1)}, f32[2,8,3072]{2,1,0:T(8,128)}, u32[]{:S(2)}) copy-start(f32[2,8,3072]{2,1,0:T(8,128)} %get-tuple-element.62) | copy-start | bytes 589828
  283.1 16.4 %collective-permute-start.5 = (bf16[2,3072,128]{2,1,0:T(8,128)(2,1)}, bf16[2,3072,128]{2,1,0:T(8,128)(2,1)S(1)}, u32[]{:S(2)}, u32[]{:S(2)}) collective-permute-start(bf16[2,3072,128]{2,1,0:T(8,128)(2,1)} %get-tuple-element.91), channel_id=1, source_target_pairs={{1,0},{5,4},{9,8},{13,12},{17,16},{21,20},{25,24},{29,28}} | collective-permute-start | bytes 4718600 | tf_op jit(solution)/shard_map/ppermute | solution.py:692
  285.6 13.9 %copy-start.4 = (bf16[2,3072,128]{2,1,0:T(8,128)(2,1)S(1)}, bf16[2,3072,128]{2,1,0:T(8,128)(2,1)}, u32[]{:S(2)}) copy-start(bf16[2,3072,128]{2,1,0:T(8,128)(2,1)} %get-tuple-element.92) | copy-start | bytes 4718596
  473.2 11.0 %copy-start.9 = (bf16[512,1536]{1,0:T(8,128)(2,1)S(1)}, bf16[512,1536]{1,0:T(8,128)(2,1)}, u32[]{:S(2)}) copy-start(bf16[512,1536]{1,0:T(8,128)(2,1)} %get-tuple-element.80) | copy-start | bytes 4718596
  479.9 5.5 %copy-start.8 = (bf16[512,1536]{1,0:T(8,128)(2,1)S(1)}, bf16[512,1536]{1,0:T(8,128)(2,1)}, u32[]{:S(2)}) copy-start(bf16[512,1536]{1,0:T(8,128)(2,1)} %get-tuple-element.81) | copy-start | bytes 4718596
  (2 other events, 3.1 us)
Sparse Core Ops, SparseCore 0:
  10.9 102.9 all-gather.2
  117.4 82.2 all-gather.4
  255.9 156.8 reduce-scatter.1

commit v5 on v4

--- a/solution.py
+++ b/solution.py
@@ -415,7 +415,8 @@
         for pair in range(GROUP // 2):
             here = pl.ds(pl.multiple_of(g * WIDTH + pair * LANES, LANES), LANES)
             scaled.append((act_ref[0, :, here] * spread(front, pair, low)).astype(bf16))
-        fresh_ref[0, at(g, WIDTH), :] = mm_tn(jnp.concatenate(scaled, axis=1), keys)
+        left = mm_tn(jnp.concatenate(scaled, axis=1), keys)
+        fresh_ref[0, at(g, WIDTH), :] = left.astype(bf16)
 
 
 def bias_of(ids_col, ids_row, transposed):
@@ -477,7 +478,7 @@
             z = z_ref[:, here].astype(f32)
             gated = y * (z * sigmoid(z))
             square = square + gated * gated
-            inner = inner + lanes_ref[0:1, here] * dgn_ref[:, here] * gated
+            inner = inner + lanes_ref[0:1, here] * dgn_ref[:, here].astype(f32) * gated
         return square, inner
 
     zero = jnp.zeros((length, LANES), f32)
@@ -503,7 +504,7 @@
             gate = z * sg
             gated = y * gate
             gain = lanes_ref[0:1, here]
-            dgn = dgn_ref[:, here]
+            dgn = dgn_ref[:, here].astype(f32)
             gn = gated * scale
             gn_ref[:, here] = (gn * gain).astype(bf16)
             dgated = scale * (gain * dgn) - gated * back
@@ -517,7 +518,7 @@
             entered.append((rounded * spread(front, pair, low)).astype(bf16))
             products.append(rounded * inside)
         entered = jnp.concatenate(entered, axis=1)
-        dstate_ref[0, at(g, WIDTH), :] = mm_tn(entered, queries)
+        dstate_ref[0, at(g, WIDTH), :] = mm_tn(entered, queries).astype(bf16)
         queries_acc[...] += MM(entered, state_ref[0, at(g, WIDTH), :])
         dq_ref[0] += head_sums(jnp.concatenate(products, axis=1), g)
 
@@ -564,7 +565,7 @@
 
 
 def after_kernel(px_ref, tail_ref, w_ref, b_ref, cols_ref, heads_ref, act_ref, tok_ref, lanes_ref,
-                 dy_ref, dx_ref, dbc_ref, q_ref, dq_ref, later_ref, kept_ref,
+                 dy_ref, dx_ref, dbc_ref, q_ref, dq_ref, later_ref, state_ref,
                  dpx_ref, dconv_ref, dheads_ref, ext, moved, grad, dstep_acc, dcol_acc, keys_acc, ends, sent, edges):
     s = pl.program_id(0)
     length = act_ref.shape[1]
@@ -599,7 +600,7 @@
             columns.append(rounded * dscaled)
             sent[0:1, here] = jnp.sum(rounded * through, axis=0, keepdims=True)
             grad[:, here] = steps * dscaled + lanes_ref[1:2, here] * dy_ref[0, :, here].astype(f32)
-            both = later.astype(f32) * kept_ref[0, here, :]
+            both = later.astype(f32) * state_ref[0, here, :].astype(f32)
             at_row = GROUP * g + 2 * pair
             ends[pl.ds(at_row, 1), :] = jnp.sum(both[:HEADDIM], axis=0, keepdims=True)
             ends[pl.ds(at_row + 1, 1), :] = jnp.sum(both[HEADDIM:], axis=0, keepdims=True)
@@ -610,7 +611,8 @@
     grad[:, INNER : INNER + STATE] = keys_acc[...]
     grad[:, INNER + STATE :] = dbc_ref[0, :, STATE:] + q_ref[0]
     dstep = dstep_acc[...]
-    at_end = jnp.sum(ends[...].T, axis=0, keepdims=True)
+    kept = jnp.exp(decay[length - 1 : length]) * cols_ref[0, length - 1 : length, 3:4]
+    at_end = kept * jnp.sum(ends[...].T, axis=0, keepdims=True)
     for g in range(GROUPS):
         at_end = at_end + head_sums(sent[:, g * WIDTH : (g + 1) * WIDTH], g)[0:1]
     row = lax.broadcasted_iota(jnp.int32, (length, LANES), 0)
@@ -688,7 +690,7 @@
     entered = jnp.zeros(own.shape, bf16)
     results = []
     for k, (source, target) in enumerate(steps):
-        sent = own.astype(bf16) if k == 0 else (own + factor * entered.astype(f32)).astype(bf16)
+        sent = own if k == 0 else (own.astype(f32) + factor * entered.astype(f32)).astype(bf16)
         came = lax.ppermute(sent, "ctx", [(source, target)])
         for work in beside[k :: len(steps)]:
             results.append(work())
@@ -1001,7 +1003,7 @@
         [(per_seq(length, CHANNELS), ((seqs, length, CHANNELS), f32)),
          (per_seq(length, 2 * LANES), ((seqs, length, 2 * LANES), f32)),
          (per_seq(HEADS, length), ((seqs, HEADS, length), f32)),
-         (per_seq(INNER, STATE), ((seqs, INNER, STATE), f32))],
+         (per_seq(INNER, STATE), ((seqs, INNER, STATE), bf16))],
         [pltpu.VMEM((length + 8, LANES), f32)],
         px, px, conv_w8, conv_b8, cols, heads,
     )
@@ -1011,7 +1013,8 @@
     g2 = cotangent.reshape(count, width)
 
     def gate_gradient():
-        return lax.dot_general(g2, w_out, (((1,), (1,)), ((), ())), preferred_element_type=f32)
+        dims = (((1,), (1,)), ((), ()))
+        return lax.dot_general(g2, w_out, dims, preferred_element_type=f32).astype(bf16)
 
     def within():
         [y] = call(
@@ -1028,7 +1031,6 @@
         return MM(normed[:count], w_z).astype(bf16)
 
     entering, (dgn, y, pz) = chain(fresh, kept, onward, (gate_gradient, within, gates))
-    stayed = kept * entering.astype(f32)
     gn, dz, dy, dstate, dqueries, ddecay, sums = call(
         gate_kernel, seqs,
         [per_rows(length, INNER), per_seq(length, CHANNELS), per_seq(length, 2 * LANES),
@@ -1037,7 +1039,7 @@
         [(per_rows(length, INNER), ((count, INNER), bf16)),
          (per_rows(length, INNER), ((count, INNER), bf16)),
          (per_seq(length, INNER), ((seqs, length, INNER), bf16)),
-         (per_seq(INNER, STATE), ((seqs, INNER, STATE), f32)),
+         (per_seq(INNER, STATE), ((seqs, INNER, STATE), bf16)),
          (per_seq(length, STATE), ((seqs, length, STATE), f32)),
          (per_seq(length, LANES), ((seqs, length, LANES), f32)),
          (per_seq(8, INNER), ((seqs, 8, INNER), f32))],
@@ -1081,7 +1083,7 @@
          pltpu.VMEM((length, LANES), f32), pltpu.VMEM((length, STATE), f32), pltpu.VMEM((LANES, LANES), f32),
          pltpu.VMEM((8, INNER), f32), pltpu.VMEM((seqs, 8, px_width), f32)],
         px, px, conv_w8, conv_b8, cols, heads, act, tok, lanes, dy, dx, dbc, dqueries, ddecay,
-        later, stayed,
+        later, entering,
     )
     sums = jnp.sum(sums, axis=0)
     dconv = jnp.sum(dconv, axis=0)

time: 502 us -> 499 us (level)
  other arithmetic: 35.7 us -> 29.3 us
    convert_element_type x6 -> x4, other arithmetic: 19.8 us -> 13.2 us  [chain(): (own.astype(f32) + factor * entered.astype(f32)).astype(bf16)]
  transfers between devices with their start and end apart: 9 -> 9, of which waited for: 2 -> 2; matrix products, arithmetic and copies ran while one was open for 20% -> 20% of each run, Pallas kernels for 63% -> 64%
where the time goes in v5:
time: 499 us; the launch traced here: 490 us
  Pallas kernels  343 us (69%)
  matrix products  51.1 us (10%)
  other arithmetic  29.3 us (6%)
  local copies, waits for them, and re-layouts  25.4 us (5%)
  waiting for transfers between devices  15.1 us (3%)
  between operations  14.5 us (3%)
  starting transfers between devices  11.8 us (2%)
    pallas_call x1, Pallas kernels, finish(): pl.pallas_call(partial(finish_kernel, tuple(lead)), out_shape=[jax.ShapeD...  131 us
    pallas_call x5, Pallas kernels, call(): pl.pallas_call(kernel, grid=(count,), in_specs=in_specs, out_specs=[spec...  121 us
    pallas_call x1, Pallas kernels, gather_all(): pl.pallas_call(partial(gather_kernel, tuple(units), n), out_shape=[jax.Sh...  90.8 us
    all_gather x1, waiting for transfers between devices, local(): w_z = lax.all_gather(w_z, BOTH, axis=0, tiled=True)  13.4 us
    convert_element_type x4, other arithmetic, chain(): (own.astype(f32) + factor * entered.astype(f32)).astype(bf16)  13.2 us
    dot_general x1, matrix products, local(): px = MM(normed, w_x).astype(bf16)  12.1 us
    ppermute x6, starting transfers between devices, chain(): came = lax.ppermute(sent, 'ctx', [(source, target)])  11.7 us
    dot_general x1, matrix products, gates(): return MM(normed[:count], w_z).astype(bf16)  10 us
  transfers between devices with their start and end apart: 9, of which 2 were waited for; matrix products, arithmetic and copies ran while one was open for 20% of the time, Pallas kernels for 64%

profile of v5, /device:TPU:0, one launch (start us, length us, event | category | flops | bytes accessed | tf_op | source)
XLA Modules:
  0.0 489.9 jit_solution(16961478023566198443)
XLA Ops:
  15.9 90.8 %shard_map.203 = (bf16[4,2,2,2,48,3456]{5,4,3,2,1,0:T(8,128)(2,1)}, bf16[4,2,2,2,16,128]{5,4,3,2,1,0:T(8,128)(2,1)}, bf16[16,1536]{1,0:T(8,128)(2,1)}) custom-call(bf16[48,3456]{1,0:T(8,128)(2,1)} %pad.54.refs_0_, bf16[16,128]{1,0:T(8,128)(2,1)} %fusion.16.refs_1_, bf16[16,1536]{1,0:T(8,128)(2,1)} %maximum_bitcast_fusion.refs_2_), custom_call_target="tpu_custom_call" | custom-call | tf_op jit(solution)/shard_map/pallas_call | solution.py:244
  114.3 12.1 %convolution_convert_fusion.2.px_ref.tail_ref = bf16[528,3456]{1,0:T(8,128)(2,1)} fusion(bf16[528,1536]{1,0:T(8,128)(2,1)S(1)} %fusion.2.normed_ref, bf16[1536,3456]{1,0:T(8,128)(2,1)} %bitcast.69), kind=kOutput, calls=%fused_computation.2 | convolution fusion | flops 5607512064 | bytes 15888384 | tf_op jit(solution)/shard_map/dot_general | solution.py:996
  126.4 19.4 %shard_map.204 = (f32[2,256,3328]{2,1,0:T(8,128)}, f32[2,256,256]{2,1,0:T(8,128)}, f32[2,48,256]{2,1,0:T(8,128)}, bf16[2,3072,128]{2,1,0:T(8,128)(2,1)}) custom-call(bf16[528,3456]{1,0:T(8,128)(2,1)} %convolution_convert_fusion.2.px_ref.tail_ref, bf16[528,3456]{1,0:T(8,128)(2,1)} %convolution_convert_fusion.2.px_ref.tail_ref, f32[8,3328]{1,0:T(8,128)} %pad.59.w_ref, ...), custom_call_target="tpu_custom_call" | custom-call | tf_op jit(solution)/shard_map/pallas_call | solution.py:678
  145.7 2.6 collective-permute-start
  149.8 9.5 %convolution_convert_fusion.4.dgn_ref = bf16[512,3072]{1,0:T(8,128)(2,1)} fusion(bf16[512,1536]{1,0:T(8,128)(2,1)} %bitcast.72, bf16[3072,1536]{1,0:T(8,128)(2,1)} %all-gather.3.cloned.1.call-done.wo_ref), kind=kOutput, calls=%fused_computation.4 | convolution fusion | flops 4833411072 | bytes 14155776 | tf_op jit(solution)/shard_map/dot_general | solution.py:1017
  159.3 3.0 fusion.3
  162.3 1.8 collective-permute-start.1
  164.7 15.2 %shard_map.205.y_ref = f32[2,256,3072]{2,1,0:T(8,128)} custom-call(f32[2,256,3328]{2,1,0:T(8,128)} %get-tuple-element.55.act_ref, f32[2,256,256]{2,1,0:T(8,128)} %get-tuple-element.56.tok_ref, f32[2,48,256]{2,1,0:T(8,128)} %get-tuple-element.53.cst_ref, f32[2,256,128]{2,1,0:T(8,128)} %pad.61.cols_ref, f32[2,8,256]{2,1,0:T(8,128)} %pad.65.rows_ref), custom_call_target="tpu_custom_call" | custom-call | tf_op jit(solution)/shard_map/pallas_call | solution.py:678
  179.9 3.5 fusion.4
  183.5 2.3 collective-permute-start.2
  186.7 13.4 %all-gather.5.cloned.1.call-done.wz_ref = bf16[1536,3072]{1,0:T(8,128)(2,1)} async-done(((bf16[48,3072]{1,0:T(8,128)(2,1)}), bf16[1536,3072]{1,0:T(8,128)(2,1)}) %all-gather.5.cloned.1.call-update) | async-done | bytes 9437200 | tf_op jit(solution)/shard_map/all_gather | solution.py:949
  200.2 10.0 %convolution_convert_fusion.3.z_ref = bf16[512,3072]{1,0:T(8,128)(2,1)} fusion(bf16[1536,3072]{1,0:T(8,128)(2,1)} %all-gather.5.cloned.1.call-done.wz_ref, bf16[528,1536]{1,0:T(8,128)(2,1)S(1)} %fusion.2.normed_ref), kind=kOutput, calls=%fused_computation.3 | convolution fusion | flops 4833411072 | bytes 14155776 | tf_op jit(solution)/shard_map/dot_general | solution.py:1031
  210.2 3.0 add.70.state_ref
  213.2 30.8 %shard_map.206 = (bf16[512,3072]{1,0:T(8,128)(2,1)}, bf16[512,3072]{1,0:T(8,128)(2,1)}, bf16[2,256,3072]{2,1,0:T(8,128)(2,1)}, bf16[2,3072,128]{2,1,0:T(8,128)(2...) custom-call(bf16[512,3072]{1,0:T(8,128)(2,1)} %convolution_convert_fusion.3.z_ref, ...), custom_call_target="tpu_custom_call" | custom-call | tf_op jit(solution)/shard_map/pallas_call | solution.py:678
  243.9 1.8 collective-permute-start.3
  245.7 9.7 %convolution_convert_fusion.1 = bf16[3072,1536]{1,0:T(8,128)(2,1)} fusion(bf16[512,3072]{1,0:T(8,128)(2,1)} %get-tuple-element.65.gn_ref, bf16[512,1536]{1,0:T(8,128)(2,1)S(1)} %bitcast.74), kind=kOutput, calls=%fused_computation.1 | convolution fusion | flops 4836556800 | bytes 14155776 | tf_op jit(solution)/shard_map/dot_general | solution.py:1052
  256.9 3.0 fusion.5
  261.6 17.0 %shard_map.207 = (f32[2,256,3072]{2,1,0:T(8,128)}, f32[2,256,256]{2,1,0:T(8,128)}) custom-call(f32[2,256,3328]{2,1,0:T(8,128)} %get-tuple-element.55.act_ref, f32[2,256,256]{2,1,0:T(8,128)} %get-tuple-element.56.tok_ref, f32[2,48,256]{2,1,0:T(8,128)} %get-tuple-element.53.cst_ref, f32[2,256,128]{2,1,0:T(8,128)} %pad.61.cols_ref, f32[2,8,256]{2,1,0:T(8,128)} %pad.65.rows_ref, ...), custom_call_target="tpu_custom_call" | custom-call | tf_op jit(solution)/shard_map/pallas_call | solution.py:678
  278.6 3.7 fusion.6
  284.8 9.8 %convolution_convert_fusion = bf16[1536,3072]{1,0:T(8,128)(2,1)} fusion(bf16[512,3072]{1,0:T(8,128)(2,1)} %get-tuple-element.74.dz_ref, bf16[528,1536]{1,0:T(8,128)(2,1)S(1)} %fusion.2.normed_ref), kind=kOutput, calls=%fused_computation | convolution fusion | flops 4836556800 | bytes 14155776 | tf_op jit(solution)/shard_map/dot_general | solution.py:1066
  297.1 38.6 %shard_map.208 = (bf16[528,3456]{1,0:T(8,128)(2,1)}, f32[2,8,3328]{2,1,0:T(8,128)}, f32[2,8,128]{2,1,0:T(8,128)}) custom-call(bf16[528,3456]{1,0:T(8,128)(2,1)} %convolution_convert_fusion.2.px_ref.tail_ref, bf16[528,3456]{1,0:T(8,128)(2,1)} %convolution_convert_fusion.2.px_ref.tail_ref, f32[8,3328]{1,0:T(8,128)} %pad.59.w_ref, f32[8,3328]{1,0:T(8,128)} %pad.60.b_ref, ...), custom_call_target="tpu_custom_call" | custom-call | tf_op jit(solution)/shard_map/pallas_call | solution.py:678
  338.7 130.9 %shard_map.209 = (f32[48,3072]{1,0:T(8,128)}, f32[48,3456]{1,0:T(8,128)}, f32[8,128]{1,0:T(8,128)}, f32[48,128]{1,0:T(8,128)}, bf16[512,1536]{1,0:T(8,128)(2,1)}, /*index=5*/bf16[512,1536]{1,0:T(8,128)(2,1)}) custom-call(f32[4,2,2,2,8,128]{5,4,3,2,1,0:T(8,128)} %bitcast.78, bf16[4,2,2,2,48,3072]{5,4,3,2,1,0:T(8,128)(2,1)} %bitcast.71, ...), custom_call_target="tpu_custom_call" | custom-call | tf_op jit(solution)/shard_map/pallas_call | solution.py:894
  476.3 2.5 pad_maximum_fusion.1
  478.8 1.8 convert_element_type.121
  (131 shorter events, 39.2 us)
Async XLA Ops:
  7.2 103.9 %copy-start.11 = (s32[2,256]{1,0:T(2,128)S(1)}, s32[2,256]{1,0:T(2,128)}, u32[]{:S(2)}) copy-start(s32[2,256]{1,0:T(2,128)} %param.22) | copy-start | bytes 6148
  7.2 105.6 %copy-start = (bf16[2,256,1536]{2,1,0:T(8,128)(2,1)S(1)}, bf16[2,256,1536]{2,1,0:T(8,128)(2,1)}, u32[]{:S(2)}) copy-start(bf16[2,256,1536]{2,1,0:T(8,128)(2,1)} %param.12) | copy-start | bytes 4718596
  7.2 142.6 %all-gather.3.cloned.1.call-start = ((), (), s32[]{:S(2)}) async-start(), calls=%async_computation.1 | async-start | bytes 9732096 | tf_op jit(solution)/shard_map/all_gather | solution.py:948
  7.9 192.2 %all-gather.5.cloned.1.call-start = ((), (), s32[]{:S(2)}) async-start(), calls=%async_computation.2 | async-start | bytes 9732096 | tf_op jit(solution)/shard_map/all_gather | solution.py:949
  9.7 103.5 %copy-start.13 = (f32[48]{0:T(128)S(1)}, f32[48]{0:T(128)}, u32[]{:S(2)}) copy-start(f32[48]{0:T(128)} %param.18) | copy-start | bytes 580
  9.7 103.5 %copy-start.14 = (f32[48]{0:T(128)S(1)}, f32[48]{0:T(128)}, u32[]{:S(2)}) copy-start(f32[48]{0:T(128)} %param.17) | copy-start | bytes 580
  9.7 469.1 %reduce-scatter.2.cloned.1.call-start = ((), (), s32[]{:S(2)}) async-start(), calls=%async_computation.3 | async-start | bytes 9732096 | tf_op jit(solution)/shard_map/reduce_scatter | solution.py:1107
  112.8 13.6 %copy-start.9 = (bf16[16,1536]{1,0:T(8,128)(2,1)}, bf16[16,1536]{1,0:T(8,128)(2,1)S(1)}, u32[]{:S(2)}) copy-start(bf16[16,1536]{1,0:T(8,128)(2,1)S(1)} %select_bitcast_fusion.tail_ref) | copy-start | bytes 147460
  114.3 170.6 %copy-start.1 = (bf16[528,1536]{1,0:T(8,128)(2,1)}, bf16[528,1536]{1,0:T(8,128)(2,1)S(1)}, u32[]{:S(2)}) copy-start(bf16[528,1536]{1,0:T(8,128)(2,1)S(1)} %fusion.2.normed_ref) | copy-start | bytes 4866052
  145.7 13.6 %collective-permute-start = (bf16[2,3072,128]{2,1,0:T(8,128)(2,1)}, bf16[2,3072,128]{2,1,0:T(8,128)(2,1)}, u32[]{:S(2)}, u32[]{:S(2)}) collective-permute-start(bf16[2,3072,128]{2,1,0:T(8,128)(2,1)} %get-tuple-element.52), channel_id=1, source_target_pairs={{0,1},{4,5},{8,9},{12,13},{16,17},{20,21},{24,25},{28,29}} | collective-permute-start | bytes 4718600 | tf_op jit(solution)/shard_map/ppermute | solution.py:694
  149.8 9.5 %copy-start.3 = (bf16[2,3072,128]{2,1,0:T(8,128)(2,1)S(1)}, bf16[2,3072,128]{2,1,0:T(8,128)(2,1)}, u32[]{:S(2)}) copy-start(bf16[2,3072,128]{2,1,0:T(8,128)(2,1)} %get-tuple-element.52) | copy-start | bytes 4718596
  162.3 17.6 %collective-permute-start.1 = (bf16[2,3072,128]{2,1,0:T(8,128)(2,1)}, bf16[2,3072,128]{2,1,0:T(8,128)(2,1)}, u32[]{:S(2)}, u32[]{:S(2)}) collective-permute-start(bf16[2,3072,128]{2,1,0:T(8,128)(2,1)} %fusion.3), channel_id=1, source_target_pairs={{1,2},{5,6},{9,10},{13,14},{17,18},{21,22},{25,26},{29,30}} | collective-permute-start | bytes 4718600 | tf_op jit(solution)/shard_map/ppermute | solution.py:694
  179.9 5.9 %copy-start.12 = (f32[48]{0:T(128)S(1)}, f32[48]{0:T(128)}, u32[]{:S(2)}) copy-start(f32[48]{0:T(128)} %param.19) | copy-start | bytes 580
  183.5 26.7 %collective-permute-start.2 = (bf16[2,3072,128]{2,1,0:T(8,128)(2,1)}, bf16[2,3072,128]{2,1,0:T(8,128)(2,1)}, u32[]{:S(2)}, u32[]{:S(2)}) collective-permute-start(bf16[2,3072,128]{2,1,0:T(8,128)(2,1)} %get-tuple-element.91), channel_id=1, source_target_pairs={{2,3},{6,7},{10,11},{14,15},{18,19},{22,23},{26,27},{30,31}} | collective-permute-start | bytes 4718600 | tf_op jit(solution)/shard_map/ppermute | solution.py:694
  186.7 23.5 %copy-start.5 = (bf16[2,3072,128]{2,1,0:T(8,128)(2,1)S(1)}, bf16[2,3072,128]{2,1,0:T(8,128)(2,1)}, u32[]{:S(2)}) copy-start(bf16[2,3072,128]{2,1,0:T(8,128)(2,1)} %get-tuple-element.92) | copy-start | bytes 4718596
  213.2 32.6 %copy-start.6 = (bf16[2,256,1536]{2,1,0:T(8,128)(2,1)S(1)}, bf16[2,256,1536]{2,1,0:T(8,128)(2,1)}, u32[]{:S(2)}) copy-start(bf16[2,256,1536]{2,1,0:T(8,128)(2,1)} %param.23) | copy-start | bytes 4718596
  243.9 11.5 %collective-permute-start.3 = (bf16[2,3072,128]{2,1,0:T(8,128)(2,1)}, bf16[2,3072,128]{2,1,0:T(8,128)(2,1)}, u32[]{:S(2)}, u32[]{:S(2)}) collective-permute-start(bf16[2,3072,128]{2,1,0:T(8,128)(2,1)} %get-tuple-element.64), channel_id=1, source_target_pairs={{3,2},{7,6},{11,10},{15,14},{19,18},{23,22},{27,26},{31,30}} | collective-permute-start | bytes 4718600 | tf_op jit(solution)/shard_map/ppermute | solution.py:694
  255.5 1.4 copy-start.2
  259.9 18.7 %collective-permute-start.4 = (bf16[2,3072,128]{2,1,0:T(8,128)(2,1)}, bf16[2,3072,128]{2,1,0:T(8,128)(2,1)}, u32[]{:S(2)}, u32[]{:S(2)}) collective-permute-start(bf16[2,3072,128]{2,1,0:T(8,128)(2,1)} %fusion.5), channel_id=1, source_target_pairs={{2,1},{6,5},{10,9},{14,13},{18,17},{22,21},{26,25},{30,29}} | collective-permute-start | bytes 4718600 | tf_op jit(solution)/shard_map/ppermute | solution.py:694
  278.6 5.9 %copy-start.10 = (f32[2,8,3072]{2,1,0:T(8,128)S(1)}, f32[2,8,3072]{2,1,0:T(8,128)}, u32[]{:S(2)}) copy-start(f32[2,8,3072]{2,1,0:T(8,128)} %get-tuple-element.62) | copy-start | bytes 589828
  282.3 13.2 %collective-permute-start.5 = (bf16[2,3072,128]{2,1,0:T(8,128)(2,1)}, bf16[2,3072,128]{2,1,0:T(8,128)(2,1)S(1)}, u32[]{:S(2)}, u32[]{:S(2)}) collective-permute-start(bf16[2,3072,128]{2,1,0:T(8,128)(2,1)} %get-tuple-element.89), channel_id=1, source_target_pairs={{1,0},{5,4},{9,8},{13,12},{17,16},{21,20},{25,24},{29,28}} | collective-permute-start | bytes 4718600 | tf_op jit(solution)/shard_map/ppermute | solution.py:694
  284.8 10.7 %copy-start.4 = (bf16[2,3072,128]{2,1,0:T(8,128)(2,1)S(1)}, bf16[2,3072,128]{2,1,0:T(8,128)(2,1)}, u32[]{:S(2)}) copy-start(bf16[2,3072,128]{2,1,0:T(8,128)(2,1)} %get-tuple-element.90) | copy-start | bytes 4718596
  469.6 11.0 %copy-start.8 = (bf16[512,1536]{1,0:T(8,128)(2,1)S(1)}, bf16[512,1536]{1,0:T(8,128)(2,1)}, u32[]{:S(2)}) copy-start(bf16[512,1536]{1,0:T(8,128)(2,1)} %get-tuple-element.80) | copy-start | bytes 4718596
  476.3 5.5 %copy-start.7 = (bf16[512,1536]{1,0:T(8,128)(2,1)S(1)}, bf16[512,1536]{1,0:T(8,128)(2,1)}, u32[]{:S(2)}) copy-start(bf16[512,1536]{1,0:T(8,128)(2,1)} %get-tuple-element.81) | copy-start | bytes 4718596
Sparse Core Ops, SparseCore 0:
  10.9 102.9 all-gather.2
  117.4 82.6 all-gather.4
  255.6 156.8 reduce-scatter.1

commit v6 on v5

--- a/solution.py
+++ b/solution.py
@@ -674,7 +674,7 @@
     return pl.BlockSpec((rows, width), lambda s: (s, 0))
 
 
-def call(kernel, count, in_specs, outs, scratch, *args):
+def call(kernel, count, in_specs, outs, scratch, *args, mib):
     return pl.pallas_call(
         kernel,
         grid=(count,),
@@ -682,7 +682,7 @@
         out_specs=[spec for spec, _unused in outs],
         out_shape=[jax.ShapeDtypeStruct(*made) for _unused, made in outs],
         scratch_shapes=scratch,
-        compiler_params=pltpu.CompilerParams(vmem_limit_bytes=VMEM),
+        compiler_params=pltpu.CompilerParams(vmem_limit_bytes=mib * 1024 * 1024),
     )(*args)
 
 
@@ -1005,7 +1005,7 @@
          (per_seq(HEADS, length), ((seqs, HEADS, length), f32)),
          (per_seq(INNER, STATE), ((seqs, INNER, STATE), bf16))],
         [pltpu.VMEM((length + 8, LANES), f32)],
-        px, px, conv_w8, conv_b8, cols, heads,
+        px, px, conv_w8, conv_b8, cols, heads, mib=24,
     )
     carried = cols[:, length - 1, 3]
     kept = jnp.exp(cst[:, :, length - 1]) * carried[:, None]
@@ -1023,7 +1023,7 @@
              per_seq(length, LANES), per_seq(8, length)],
             [(per_seq(length, INNER), ((seqs, length, INNER), f32))],
             [pltpu.VMEM((length, length), f32), pltpu.VMEM((length, length), f32)],
-            act, tok, cst, cols, rows,
+            act, tok, cst, cols, rows, mib=24,
         )
         return y
 
@@ -1044,7 +1044,7 @@
          (per_seq(length, LANES), ((seqs, length, LANES), f32)),
          (per_seq(8, INNER), ((seqs, 8, INNER), f32))],
         [pltpu.VMEM((length, INNER), f32), pltpu.VMEM((length, STATE), f32)],
-        pz, act, tok, cols, y, entering, dgn, lanes,
+        pz, act, tok, cols, y, entering, dgn, lanes, mib=44,
     )
     tn = (((0,), (0,)), ((), ()))
 
@@ -1059,7 +1059,7 @@
             [(per_seq(length, INNER), ((seqs, length, INNER), f32)),
              (per_seq(length, 2 * STATE), ((seqs, length, 2 * STATE), f32))],
             [pltpu.VMEM((length, length), f32)] * 3,
-            act, tok, cst, cols, rows, dy,
+            act, tok, cst, cols, rows, dy, mib=28,
         )
 
     def gate_weights():
@@ -1083,7 +1083,7 @@
          pltpu.VMEM((length, LANES), f32), pltpu.VMEM((length, STATE), f32), pltpu.VMEM((LANES, LANES), f32),
          pltpu.VMEM((8, INNER), f32), pltpu.VMEM((seqs, 8, px_width), f32)],
         px, px, conv_w8, conv_b8, cols, heads, act, tok, lanes, dy, dx, dbc, dqueries, ddecay,
-        later, entering,
+        later, entering, mib=48,
     )
     sums = jnp.sum(sums, axis=0)
     dconv = jnp.sum(dconv, axis=0)

time: 499 us -> 494 us (0.990)
  Pallas kernels: 343 us -> 324 us
  waiting for transfers between devices: 15.1 us -> 28.6 us
  local copies, waits for them, and re-layouts: 25.4 us -> 32 us
    pallas_call x5, Pallas kernels: 121 us -> 105 us  [call(): pl.pallas_call(kernel, grid=(count,), in_specs=in_specs, out_specs=[spec...]
    all_gather x1, waiting for transfers between devices: 13.4 us -> 27.9 us  [local(): w_z = lax.all_gather(w_z, BOTH, axis=0, tiled=True)]
    unnamed x34 -> x72, local copies, waits for them, and re-layouts: 5.35 us -> 13.4 us
  transfers between devices with their start and end apart: 9 -> 9, of which waited for: 2 -> 1; matrix products, arithmetic and copies ran while one was open for 20% -> 19% of each run, Pallas kernels for 64% -> 61%
where the time goes in v6:
time: 494 us; the launch traced here: 485 us
  Pallas kernels  324 us (66%)
  matrix products  46.9 us (9%)
  local copies, waits for them, and re-layouts  32 us (6%)
  other arithmetic  29.5 us (6%)
  waiting for transfers between devices  28.6 us (6%)
  between operations  14.9 us (3%)
  starting transfers between devices  9.13 us (2%)
    pallas_call x1, Pallas kernels, finish(): pl.pallas_call(partial(finish_kernel, tuple(lead)), out_shape=[jax.ShapeD...  128 us
    pallas_call x5, Pallas kernels, call(): pl.pallas_call(kernel, grid=(count,), in_specs=in_specs, out_specs=[spec...  105 us
    pallas_call x1, Pallas kernels, gather_all(): pl.pallas_call(partial(gather_kernel, tuple(units), n), out_shape=[jax.Sh...  90.8 us
    all_gather x1, waiting for transfers between devices, local(): w_z = lax.all_gather(w_z, BOTH, axis=0, tiled=True)  27.9 us
    convert_element_type x4, other arithmetic, chain(): (own.astype(f32) + factor * entered.astype(f32)).astype(bf16)  15.2 us
    unnamed x72, local copies, waits for them, and re-layouts  13.4 us
    dot_general x1, matrix products, local(): px = MM(normed, w_x).astype(bf16)  10.8 us
  transfers between devices with their start and end apart: 9, of which 1 were waited for; matrix products, arithmetic and copies ran while one was open for 19% of the time, Pallas kernels for 61%

profile of v6, /device:TPU:0, one launch (start us, length us, event | category | flops | bytes accessed | tf_op | source)
XLA Modules:
  0.0 485.3 jit_solution(8958535140218853237)
XLA Ops:
  15.9 90.8 %shard_map.203 = (bf16[4,2,2,2,48,3456]{5,4,3,2,1,0:T(8,128)(2,1)}, bf16[4,2,2,2,16,128]{5,4,3,2,1,0:T(8,128)(2,1)}, bf16[16,1536]{1,0:T(8,128)(2,1)}) custom-call(bf16[48,3456]{1,0:T(8,128)(2,1)} %pad.54.refs_0_, bf16[16,128]{1,0:T(8,128)(2,1)} %fusion.16.refs_1_, bf16[16,1536]{1,0:T(8,128)(2,1)} %maximum_bitcast_fusion.refs_2_), custom_call_target="tpu_custom_call" | custom-call | tf_op jit(solution)/shard_map/pallas_call | solution.py:244
  112.1 10.8 %convolution_convert_fusion.2.px_ref.tail_ref = bf16[528,3456]{1,0:T(8,128)(2,1)S(1)} fusion(bf16[528,1536]{1,0:T(8,128)(2,1)S(1)} %fusion.2.normed_ref, bf16[1536,3456]{1,0:T(8,128)(2,1)} %bitcast.71), kind=kOutput, calls=%fused_computation.2 | convolution fusion | flops 5607512064 | bytes 15888384 | tf_op jit(solution)/shard_map/dot_general | solution.py:996
  123.0 15.6 %shard_map.204 = (f32[2,256,3328]{2,1,0:T(8,128)S(1)}, f32[2,256,256]{2,1,0:T(8,128)S(1)}, f32[2,48,256]{2,1,0:T(8,128)S(1)}, bf16[2,3072,128]{2,1,0:T(8,128)(2,1)S(1)}) custom-call(bf16[528,3456]{1,0:T(8,128)(2,1)S(1)} %convolution_convert_fusion.2.px_ref.tail_ref, bf16[528,3456]{1,0:T(8,128)(2,1)S(1)} %convolution_convert_fusion.2.px_ref.tail_ref, ...), custom_call_target="tpu_custom_call" | custom-call | tf_op jit(solution)/shard_map/pallas_call | solution.py:678
  138.6 2.8 copy-done
  141.4 2.7 collective-permute-start
  144.8 9.5 %convolution_convert_fusion.4.dgn_ref = bf16[512,3072]{1,0:T(8,128)(2,1)} fusion(bf16[512,1536]{1,0:T(8,128)(2,1)} %bitcast.74, bf16[3072,1536]{1,0:T(8,128)(2,1)} %all-gather.3.cloned.1.call-done.wo_ref), kind=kOutput, calls=%fused_computation.4 | convolution fusion | flops 4833411072 | bytes 14155776 | tf_op jit(solution)/shard_map/dot_general | solution.py:1017
  154.3 2.1 fusion.3
  157.2 11.5 %shard_map.205.y_ref = f32[2,256,3072]{2,1,0:T(8,128)S(1)} custom-call(f32[2,256,3328]{2,1,0:T(8,128)S(1)} %bitcast.67, f32[2,256,256]{2,1,0:T(8,128)S(1)} %get-tuple-element.56.tok_ref, f32[2,48,256]{2,1,0:T(8,128)S(1)} %get-tuple-element.53.cst_ref, f32[2,256,128]{2,1,0:T(8,128)S(1)} %pad.61.cols_ref, f32[2,8,256]{2,1,0:T(8,128)S(1)} %pad.65.rows_ref), custom_call_target="tpu_custom_call" | custom-call | tf_op jit(solution)/shard_map/pallas_call | solution.py:678
  168.8 4.3 fusion.4
  174.8 27.9 %all-gather.5.cloned.1.call-done.wz_ref = bf16[1536,3072]{1,0:T(8,128)(2,1)} async-done(((bf16[48,3072]{1,0:T(8,128)(2,1)}), bf16[1536,3072]{1,0:T(8,128)(2,1)}) %all-gather.5.cloned.1.call-update) | async-done | bytes 9437200 | tf_op jit(solution)/shard_map/all_gather | solution.py:949
  202.6 9.4 %convolution_convert_fusion.3.z_ref = bf16[512,3072]{1,0:T(8,128)(2,1)} fusion(bf16[1536,3072]{1,0:T(8,128)(2,1)} %all-gather.5.cloned.1.call-done.wz_ref, bf16[528,1536]{1,0:T(8,128)(2,1)} %copy-done.16), kind=kOutput, calls=%fused_computation.3 | convolution fusion | flops 4833411072 | bytes 14155776 | tf_op jit(solution)/shard_map/dot_general | solution.py:1031
  215.0 28.1 %shard_map.206 = (bf16[512,3072]{1,0:T(8,128)(2,1)S(1)}, bf16[512,3072]{1,0:T(8,128)(2,1)}, bf16[2,256,3072]{2,1,0:T(8,128)(2,1)}, bf16[2,3072,128]{2,1,0:T(8,12...) custom-call(bf16[512,3072]{1,0:T(8,128)(2,1)} %convolution_convert_fusion.3.z_ref, ...), custom_call_target="tpu_custom_call" | custom-call | tf_op jit(solution)/shard_map/pallas_call | solution.py:678
  244.5 2.1 collective-permute-start.3
  246.6 7.5 %convolution_convert_fusion.1 = bf16[3072,1536]{1,0:T(8,128)(2,1)} fusion(bf16[512,3072]{1,0:T(8,128)(2,1)S(1)} %get-tuple-element.65.gn_ref, bf16[512,1536]{1,0:T(8,128)(2,1)S(1)} %bitcast.76), kind=kOutput, calls=%fused_computation.1 | convolution fusion | flops 4836556800 | bytes 14155776 | tf_op jit(solution)/shard_map/dot_general | solution.py:1052
  254.2 2.5 fusion.5
  257.5 2.9 copy-done.1
  260.4 12.9 %shard_map.207 = (f32[2,256,3072]{2,1,0:T(8,128)S(1)}, f32[2,256,256]{2,1,0:T(8,128)S(1)}) custom-call(f32[2,256,3328]{2,1,0:T(8,128)S(1)} %copy-done.1, f32[2,256,256]{2,1,0:T(8,128)S(1)} %get-tuple-element.56.tok_ref, f32[2,48,256]{2,1,0:T(8,128)S(1)} %get-tuple-element.53.cst_ref, f32[2,256,128]{2,1,0:T(8,128)S(1)} %pad.61.cols_ref, ...), custom_call_target="tpu_custom_call" | custom-call | tf_op jit(solution)/shard_map/pallas_call | solution.py:678
  273.3 6.2 %fusion.6 = (bf16[2,3072,128]{2,1,0:T(8,128)(2,1)}, bf16[2,3072,128]{2,1,0:T(8,128)(2,1)}) fusion(bf16[2,3072,128]{2,1,0:T(8,128)(2,1)} %get-tuple-element.64, f32[2,3072]{1,0:T(2,128)S(1)} %copy-done.25, bf16[2,3072,128]{2,1,0:T(8,128)(2,1)} %collective-permute-done.3, bf16[2,3072,128]{2,1,0:T(8,128)(2,1)S(1)} %collective-permute-done.4), kind=kLoop, calls=%fused_computation.17 | loop fusion | flops 4718592 | bytes 7888896 | tf_op jit(solution)/shard_map/convert_element_type | solution.py:693
  285.0 9.7 %convolution_convert_fusion = bf16[1536,3072]{1,0:T(8,128)(2,1)} fusion(bf16[512,3072]{1,0:T(8,128)(2,1)} %get-tuple-element.74.dz_ref, bf16[528,1536]{1,0:T(8,128)(2,1)} %copy-done.16), kind=kOutput, calls=%fused_computation | convolution fusion | flops 4836556800 | bytes 14155776 | tf_op jit(solution)/shard_map/dot_general | solution.py:1066
  294.7 1.9 add.74.later_ref
  296.7 37.3 %shard_map.208 = (bf16[528,3456]{1,0:T(8,128)(2,1)}, f32[2,8,3328]{2,1,0:T(8,128)S(1)}, f32[2,8,128]{2,1,0:T(8,128)S(1)}) custom-call(bf16[528,3456]{1,0:T(8,128)(2,1)} %copy-done.2, bf16[528,3456]{1,0:T(8,128)(2,1)} %copy-done.2, f32[8,3328]{1,0:T(8,128)S(1)} %pad.59.w_ref, f32[8,3328]{1,0:T(8,128)S(1)} %pad.60.b_ref, f32[2,256,128]{2,1,0:T(8,128)S(1)} %pad.61.cols_ref, ...), custom_call_target="tpu_custom_call" | custom-call | tf_op jit(solution)/shard_map/pallas_call | solution.py:678
  337.0 128.0 %shard_map.209 = (f32[48,3072]{1,0:T(8,128)}, f32[48,3456]{1,0:T(8,128)}, f32[8,128]{1,0:T(8,128)}, f32[48,128]{1,0:T(8,128)}, bf16[512,1536]{1,0:T(8,128)(2,1)}, /*index=5*/bf16[512,1536]{1,0:T(8,128)(2,1)}) custom-call(f32[4,2,2,2,8,128]{5,4,3,2,1,0:T(8,128)} %bitcast.80, bf16[4,2,2,2,48,3072]{5,4,3,2,1,0:T(8,128)(2,1)} %bitcast.73, ...), custom_call_target="tpu_custom_call" | custom-call | tf_op jit(solution)/shard_map/pallas_call | solution.py:894
  471.7 2.5 pad_maximum_fusion.1
  474.2 1.8 convert_element_type.121
  (170 shorter events, 39.4 us)
Async XLA Ops:
  7.2 103.0 %copy-start.28 = (s32[2,256]{1,0:T(2,128)S(1)}, s32[2,256]{1,0:T(2,128)}, u32[]{:S(2)}) copy-start(s32[2,256]{1,0:T(2,128)} %param.22) | copy-start | bytes 6148
  7.2 104.0 %copy-start.15 = (bf16[2,256,1536]{2,1,0:T(8,128)(2,1)S(1)}, bf16[2,256,1536]{2,1,0:T(8,128)(2,1)}, u32[]{:S(2)}) copy-start(bf16[2,256,1536]{2,1,0:T(8,128)(2,1)} %param.12) | copy-start | bytes 4718596
  7.2 137.6 %all-gather.3.cloned.1.call-start = ((), (), s32[]{:S(2)}) async-start(), calls=%async_computation.1 | async-start | bytes 9732096 | tf_op jit(solution)/shard_map/all_gather | solution.py:948
  7.9 194.7 %all-gather.5.cloned.1.call-start = ((), (), s32[]{:S(2)}) async-start(), calls=%async_computation.2 | async-start | bytes 9732096 | tf_op jit(solution)/shard_map/all_gather | solution.py:949
  9.7 101.9 %copy-start.30 = (f32[48]{0:T(128)S(1)}, f32[48]{0:T(128)}, u32[]{:S(2)}) copy-start(f32[48]{0:T(128)} %param.18) | copy-start | bytes 580
  9.7 101.9 %copy-start.31 = (f32[48]{0:T(128)S(1)}, f32[48]{0:T(128)}, u32[]{:S(2)}) copy-start(f32[48]{0:T(128)} %param.17) | copy-start | bytes 580
  9.7 464.5 %reduce-scatter.2.cloned.1.call-start = ((), (), s32[]{:S(2)}) async-start(), calls=%async_computation.3 | async-start | bytes 9732096 | tf_op jit(solution)/shard_map/reduce_scatter | solution.py:1107
  111.6 11.3 %copy-start.13 = (f32[8,128]{1,0:T(8,128)}, f32[8,128]{1,0:T(8,128)S(1)}, u32[]{:S(2)}) copy-start(f32[8,128]{1,0:T(8,128)S(1)} %select_maximum_fusion.1.heads_ref) | copy-start | bytes 12292
  112.1 10.9 %copy-start.16 = (bf16[528,1536]{1,0:T(8,128)(2,1)}, bf16[528,1536]{1,0:T(8,128)(2,1)S(1)}, u32[]{:S(2)}) copy-start(bf16[528,1536]{1,0:T(8,128)(2,1)S(1)} %fusion.2.normed_ref) | copy-start | bytes 4866052
  123.0 15.6 %copy-start.2 = (bf16[528,3456]{1,0:T(8,128)(2,1)}, bf16[528,3456]{1,0:T(8,128)(2,1)S(1)}, u32[]{:S(2)}) copy-start(bf16[528,3456]{1,0:T(8,128)(2,1)S(1)} %convolution_convert_fusion.2.px_ref.tail_ref) | copy-start | bytes 10948612
  141.4 12.8 %collective-permute-start = (bf16[2,3072,128]{2,1,0:T(8,128)(2,1)S(1)}, bf16[2,3072,128]{2,1,0:T(8,128)(2,1)}, u32[]{:S(2)}, u32[]{:S(2)}) collective-permute-start(bf16[2,3072,128]{2,1,0:T(8,128)(2,1)S(1)} %get-tuple-element.52), channel_id=1, source_target_pairs={{0,1},{4,5},{8,9},{12,13},{16,17},{20,21},{24,25},{28,29}} | collective-permute-start | bytes 4718600 | tf_op jit(solution)/shard_map/ppermute | solution.py:694
  144.7 109.4 %copy-start.24 = (f32[2,3072]{1,0:T(2,128)}, f32[2,3072]{1,0:T(2,128)S(1)}, u32[]{:S(2)}) copy-start(f32[2,3072]{1,0:T(2,128)S(1)} %mul.68) | copy-start | bytes 73732
  144.8 12.4 %slice-start = ((s8[6815744]{0:T(1024)(128)(4,1)}), s8[4194304]{0:T(1024)(128)(4,1)S(1)}, s32[]{:S(2)}) async-start(s8[6815744]{0:T(1024)(128)(4,1)} %bitcast.66), calls=%async_computation.4 | async-start | bytes 8388608
  144.8 12.4 %slice-start.1 = ((s8[6815744]{0:T(1024)(128)(4,1)}), s8[2621440]{0:T(1024)(128)(4,1)S(1)}, s32[]{:S(2)}) async-start(s8[6815744]{0:T(1024)(128)(4,1)} %bitcast.66), calls=%async_computation.5 | async-start | bytes 5242880
  156.4 12.4 %collective-permute-start.1 = (bf16[2,3072,128]{2,1,0:T(8,128)(2,1)S(1)}, bf16[2,3072,128]{2,1,0:T(8,128)(2,1)S(1)}, u32[]{:S(2)}, u32[]{:S(2)}) collective-permute-start(bf16[2,3072,128]{2,1,0:T(8,128)(2,1)S(1)} %fusion.3), channel_id=1, source_target_pairs={{1,2},{5,6},{9,10},{13,14},{17,18},{21,22},{25,26},{29,30}} | collective-permute-start | bytes 4718600 | tf_op jit(solution)/shard_map/ppermute | solution.py:694
  157.2 11.6 %copy-start.11 = (f32[2,8,256]{2,1,0:T(8,128)}, f32[2,8,256]{2,1,0:T(8,128)S(1)}, u32[]{:S(2)}) copy-start(f32[2,8,256]{2,1,0:T(8,128)S(1)} %pad.65.rows_ref) | copy-start | bytes 49156
  173.2 38.9 %collective-permute-start.2 = (bf16[2,3072,128]{2,1,0:T(8,128)(2,1)}, bf16[2,3072,128]{2,1,0:T(8,128)(2,1)S(1)}, u32[]{:S(2)}, u32[]{:S(2)}) collective-permute-start(bf16[2,3072,128]{2,1,0:T(8,128)(2,1)} %get-tuple-element.91), channel_id=1, source_target_pairs={{2,3},{6,7},{10,11},{14,15},{18,19},{22,23},{26,27},{30,31}} | collective-permute-start | bytes 4718600 | tf_op jit(solution)/shard_map/ppermute | solution.py:694
  202.6 10.5 %copy-start.18 = (bf16[2,3072,128]{2,1,0:T(8,128)(2,1)S(1)}, bf16[2,3072,128]{2,1,0:T(8,128)(2,1)}, u32[]{:S(2)}) copy-start(bf16[2,3072,128]{2,1,0:T(8,128)(2,1)} %get-tuple-element.92) | copy-start | bytes 4718596
  215.0 31.6 %copy-start.19 = (bf16[2,256,1536]{2,1,0:T(8,128)(2,1)S(1)}, bf16[2,256,1536]{2,1,0:T(8,128)(2,1)}, u32[]{:S(2)}) copy-start(bf16[2,256,1536]{2,1,0:T(8,128)(2,1)} %param.23) | copy-start | bytes 4718596
  244.5 9.6 %collective-permute-start.3 = (bf16[2,3072,128]{2,1,0:T(8,128)(2,1)}, bf16[2,3072,128]{2,1,0:T(8,128)(2,1)}, u32[]{:S(2)}, u32[]{:S(2)}) collective-permute-start(bf16[2,3072,128]{2,1,0:T(8,128)(2,1)} %get-tuple-element.64), channel_id=1, source_target_pairs={{3,2},{7,6},{11,10},{15,14},{19,18},{23,22},{27,26},{31,30}} | collective-permute-start | bytes 4718600 | tf_op jit(solution)/shard_map/ppermute | solution.py:694
  256.7 16.6 %collective-permute-start.4 = (bf16[2,3072,128]{2,1,0:T(8,128)(2,1)S(1)}, bf16[2,3072,128]{2,1,0:T(8,128)(2,1)S(1)}, u32[]{:S(2)}, u32[]{:S(2)}) collective-permute-start(bf16[2,3072,128]{2,1,0:T(8,128)(2,1)S(1)} %fusion.5), channel_id=1, source_target_pairs={{2,1},{6,5},{10,9},{14,13},{18,17},{22,21},{26,25},{30,29}} | collective-permute-start | bytes 4718600 | tf_op jit(solution)/shard_map/ppermute | solution.py:694
  260.4 12.9 %copy-start.25 = (f32[2,3072]{1,0:T(2,128)S(1)}, f32[2,3072]{1,0:T(2,128)}, u32[]{:S(2)}) copy-start(f32[2,3072]{1,0:T(2,128)} %copy-done.24) | copy-start | bytes 73732
  279.5 15.2 %collective-permute-start.5 = (bf16[2,3072,128]{2,1,0:T(8,128)(2,1)}, bf16[2,3072,128]{2,1,0:T(8,128)(2,1)}, u32[]{:S(2)}, u32[]{:S(2)}) collective-permute-start(bf16[2,3072,128]{2,1,0:T(8,128)(2,1)} %get-tuple-element.89), channel_id=1, source_target_pairs={{1,0},{5,4},{9,8},{13,12},{17,16},{21,20},{25,24},{29,28}} | collective-permute-start | bytes 4718600 | tf_op jit(solution)/shard_map/ppermute | solution.py:694
  465.0 11.0 %copy-start.21 = (bf16[512,1536]{1,0:T(8,128)(2,1)S(1)}, bf16[512,1536]{1,0:T(8,128)(2,1)}, u32[]{:S(2)}) copy-start(bf16[512,1536]{1,0:T(8,128)(2,1)} %get-tuple-element.80) | copy-start | bytes 4718596
  (19 other events, 62.3 us)
Sparse Core Ops, SparseCore 0:
  10.9 102.9 all-gather.2
  117.4 85.1 all-gather.4
  254.3 148.9 reduce-scatter.1
